TPU v7x, 32 devices: a whole 2x2x4 slice. The times are simulated.
32 devices in a mesh: dp: 8 (over y, x, core), replica: 4 (over z).
Axes of the slice: x: 2, y: 2, z: 4, core: 2. Of those that a mesh axis runs over, the one named last changes fastest.
Arguments:
- image_emb: bfloat16 [4, 1024, 1152], P('replica', 'dp'), may hold values from -6 to 6
- text_feat: bfloat16 [4, 1024, 1152], P('replica', 'dp'), may hold values from -6 to 6
- head_w: bfloat16 [1152, 1152], replicated, may hold values from -0.1875 to 0.1875
- log_scale: float32 [1], replicated, may hold values from 1.6 to 2.4
- bias: float32 [1], replicated, may hold values from -2 to 0
- pair_ids: int32 [4, 1024], P('replica', 'dp'), may hold values from 0 to 127
Outputs:
- grad_feat: bfloat16 [4, 1024, 1152], P('replica', 'dp')
- head_grad: float32 [1152, 1152], P('replica', 'dp')
All inputs are finite; a program needn't handle non-finite values.
Results may differ from a plain program's by a relative error of at most 0.017.
Values may be sent and summed in bfloat16 or wider, within the bound.
No kernel may reach another device: no remote copies, remote signals or barrier semaphores. Data moves between devices by JAX's collectives and lax.ppermute only.
A program may use at most 64 MiB of HBM per device.

v0:
```python
import jax
import jax.numpy as jnp
from jax import lax
from jax.sharding import PartitionSpec as P

HOPS = 3


LOSS_SCALE = 2048.0


def shifted(shard, axis, by):
    size = lax.axis_size(axis)
    return lax.ppermute(shard, axis, [(i, (i + by) % size) for i in range(size)])


def pair_grads(img_block, img_ids, txt_block, txt_ids, scale, shift_b, factor):
    sims = lax.dot_general(
        img_block, txt_block, (((1,), (1,)), ((), ())), preferred_element_type=jnp.float32
    )
    logits = scale * sims + shift_b
    match = (img_ids[:, None] == txt_ids[None, :]).astype(jnp.float32)
    return (factor * (jax.nn.sigmoid(logits) - match)).astype(jnp.bfloat16)


def left_product(first, second):
    return lax.dot_general(
        first, second, (((0,), (0,)), ((), ())), preferred_element_type=jnp.float32
    )


def shards(image_emb, text_feat, head_w, log_scale, bias, pair_ids):
    images = image_emb[0]
    feats = text_feat[0]
    ids = pair_ids[0]
    rows = feats.shape[0]
    factor = LOSS_SCALE / (HOPS * rows)
    scale = jnp.exp(log_scale[0])
    shift_b = bias[0]
    img32 = images.astype(jnp.float32)
    unit_img = (img32 / jnp.sqrt(jnp.sum(img32 * img32, axis=1, keepdims=True) + 1e-06)).astype(
        jnp.bfloat16
    )
    raw = jnp.dot(feats, head_w, preferred_element_type=jnp.float32)
    norms = jnp.sqrt(jnp.sum(raw * raw, axis=1, keepdims=True) + 1e-06)
    unit_txt = raw / norms
    txt_bf = unit_txt.astype(jnp.bfloat16)
    id_words = ids.astype(jnp.bfloat16)
    summed = jnp.zeros((rows, head_w.shape[1]), jnp.float32)
    block = txt_bf
    block_ids = id_words
    for offset in range(HOPS):
        grads = pair_grads(
            unit_img, ids, block, block_ids.astype(jnp.int32), scale, shift_b, factor
        )
        summed = summed + left_product(grads, unit_img)
        if offset + 1 < HOPS:
            block, block_ids = shifted((block, block_ids), "dp", 1)
            summed = shifted(summed.astype(jnp.bfloat16), "dp", 1).astype(summed.dtype)
    summed = shifted(summed.astype(jnp.bfloat16), "dp", 1 - HOPS).astype(summed.dtype)
    dvec = scale * summed
    dzed = ((dvec - unit_txt * jnp.sum(unit_txt * dvec, axis=1, keepdims=True)) / norms).astype(
        jnp.bfloat16
    )
    grad_feat = lax.dot_general(
        dzed, head_w, (((1,), (1,)), ((), ())), preferred_element_type=jnp.float32
    ).astype(jnp.bfloat16)
    columns = lax.all_to_all(feats, "replica", split_axis=1, concat_axis=0, tiled=True)
    local_head = left_product(columns, lax.all_gather(dzed, "replica", axis=0, tiled=True))
    head_grad = lax.psum_scatter(local_head, "dp", scatter_dimension=1, tiled=True)
    return (grad_feat[None], head_grad)


def solution(mesh):
    return jax.shard_map(
        shards,
        mesh=mesh,
        in_specs=(
            P("replica", "dp", None),
            P("replica", "dp", None),
            P(),
            P(),
            P(),
            P("replica", "dp"),
        ),
        out_specs=(P("replica", "dp", None), P("replica", "dp")),
        check_vma=False,
    )
```

profile of v0, /device:TPU:0, one launch (start us, length us, event | category | flops | bytes accessed | tf_op | source)
XLA Modules:
  0.0 138.7 jit_solution(17418532491275111167)
XLA Ops:
  7.2 0.0 copy-start
  7.2 0.0 copy-start.8
  7.2 0.0 all-gather.2.cloned.1.call-start
  8.7 1.1 fusion.29
  9.8 0.5 add_sqrt_fusion.1
  10.4 0.7 bitcast_convert_fusion.1
  11.1 0.0 copy-done
  11.1 1.6 %multiply_reduce_fusion.1 = (f32[128]{0:T(128)S(1)}, f32[128,1152]{1,0:T(8,128)S(1)}) fusion(bf16[1152,1152]{1,0:T(8,128)(2,1)S(1)} %copy-done, bf16[1,128,1152]{2,1,0:T(8,128)(2,1)} %param.7), kind=kOutput, calls=%fused_computation.43 | convolution fusion | flops 340033408 | bytes 3539456 | tf_op jit(solution)/shard_map/dot_general | solution.py:44
  12.8 0.1 fusion.65
  12.9 0.0 copy-done.8
  12.9 2.4 %convolution_convert_fusion.1 = bf16[128,1152]{1,0:T(8,128)(2,1)} fusion(bf16[128,1152]{1,0:T(8,128)(2,1)S(1)} %fusion.65, s32[128]{0:T(128)S(1)} %get-tuple-element.9, f32[]{:T(128)} %bitcast.44, f32[]{:T(128)} %bitcast, s32[128]{0:T(128)S(1)} %bitcast.50, bf16[1,128,1152]{2,1,0:T(8,128)(2,1)} %param.6, f32[128]{0:T(128)} %add_sqrt_fusion.1), kind=kOutput, calls=%fused_computation.2 | convolution fusion | flops 76693504 | bytes 886280 | tf_op jit(solution)/shard_map/dot_general | solution.py:27
  15.4 0.5 collective-permute-start
  15.8 2.6 %collective-permute-start.1 = (bf16[128,1152]{1,0:T(8,128)(2,1)S(1)}, bf16[128,1152]{1,0:T(8,128)(2,1)S(1)}, u32[]{:S(2)}, u32[]{:S(2)}) collective-permute-start(bf16[128,1152]{1,0:T(8,128)(2,1)S(1)} %fusion.65), channel_id=1, source_target_pairs={{0,4},{4,8},{8,12},{12,16},{16,20},{20,24},{24,28},{28,0},{1,5},{5... | collective-permute-start | bytes 884744 | tf_op jit(solution)/shard_map/ppermute | solution.py:14
  18.4 0.0 collective-permute-start.2
  18.4 8.1 %collective-permute-done.2 = bf16[128]{0:T(256)(128)(2,1)S(1)} collective-permute-done((bf16[128]{0:T(256)(128)(2,1)S(1)}, bf16[128]{0:T(256)(128)(2,1)S(1)}, u32[]{:S(2)}, u32[]{:S(2)}) %collective-permute-start.2) | collective-permute-done | bytes 288 | tf_op jit(solution)/shard_map/ppermute | solution.py:14
  26.5 0.0 collective-permute-done
  26.5 0.0 copy-start.6
  26.5 0.0 collective-permute-done.1
  26.5 0.7 copy-done.6
  27.3 0.0 copy-start.3
  27.3 0.7 copy-done.3
  28.0 2.7 %add_convert_fusion = bf16[128,1152]{1,0:T(8,128)(2,1)} fusion(bf16[128,1152]{1,0:T(8,128)(2,1)} %copy-done.6, bf16[128,1152]{1,0:T(8,128)(2,1)} %copy-done.3, s32[128]{0:T(128)S(1)} %convert_element_type.78, f32[]{:T(128)} %bitcast.46, f32[]{:T(128)} %bitcast, s32[128]{0:T(128)S(1)} %bitcast.51, bf16[1,128,1152]{2,1,0:T(8,128)(2,1)} %param.6, ...), kind=kOutput, calls=%fused_computation.42 | convolution fusion | flops 76988416 | bytes 1181192 | tf_op jit(solution)/shard_map/dot_general | solution.py:27
  30.6 0.0 collective-permute-start.3
  30.6 0.0 copy-done.4
  30.6 1.5 %collective-permute-start.4 = (bf16[128,1152]{1,0:T(8,128)(2,1)S(1)}, bf16[128,1152]{1,0:T(8,128)(2,1)S(1)}, u32[]{:S(2)}, u32[]{:S(2)}) collective-permute-start(bf16[128,1152]{1,0:T(8,128)(2,1)S(1)} %copy-done.4), channel_id=1, source_target_pairs={{0,4},{4,8},{8,12},{12,16},{16,20},{20,24},{24,28},{28,0},{1,5},{5... | collective-permute-start | bytes 884744 | tf_op jit(solution)/shard_map/ppermute | solution.py:14
  32.1 0.1 collective-permute-start.5
  32.2 9.0 %collective-permute-done.5 = bf16[128]{0:T(256)(128)(2,1)S(1)} collective-permute-done((bf16[128]{0:T(256)(128)(2,1)S(1)}, bf16[128]{0:T(256)(128)(2,1)S(1)}, u32[]{:S(2)}, u32[]{:S(2)}) %collective-permute-start.5) | collective-permute-done | bytes 288 | tf_op jit(solution)/shard_map/ppermute | solution.py:14
  41.1 0.0 collective-permute-done.3
  41.1 0.0 collective-permute-done.4
  41.1 0.7 copy-done.5
  41.8 0.7 copy-done.7
  42.6 2.7 %fusion.27 = bf16[128,1152]{1,0:T(8,128)(2,1)} fusion(bf16[128,1152]{1,0:T(8,128)(2,1)} %copy-done.7, bf16[128,1152]{1,0:T(8,128)(2,1)} %copy-done.5, s32[128]{0:T(128)S(1)} %convert_element_type.83, f32[]{:T(128)} %bitcast.45, f32[]{:T(128)} %bitcast, s32[128]{0:T(128)S(1)} %bitcast.52, bf16[1,128,1152]{2,1,0:T(8,128)(2,1)} %param.6, f32[128]{0:T(128)} %add_sqrt_fusion.1), kind=kOutput, calls=%fused_computation.33 | convolution fusion | flops 76988416 | bytes 1181192 | tf_op jit(solution)/shard_map/dot_general | solution.py:27
  45.2 1.4 %collective-permute-start.6 = (bf16[128,1152]{1,0:T(8,128)(2,1)}, bf16[128,1152]{1,0:T(8,128)(2,1)S(1)}, u32[]{:S(2)}, u32[]{:S(2)}) collective-permute-start(bf16[128,1152]{1,0:T(8,128)(2,1)} %fusion.27), channel_id=1, source_target_pairs={{0,24},{4,28},{8,0},{12,4},{16,8},{20,12},{24,16},{28,20},{1,25},{... | collective-permute-start | bytes 884744 | tf_op jit(solution)/shard_map/ppermute | solution.py:14
  46.6 6.4 %collective-permute-done.6 = bf16[128,1152]{1,0:T(8,128)(2,1)S(1)} collective-permute-done((bf16[128,1152]{1,0:T(8,128)(2,1)}, bf16[128,1152]{1,0:T(8,128)(2,1)S(1)}, u32[]{:S(2)}, u32[]{:S(2)}) %collective-permute-start.6) | collective-permute-done | bytes 294944 | tf_op jit(solution)/shard_map/ppermute | solution.py:14
  53.1 0.2 multiply_reduce_fusion
  53.3 0.9 divide_convert_fusion
  54.2 0.0 all-gather.2.cloned.1.call-update
  54.2 0.0 reduce-scatter.4.cloned.1.call-start
  54.2 0.0 copy-done.2
  54.3 0.2 copy.12
  54.5 12.4 %all_to_all.19 = bf16[128,4,288]{0,2,1:T(8,128)(2,1)S(1)} all-to-all(bf16[128,4,288]{0,2,1:T(8,128)(2,1)S(1)} %bitcast.48), channel_id=1, replica_groups=mesh['dp'=8,'replica'=4] {'replica'}, dimensions={1} | all-to-all | bytes 589824 | tf_op jit(solution)/shard_map/all_to_all | solution.py:68
  66.9 19.3 %all-gather.2.cloned.1.call-done = bf16[512,1152]{1,0:T(8,128)(2,1)} async-done(((bf16[128,1152]{1,0:T(8,128)(2,1)}), bf16[512,1152]{1,0:T(8,128)(2,1)}) %all-gather.2.cloned.1.call-update) | async-done | bytes 1179664 | tf_op jit(solution)/shard_map/all_gather | solution.py:69
  86.2 2.9 %convolution_bitcast_fusion = f32[288,1152]{1,0:T(8,128)} fusion(bf16[512,1152]{1,0:T(8,128)(2,1)} %all-gather.2.cloned.1.call-done, bf16[128,4,288]{0,2,1:T(8,128)(2,1)S(1)} %all_to_all.19), kind=kOutput, calls=%fused_computation | convolution fusion | flops 339738624 | bytes 2801664 | tf_op jit(solution)/shard_map/dot_general | solution.py:27
  89.1 3.1 %copy.15 = f32[288,1152]{0,1:T(8,128)} copy(f32[288,1152]{1,0:T(8,128)} %convolution_bitcast_fusion) | data formatting | bytes 2654208
  92.3 0.0 reduce-scatter.4.cloned.1.call-update
  92.3 0.0 copy-done.1
  92.3 1.6 %fusion = bf16[1,128,1152]{2,1,0:T(8,128)(2,1)} fusion(bf16[128,1152]{1,0:T(8,128)(2,1)S(1)} %copy-done.1, bf16[1152,1152]{1,0:T(8,128)(2,1)S(1)} %copy-done), kind=kOutput, calls=%fused_computation.3 | convolution fusion | flops 339886080 | bytes 3244032 | tf_op jit(solution)/shard_map/dot_general | solution.py:65
  93.9 38.0 %reduce-scatter.4.cloned.1.call-done = f32[144,288]{1,0:T(8,128)} async-done(((f32[1152,288]{1,0:T(8,128)}), f32[144,288]{1,0:T(8,128)}) %reduce-scatter.4.cloned.1.call-update) | async-done | bytes 165904
  (8 shorter events, 0.0 us)
Async XLA Ops:
  7.2 3.9 %copy-start = (bf16[1152,1152]{1,0:T(8,128)(2,1)S(1)}, bf16[1152,1152]{1,0:T(8,128)(2,1)}, u32[]{:S(2)}) copy-start(bf16[1152,1152]{1,0:T(8,128)(2,1)} %param.8) | copy-start | bytes 7962628
  7.2 5.7 %copy-start.8 = (s32[1,128]{1,0:T(1,128)S(1)}, s32[1,128]{1,0:T(1,128)}, u32[]{:S(2)}) copy-start(s32[1,128]{1,0:T(1,128)} %param.11) | copy-start | bytes 1540
  7.2 79.0 %all-gather.2.cloned.1.call-start = ((), (), s32[]{:S(2)}) async-start(), calls=%async_computation.2 | async-start | bytes 1474560 | tf_op jit(solution)/shard_map/all_gather | solution.py:69
  15.4 11.2 %collective-permute-start = (bf16[128,1152]{1,0:T(8,128)(2,1)}, bf16[128,1152]{1,0:T(8,128)(2,1)S(1)}, u32[]{:S(2)}, u32[]{:S(2)}) collective-permute-start(bf16[128,1152]{1,0:T(8,128)(2,1)} %convolution_convert_fusion.1), channel_id=1, source_target_pairs={{0,4},{4,8},{8,12},{12,16},{16,20},{20,24},{24,28},{28,0},{1,5},{5... | collective-permute-start | bytes 884744 | tf_op jit(solution)/shard_map/ppermute | solution.py:14
  15.8 10.7 %collective-permute-start.1 = (bf16[128,1152]{1,0:T(8,128)(2,1)S(1)}, bf16[128,1152]{1,0:T(8,128)(2,1)S(1)}, u32[]{:S(2)}, u32[]{:S(2)}) collective-permute-start(bf16[128,1152]{1,0:T(8,128)(2,1)S(1)} %fusion.65), channel_id=1, source_target_pairs={{0,4},{4,8},{8,12},{12,16},{16,20},{20,24},{24,28},{28,0},{1,5},{5... | collective-permute-start | bytes 884744 | tf_op jit(solution)/shard_map/ppermute | solution.py:14
  18.4 8.1 %collective-permute-start.2 = (bf16[128]{0:T(256)(128)(2,1)S(1)}, bf16[128]{0:T(256)(128)(2,1)S(1)}, u32[]{:S(2)}, u32[]{:S(2)}) collective-permute-start(bf16[128]{0:T(256)(128)(2,1)S(1)} %get-tuple-element.8), channel_id=1, source_target_pairs={{0,4},{4,8},{8,12},{12,16},{16,20},{20,24},{24,28},{28,0},{1,5},{5... | collective-permute-start | bytes 776 | tf_op jit(solution)/shard_map/ppermute | solution.py:14
  26.5 0.7 copy-start.6
  27.3 0.7 copy-start.3
  28.0 2.7 %copy-start.4 = (bf16[128,1152]{1,0:T(8,128)(2,1)S(1)}, bf16[128,1152]{1,0:T(8,128)(2,1)}, u32[]{:S(2)}) copy-start(bf16[128,1152]{1,0:T(8,128)(2,1)} %copy-done.3) | copy-start | bytes 884740
  30.6 10.5 %collective-permute-start.3 = (bf16[128,1152]{1,0:T(8,128)(2,1)}, bf16[128,1152]{1,0:T(8,128)(2,1)S(1)}, u32[]{:S(2)}, u32[]{:S(2)}) collective-permute-start(bf16[128,1152]{1,0:T(8,128)(2,1)} %add_convert_fusion), channel_id=1, source_target_pairs={{0,4},{4,8},{8,12},{12,16},{16,20},{20,24},{24,28},{28,0},{1,5},{5... | collective-permute-start | bytes 884744 | tf_op jit(solution)/shard_map/ppermute | solution.py:14
  30.6 10.5 %collective-permute-start.4 = (bf16[128,1152]{1,0:T(8,128)(2,1)S(1)}, bf16[128,1152]{1,0:T(8,128)(2,1)S(1)}, u32[]{:S(2)}, u32[]{:S(2)}) collective-permute-start(bf16[128,1152]{1,0:T(8,128)(2,1)S(1)} %copy-done.4), channel_id=1, source_target_pairs={{0,4},{4,8},{8,12},{12,16},{16,20},{20,24},{24,28},{28,0},{1,5},{5... | collective-permute-start | bytes 884744 | tf_op jit(solution)/shard_map/ppermute | solution.py:14
  32.1 9.0 %collective-permute-start.5 = (bf16[128]{0:T(256)(128)(2,1)S(1)}, bf16[128]{0:T(256)(128)(2,1)S(1)}, u32[]{:S(2)}, u32[]{:S(2)}) collective-permute-start(bf16[128]{0:T(256)(128)(2,1)S(1)} %collective-permute-done.2), channel_id=1, source_target_pairs={{0,4},{4,8},{8,12},{12,16},{16,20},{20,24},{24,28},{28,0},{1,5},{5... | collective-permute-start | bytes 776 | tf_op jit(solution)/shard_map/ppermute | solution.py:14
  41.1 0.7 copy-start.5
  41.8 0.7 copy-start.7
  42.6 11.7 %copy-start.2 = (bf16[1,128,1152]{2,1,0:T(8,128)(2,1)S(1)}, bf16[1,128,1152]{2,1,0:T(8,128)(2,1)}, u32[]{:S(2)}) copy-start(bf16[1,128,1152]{2,1,0:T(8,128)(2,1)} %param.7) | copy-start | bytes 884740
  45.2 7.8 %collective-permute-start.6 = (bf16[128,1152]{1,0:T(8,128)(2,1)}, bf16[128,1152]{1,0:T(8,128)(2,1)S(1)}, u32[]{:S(2)}, u32[]{:S(2)}) collective-permute-start(bf16[128,1152]{1,0:T(8,128)(2,1)} %fusion.27), channel_id=1, source_target_pairs={{0,24},{4,28},{8,0},{12,4},{16,8},{20,12},{24,16},{28,20},{1,25},{... | collective-permute-start | bytes 884744 | tf_op jit(solution)/shard_map/ppermute | solution.py:14
  54.2 77.7 %reduce-scatter.4.cloned.1.call-start = ((), (), s32[]{:S(2)}) async-start(), calls=%async_computation.3 | async-start | bytes 1990656
  89.1 3.1 %copy-start.1 = (bf16[128,1152]{1,0:T(8,128)(2,1)S(1)}, bf16[128,1152]{1,0:T(8,128)(2,1)}, u32[]{:S(2)}) copy-start(bf16[128,1152]{1,0:T(8,128)(2,1)} %divide_convert_fusion) | copy-start | bytes 884740
Sparse Core Ops, SparseCore 0:
  54.3 31.8 all-gather.1
  92.4 39.4 reduce-scatter.3
where the time goes:
time: 139 us
  waiting for transfers between devices  80.8 us (58%)
  between operations  15.6 us (11%)
  matrix products  13.9 us (10%)
  blocking collectives  12.4 us (9%)
  local copies, waits for them, and re-layouts  6.21 us (4%)
  starting transfers between devices  6.1 us (4%)
  other arithmetic  3.63 us (3%)
    unnamed x3, waiting for transfers between devices  38 us
    ppermute x7, waiting for transfers between devices, shifted(): lax.ppermute(shard, axis, [(i, (i + by) % size) for i in range(size)])  23.5 us
    all_gather x1, waiting for transfers between devices, shards(): lax.all_gather(dzed, 'replica', axis=0, tiled=True)  19.3 us
    all_to_all x1, blocking collectives, shards(): lax.all_to_all(feats, 'replica', split_axis=1, concat_axis=0, tiled=True)  12.4 us
    dot_general x4, matrix products, left_product(): lax.dot_general(first, second, (((0,), (0,)), ((), ())), preferred_elemen...  10.7 us
    unnamed x20, local copies, waits for them, and re-layouts  6.21 us
    ppermute x7, starting transfers between devices, shifted(): lax.ppermute(shard, axis, [(i, (i + by) % size) for i in range(size)])  6.02 us
  transfers between devices with their start and end apart: 9, of which 5 were waited for; matrix products, arithmetic and copies ran while one was open for 1% of the time, Pallas kernels for 0%

commit v1 on v0

v1 whole, which is shorter than its diff:
```python
import jax
import jax.numpy as jnp
from jax import lax
from jax.sharding import PartitionSpec as P

HOPS = 3
LOSS_SCALE = 2048.0


def rotated(x, axis, by):
    size = lax.axis_size(axis)
    return lax.ppermute(x, axis, [(i, (i + by) % size) for i in range(size)])


def swapped(x, axis, mask):
    size = lax.axis_size(axis)
    return lax.ppermute(x, axis, [(i, i ^ mask) for i in range(size)])


def shards(image_emb, text_feat, head_w, log_scale, bias, pair_ids):
    images = image_emb[0]
    feats = text_feat[0]
    ids = pair_ids[0]
    rows = feats.shape[0]
    dp = lax.axis_size("dp")
    replica = lax.axis_size("replica")
    chips = dp // 2
    factor = LOSS_SCALE / (HOPS * rows)
    scale = jnp.exp(log_scale[0])
    shift_b = bias[0]

    others = [rotated(images, "dp", -k) for k in range(1, HOPS)]
    other_ids = [rotated(ids, "dp", -k) for k in range(1, HOPS)]
    held = [feats] + [swapped(feats, "dp", 2 * k) for k in range(1, chips)]
    held2 = [swapped(f, "dp", 1) for f in held]

    raw = jnp.dot(feats, head_w, preferred_element_type=jnp.float32)
    norms = jnp.sqrt(jnp.sum(raw * raw, axis=1, keepdims=True) + 1e-06)
    unit_txt = raw / norms
    txt_bf = unit_txt.astype(jnp.bfloat16)

    imgs = jnp.concatenate([images] + others, axis=0)
    img_ids = jnp.concatenate([ids] + other_ids, axis=0)
    img32 = imgs.astype(jnp.float32)
    unit_img = (img32 / jnp.sqrt(jnp.sum(img32 * img32, axis=1, keepdims=True) + 1e-06)).astype(
        jnp.bfloat16
    )
    sims = lax.dot_general(
        txt_bf, unit_img, (((1,), (1,)), ((), ())), preferred_element_type=jnp.float32
    )
    match = (ids[:, None] == img_ids[None, :]).astype(jnp.float32)
    grads = (factor * (jax.nn.sigmoid(scale * sims + shift_b) - match)).astype(jnp.bfloat16)
    dvec = scale * jnp.dot(grads, unit_img, preferred_element_type=jnp.float32)
    dzed = ((dvec - unit_txt * jnp.sum(unit_txt * dvec, axis=1, keepdims=True)) / norms).astype(
        jnp.bfloat16
    )
    grad_feat = lax.dot_general(
        dzed, head_w, (((1,), (1,)), ((), ())), preferred_element_type=jnp.float32
    ).astype(jnp.bfloat16)

    me = lax.axis_index("dp")
    chip, core = me // 2, me % 2
    cols = head_w.shape[1] // dp
    dz_t = dzed.T
    parts = [
        lax.dynamic_slice_in_dim(dz_t, (chip ^ k) * 2 * cols, 2 * cols, 0) for k in range(chips)
    ]
    got = [parts[0]] + [swapped(parts[k], "dp", 2 * k) for k in range(1, chips)]
    got2 = [swapped(g, "dp", 1) for g in got]
    dz_all = jnp.concatenate(got + got2, axis=1)
    dz_all = lax.dynamic_slice_in_dim(dz_all, core * cols, cols, 0)
    feats_all = jnp.concatenate(held + held2, axis=0)
    local_head = lax.dot_general(
        feats_all, dz_all, (((0,), (1,)), ((), ())), preferred_element_type=jnp.float32
    )
    r = lax.axis_index("replica")
    depth = head_w.shape[0] // replica
    head_grad = lax.dynamic_slice_in_dim(local_head, r * depth, depth, 0)
    local_bf = local_head.astype(jnp.bfloat16)
    for k in range(1, replica):
        piece = lax.dynamic_slice_in_dim(local_bf, (r ^ k) * depth, depth, 0)
        head_grad = head_grad + swapped(piece, "replica", k).astype(jnp.float32)
    return (grad_feat[None], head_grad)


def solution(mesh):
    return jax.shard_map(
        shards,
        mesh=mesh,
        in_specs=(
            P("replica", "dp", None),
            P("replica", "dp", None),
            P(),
            P(),
            P(),
            P("replica", "dp"),
        ),
        out_specs=(P("replica", "dp", None), P("replica", "dp")),
        check_vma=False,
    )
```

time: 139 us -> 56.9 us (0.41)
  waiting for transfers between devices: 80.8 us -> 14.9 us
  starting transfers between devices: 6.1 us -> 20.8 us
  between operations: 15.6 us -> 2.28 us
  blocking collectives: 12.4 us -> 0 us
  matrix products: 13.9 us -> 7.26 us
    unnamed x3 -> x0, waiting for transfers between devices: 38 us -> none
    all_gather x1 -> x0, waiting for transfers between devices: 19.3 us -> none  [shards(): lax.all_gather(dzed, 'replica', axis=0, tiled=True)]
    ppermute x7 -> x21, starting transfers between devices: 6.02 us -> 20.8 us  [the longest x17 15.1 us: swapped(): return lax.ppermute(x, axis, [(i, i ^ mask) for i in range(size)])]
    all_to_all x1 -> x0, blocking collectives: 12.4 us -> none  [shards(): lax.all_to_all(feats, 'replica', split_axis=1, concat_axis=0, tiled=True)]
    ppermute x7 -> x21, waiting for transfers between devices: 23.5 us -> 14.9 us  [the longest x17 9.18 us: swapped(): return lax.ppermute(x, axis, [(i, i ^ mask) for i in range(size)])]
    dot_general x4 -> x2, matrix products: 10.7 us -> 3.98 us  [the longest x1 3.2 us: shards(): dvec = scale * jnp.dot(grads, unit_img, preferred_element_type=jnp.float32)]
    unnamed x20 -> x24, local copies, waits for them, and re-layouts: 6.21 us -> 6.51 us
  transfers between devices with their start and end apart: 9 -> 21, of which waited for: 5 -> 5; matrix products, arithmetic and copies ran while one was open for 1% -> 29% of each run, Pallas kernels for 0% -> 0%
where the time goes in v1:
time: 56.9 us; the launch traced here: 56.5 us
  starting transfers between devices  20.8 us (37%)
  waiting for transfers between devices  14.9 us (26%)
  matrix products  7.26 us (13%)
  local copies, waits for them, and re-layouts  6.95 us (12%)
  other arithmetic  4.27 us (8%)
  between operations  2.28 us (4%)
    ppermute x17, starting transfers between devices, swapped(): return lax.ppermute(x, axis, [(i, i ^ mask) for i in range(size)])  15.1 us
    ppermute x17, waiting for transfers between devices, swapped(): return lax.ppermute(x, axis, [(i, i ^ mask) for i in range(size)])  9.18 us
    unnamed x24, local copies, waits for them, and re-layouts  6.51 us
    ppermute x4, waiting for transfers between devices, rotated(): return lax.ppermute(x, axis, [(i, (i + by) % size) for i in range(size)])  5.75 us
    ppermute x4, starting transfers between devices, rotated(): return lax.ppermute(x, axis, [(i, (i + by) % size) for i in range(size)])  5.75 us
    dot_general x1, matrix products, shards(): dvec = scale * jnp.dot(grads, unit_img, preferred_element_type=jnp.float32)  3.2 us
    dot_general x1, matrix products, shards(): raw = jnp.dot(feats, head_w, preferred_element_type=jnp.float32)  1.65 us
    dot_general x1, matrix products, shards(): lax.dot_general(dzed, head_w, (((1,), (1,)), ((), ())), preferred_element...  1.63 us
  transfers between devices with their start and end apart: 21, of which 5 were waited for; matrix products, arithmetic and copies ran while one was open for 29% of the time, Pallas kernels for 0%

profile of v1, /device:TPU:0, one launch (start us, length us, event | category | flops | bytes accessed | tf_op | source)
XLA Modules:
  0.0 56.5 jit_solution(8669717600742063544)
XLA Ops:
  0.6 0.0 copy-start
  0.6 0.0 copy-start.3
  0.7 0.0 copy-start.2
  0.7 3.9 %collective-permute-start.1 = (bf16[128,1152]{1,0:T(8,128)(2,1)}, bf16[128,1152]{1,0:T(8,128)(2,1)}, u32[]{:S(2)}, u32[]{:S(2)}) collective-permute-start(bf16[128,1152]{1,0:T(8,128)(2,1)} %bitcast.30), channel_id=1, source_target_pairs={{0,24},{4,28},{8,0},{12,4},{16,8},{20,12},{24,16},{28,20},{1,25},{... | collective-permute-start | bytes 884744 | tf_op jit(solution)/shard_map/ppermute | solution.py:12
  4.6 0.0 collective-permute-start
  4.6 1.1 %collective-permute-start.3 = (s32[128]{0:T(128)}, s32[128]{0:T(128)S(1)}, u32[]{:S(2)}, u32[]{:S(2)}) collective-permute-start(s32[128]{0:T(128)} %bitcast.34), channel_id=1, source_target_pairs={{0,24},{4,28},{8,0},{12,4},{16,8},{20,12},{24,16},{28,20},{1,25},{... | collective-permute-start | bytes 1544 | tf_op jit(solution)/shard_map/ppermute | solution.py:12
  5.7 0.7 %collective-permute-start.2 = (s32[128]{0:T(128)}, s32[128]{0:T(128)S(1)}, u32[]{:S(2)}, u32[]{:S(2)}) collective-permute-start(s32[128]{0:T(128)} %bitcast.35), channel_id=1, source_target_pairs={{0,28},{4,0},{8,4},{12,8},{16,12},{20,16},{24,20},{28,24},{1,29},{... | collective-permute-start | bytes 1544 | tf_op jit(solution)/shard_map/ppermute | solution.py:12
  6.4 0.6 %collective-permute-start.4 = (bf16[128,1152]{1,0:T(8,128)(2,1)}, bf16[128,1152]{1,0:T(8,128)(2,1)}, u32[]{:S(2)}, u32[]{:S(2)}) collective-permute-start(bf16[128,1152]{1,0:T(8,128)(2,1)} %bitcast.26), channel_id=1, source_target_pairs={{0,8},{4,12},{8,0},{12,4},{16,24},{20,28},{24,16},{28,20},{1,9},{5... | collective-permute-start | bytes 884744 | tf_op jit(solution)/shard_map/ppermute | solution.py:17
  7.0 1.7 %constant_dynamic-update-slice_fusion.7 = bf16[1024,1152]{1,0:T(8,128)(2,1)} fusion(bf16[1,128,1152]{2,1,0:T(8,128)(2,1)} %param.7), kind=kLoop, calls=%fused_computation.45 | loop fusion | bytes 589824
  8.7 1.7 %multiply_reduce_fusion.1 = (f32[128]{0:T(128)S(1)}, f32[128,1152]{1,0:T(8,128)S(1)}) fusion(bf16[1152,1152]{1,0:T(8,128)(2,1)S(1)} %copy-done, bf16[1,128,1152]{2,1,0:T(8,128)(2,1)} %param.7), kind=kOutput, calls=%fused_computation.20 | convolution fusion | flops 340033408 | bytes 3539456 | tf_op jit(solution)/shard_map/dot_general | solution.py:37
  11.8 5.7 %collective-permute-done.3 = s32[128]{0:T(128)S(1)} collective-permute-done((s32[128]{0:T(128)}, s32[128]{0:T(128)S(1)}, u32[]{:S(2)}, u32[]{:S(2)}) %collective-permute-start.3) | collective-permute-done | bytes 544 | tf_op jit(solution)/shard_map/ppermute | solution.py:12
  17.6 1.4 %collective-permute-start.5 = (bf16[128,1152]{1,0:T(8,128)(2,1)S(1)}, bf16[128,1152]{1,0:T(8,128)(2,1)}, u32[]{:S(2)}, u32[]{:S(2)}) collective-permute-start(bf16[128,1152]{1,0:T(8,128)(2,1)S(1)} %bitcast.27), channel_id=1, source_target_pairs={{0,16},{4,20},{8,24},{12,28},{16,0},{20,4},{24,8},{28,12},{1,17},{... | collective-permute-start | bytes 884744 | tf_op jit(solution)/shard_map/ppermute | solution.py:17
  19.0 0.5 copy-done.4
  19.5 2.4 %collective-permute-start.6 = (bf16[128,1152]{1,0:T(8,128)(2,1)S(1)}, bf16[128,1152]{1,0:T(8,128)(2,1)}, u32[]{:S(2)}, u32[]{:S(2)}) collective-permute-start(bf16[128,1152]{1,0:T(8,128)(2,1)S(1)} %bitcast.28), channel_id=1, source_target_pairs={{0,24},{4,28},{8,16},{12,20},{16,8},{20,12},{24,0},{28,4},{1,25},{... | collective-permute-start | bytes 884744 | tf_op jit(solution)/shard_map/ppermute | solution.py:17
  21.9 0.7 %pad_add_fusion = s32[384]{0:T(512)S(1)} fusion(s32[128]{0:T(128)S(1)} %collective-permute-done.3, s32[128]{0:T(128)} %copy-done.4, s32[128]{0:T(128)S(1)} %bitcast.37), kind=kLoop, calls=%fused_computation.58 | loop fusion | flops 768 | bytes 3072 | tf_op jit(solution)/shard_map/concatenate | solution.py:43
  22.6 0.0 collective-permute-done.1
  22.6 0.1 collective-permute-start.7
  22.7 0.0 collective-permute-done
  22.7 1.4 %fusion.1 = f32[384]{0:T(512)S(1)} fusion(bf16[128,1152]{1,0:T(8,128)(2,1)} %collective-permute-done.1, bf16[128,1152]{1,0:T(8,128)(2,1)} %collective-permute-done, bf16[128,1152]{1,0:T(8,128)(2,1)} %bitcast.32), kind=kLoop, calls=%fused_computation.5 | loop fusion | flops 3538560 | bytes 886272 | tf_op jit(solution)/shard_map/reduce_sum | solution.py:45
  24.1 3.2 %multiply_reduce_fusion = (f32[128]{0:T(128)S(1)}, f32[128,1152]{1,0:T(8,128)}) fusion(f32[128,1152]{1,0:T(8,128)S(1)} %get-tuple-element.11, f32[128]{0:T(128)S(1)} %add_sqrt_fusion.1, f32[384]{0:T(512)S(1)} %add_sqrt_fusion, bf16[128,1152]{1,0:T(8,128)(2,1)} %collective-permute-done.1, bf16[128,1152]{1,0:T(8,128)(2,1)} %collective-permute-done, ...), kind=kOutput, calls=%fused_computation.19 | convolution fusion | flops 234946432 | bytes 2069000 | tf_op jit(solution)/shard_map/dot_general | solution.py:53
  27.3 1.4 %divide_convert_fusion = bf16[128,1152]{1,0:T(8,128)(2,1)S(1)} fusion(f32[128,1152]{1,0:T(8,128)} %get-tuple-element.13, f32[128]{0:T(128)S(1)} %get-tuple-element.12, f32[128]{0:T(128)S(1)} %add_sqrt_fusion.1, f32[128,1152]{1,0:T(8,128)S(1)} %get-tuple-element.11), kind=kLoop, calls=%fused_computation.18 | loop fusion | flops 737280 | bytes 1475584 | tf_op jit(solution)/shard_map/convert_element_type | solution.py:54
  28.7 0.2 dynamic-slice_bitcast_fusion
  28.9 0.1 constant_dynamic-update-slice_fusion.15
  29.0 0.1 collective-permute-start.11
  29.1 1.6 %collective-permute-start.12 = (bf16[288,128]{0,1:T(8,128)(2,1)S(1)}, bf16[288,128]{0,1:T(8,128)(2,1)S(1)}, u32[]{:S(2)}, u32[]{:S(2)}) collective-permute-start(bf16[288,128]{0,1:T(8,128)(2,1)S(1)} %get-tuple-element.8), channel_id=1, source_target_pairs={{0,16},{4,20},{8,24},{12,28},{16,0},{20,4},{24,8},{28,12},{1,17},{... | collective-permute-start | bytes 221192 | tf_op jit(solution)/shard_map/ppermute | solution.py:17
  30.7 1.0 %constant_dynamic-update-slice_fusion.6 = bf16[1024,1152]{1,0:T(8,128)(2,1)S(1)} fusion(bf16[1024,1152]{1,0:T(8,128)(2,1)S(1)} %copy-done.1, bf16[128,1152]{1,0:T(8,128)(2,1)} %collective-permute-done.4), kind=kLoop, calls=%fused_computation.44 | loop fusion | bytes 589824
  31.6 0.0 collective-permute-done.5
  31.7 2.4 %collective-permute-start.13 = (bf16[288,128]{0,1:T(8,128)(2,1)S(1)}, bf16[288,128]{0,1:T(8,128)(2,1)S(1)}, u32[]{:S(2)}, u32[]{:S(2)}) collective-permute-start(bf16[288,128]{0,1:T(8,128)(2,1)S(1)} %get-tuple-element.7), channel_id=1, source_target_pairs={{0,24},{4,28},{8,16},{12,20},{16,8},{20,12},{24,0},{28,4},{1,25},{... | collective-permute-start | bytes 221192 | tf_op jit(solution)/shard_map/ppermute | solution.py:17
  34.0 1.0 %constant_dynamic-update-slice_fusion.5 = bf16[1024,1152]{1,0:T(8,128)(2,1)S(1)} fusion(bf16[1024,1152]{1,0:T(8,128)(2,1)S(1)} %constant_dynamic-update-slice_fusion.6, bf16[128,1152]{1,0:T(8,128)(2,1)} %collective-permute-done.5), kind=kLoop, calls=%fused_computation.43 | loop fusion | bytes 589824
  35.0 0.1 collective-permute-start.14
  35.1 1.0 %constant_dynamic-update-slice_fusion.4 = bf16[1024,1152]{1,0:T(8,128)(2,1)S(1)} fusion(bf16[1024,1152]{1,0:T(8,128)(2,1)S(1)} %constant_dynamic-update-slice_fusion.5, bf16[128,1152]{1,0:T(8,128)(2,1)} %collective-permute-done.6), kind=kLoop, calls=%fused_computation.42 | loop fusion | bytes 589824
  36.1 0.6 collective-permute-start.8
  36.7 1.0 %constant_dynamic-update-slice_fusion.3 = bf16[1024,1152]{1,0:T(8,128)(2,1)S(1)} fusion(bf16[1024,1152]{1,0:T(8,128)(2,1)S(1)} %constant_dynamic-update-slice_fusion.4, bf16[128,1152]{1,0:T(8,128)(2,1)} %collective-permute-done.7), kind=kLoop, calls=%fused_computation.41 | loop fusion | bytes 589824
  37.7 0.1 collective-permute-start.9
  37.8 0.6 collective-permute-start.10
  38.4 0.1 collective-permute-start.15
  38.5 0.6 collective-permute-start.16
  39.1 0.8 %collective-permute-done.15 = bf16[288,128]{0,1:T(8,128)(2,1)S(1)} collective-permute-done((bf16[288,128]{0,1:T(8,128)(2,1)S(1)}, bf16[288,128]{0,1:T(8,128)(2,1)S(1)}, u32[]{:S(2)}, u32[]{:S(2)}) %collective-permute-start.15) | collective-permute-done | bytes 73760 | tf_op jit(solution)/shard_map/ppermute | solution.py:17
  39.9 0.2 collective-permute-start.17
  40.1 1.1 %collective-permute-done.17 = bf16[288,128]{0,1:T(8,128)(2,1)S(1)} collective-permute-done((bf16[288,128]{0,1:T(8,128)(2,1)S(1)}, bf16[288,128]{0,1:T(8,128)(2,1)S(1)}, u32[]{:S(2)}, u32[]{:S(2)}) %collective-permute-start.17) | collective-permute-done | bytes 73760 | tf_op jit(solution)/shard_map/ppermute | solution.py:17
  41.4 0.8 %fusion.38 = (bf16[1152,144]{0,1:T(8,128)(2,1)S(1)}, f32[1152,144]{0,1:T(8,128)S(1)}) fusion(bf16[1024,1152]{1,0:T(8,128)(2,1)S(1)} %constant_dynamic-update-slice_fusion, bf16[288,1024]{0,1:T(8,128)(2,1)S(1)} %constant_dynamic-update-slice_fusion.8, s32[]{:T(128)S(6)} %select_n.44), kind=kOutput, calls=%fused_computation.66 | convolution fusion | flops 339904512 | bytes 3878916 | tf_op jit(solution)/shard_map/dot_general | solution.py:73
  42.1 0.2 constant_dynamic-slice_fusion.2
  42.4 3.7 %collective-permute-start.20 = (bf16[288,144]{0,1:T(8,128)(2,1)S(1)}, bf16[288,144]{0,1:T(8,128)(2,1)S(1)}, u32[]{:S(2)}, u32[]{:S(2)}) collective-permute-start(bf16[288,144]{0,1:T(8,128)(2,1)S(1)} %get-tuple-element.5), channel_id=1, source_target_pairs={{0,3},{1,2},{2,1},{3,0},{4,7},{5,6},{6,5},{7,4},{8,11},{9,10},{10,... | collective-permute-start | bytes 248840 | tf_op jit(solution)/shard_map/ppermute | solution.py:17
  46.0 0.8 %collective-permute-start.18 = (bf16[288,144]{0,1:T(8,128)(2,1)S(1)}, bf16[288,144]{0,1:T(8,128)(2,1)S(1)}, u32[]{:S(2)}, u32[]{:S(2)}) collective-permute-start(bf16[288,144]{0,1:T(8,128)(2,1)S(1)} %get-tuple-element.4), channel_id=1, source_target_pairs={{0,1},{1,0},{2,3},{3,2},{4,5},{5,4},{6,7},{7,6},{8,9},{9,8},{10,11... | collective-permute-start | bytes 248840 | tf_op jit(solution)/shard_map/ppermute | solution.py:17
  46.8 1.6 %fusion = bf16[1,128,1152]{2,1,0:T(8,128)(2,1)} fusion(bf16[128,1152]{1,0:T(8,128)(2,1)S(1)} %divide_convert_fusion, bf16[1152,1152]{1,0:T(8,128)(2,1)S(1)} %copy-done), kind=kOutput, calls=%fused_computation.2 | convolution fusion | flops 339886080 | bytes 3244032 | tf_op jit(solution)/shard_map/dot_general | solution.py:57
  48.4 1.8 %collective-permute-done.20 = bf16[288,144]{0,1:T(8,128)(2,1)S(1)} collective-permute-done((bf16[288,144]{0,1:T(8,128)(2,1)S(1)}, bf16[288,144]{0,1:T(8,128)(2,1)S(1)}, u32[]{:S(2)}, u32[]{:S(2)}) %collective-permute-start.20) | collective-permute-done | bytes 82976 | tf_op jit(solution)/shard_map/ppermute | solution.py:17
  50.2 5.5 %collective-permute-done.19 = bf16[288,144]{0,1:T(8,128)(2,1)S(1)} collective-permute-done((bf16[288,144]{0,1:T(8,128)(2,1)S(1)}, bf16[288,144]{0,1:T(8,128)(2,1)S(1)}, u32[]{:S(2)}, u32[]{:S(2)}) %collective-permute-start.19) | collective-permute-done | bytes 82976 | tf_op jit(solution)/shard_map/ppermute | solution.py:17
  55.7 0.8 %convert_add_fusion = f32[288,144]{0,1:T(8,128)} fusion(bf16[288,144]{0,1:T(8,128)(2,1)S(1)} %collective-permute-done.20, bf16[288,144]{0,1:T(8,128)(2,1)S(1)} %collective-permute-done.19, bf16[288,144]{0,1:T(8,128)(2,1)S(1)} %collective-permute-done.18, f32[1152,144]{0,1:T(8,128)S(1)} %get-tuple-element.15, s32[]{:T(128)S(6)} %select_n.45), kind=kLoop, calls=%fused_computation.25 | loop fusion | flops 248832 | bytes 580612 | tf_op jit(solution)/shard_map/add | solution.py:82
  (32 shorter events, 0.3 us)
Async XLA Ops:
  0.6 8.1 %copy-start = (bf16[1152,1152]{1,0:T(8,128)(2,1)S(1)}, bf16[1152,1152]{1,0:T(8,128)(2,1)}, u32[]{:S(2)}) copy-start(bf16[1152,1152]{1,0:T(8,128)(2,1)} %param.8) | copy-start | bytes 7962628
  0.6 21.3 %copy-start.3 = (s32[1,128]{1,0:T(1,128)S(1)}, s32[1,128]{1,0:T(1,128)}, u32[]{:S(2)}) copy-start(s32[1,128]{1,0:T(1,128)} %param.11) | copy-start | bytes 1540
  0.7 16.9 %copy-start.2 = (bf16[1,128,1152]{2,1,0:T(8,128)(2,1)S(1)}, bf16[1,128,1152]{2,1,0:T(8,128)(2,1)}, u32[]{:S(2)}) copy-start(bf16[1,128,1152]{2,1,0:T(8,128)(2,1)} %param.7) | copy-start | bytes 884740
  0.7 21.9 %collective-permute-start.1 = (bf16[128,1152]{1,0:T(8,128)(2,1)}, bf16[128,1152]{1,0:T(8,128)(2,1)}, u32[]{:S(2)}, u32[]{:S(2)}) collective-permute-start(bf16[128,1152]{1,0:T(8,128)(2,1)} %bitcast.30), channel_id=1, source_target_pairs={{0,24},{4,28},{8,0},{12,4},{16,8},{20,12},{24,16},{28,20},{1,25},{... | collective-permute-start | bytes 884744 | tf_op jit(solution)/shard_map/ppermute | solution.py:12
  4.6 18.0 %collective-permute-start = (bf16[128,1152]{1,0:T(8,128)(2,1)}, bf16[128,1152]{1,0:T(8,128)(2,1)}, u32[]{:S(2)}, u32[]{:S(2)}) collective-permute-start(bf16[128,1152]{1,0:T(8,128)(2,1)} %bitcast.31), channel_id=1, source_target_pairs={{0,28},{4,0},{8,4},{12,8},{16,12},{20,16},{24,20},{28,24},{1,29},{... | collective-permute-start | bytes 884744 | tf_op jit(solution)/shard_map/ppermute | solution.py:12
  4.6 12.9 %collective-permute-start.3 = (s32[128]{0:T(128)}, s32[128]{0:T(128)S(1)}, u32[]{:S(2)}, u32[]{:S(2)}) collective-permute-start(s32[128]{0:T(128)} %bitcast.34), channel_id=1, source_target_pairs={{0,24},{4,28},{8,0},{12,4},{16,8},{20,12},{24,16},{28,20},{1,25},{... | collective-permute-start | bytes 1544 | tf_op jit(solution)/shard_map/ppermute | solution.py:12
  5.7 13.2 %collective-permute-start.2 = (s32[128]{0:T(128)}, s32[128]{0:T(128)S(1)}, u32[]{:S(2)}, u32[]{:S(2)}) collective-permute-start(s32[128]{0:T(128)} %bitcast.35), channel_id=1, source_target_pairs={{0,28},{4,0},{8,4},{12,8},{16,12},{20,16},{24,20},{28,24},{1,29},{... | collective-permute-start | bytes 1544 | tf_op jit(solution)/shard_map/ppermute | solution.py:12
  6.4 22.7 %collective-permute-start.4 = (bf16[128,1152]{1,0:T(8,128)(2,1)}, bf16[128,1152]{1,0:T(8,128)(2,1)}, u32[]{:S(2)}, u32[]{:S(2)}) collective-permute-start(bf16[128,1152]{1,0:T(8,128)(2,1)} %bitcast.26), channel_id=1, source_target_pairs={{0,8},{4,12},{8,0},{12,4},{16,24},{20,28},{24,16},{28,20},{1,9},{5... | collective-permute-start | bytes 884744 | tf_op jit(solution)/shard_map/ppermute | solution.py:17
  17.6 14.1 %collective-permute-start.5 = (bf16[128,1152]{1,0:T(8,128)(2,1)S(1)}, bf16[128,1152]{1,0:T(8,128)(2,1)}, u32[]{:S(2)}, u32[]{:S(2)}) collective-permute-start(bf16[128,1152]{1,0:T(8,128)(2,1)S(1)} %bitcast.27), channel_id=1, source_target_pairs={{0,16},{4,20},{8,24},{12,28},{16,0},{20,4},{24,8},{28,12},{1,17},{... | collective-permute-start | bytes 884744 | tf_op jit(solution)/shard_map/ppermute | solution.py:17
  19.0 0.5 copy-start.4
  19.5 15.6 %collective-permute-start.6 = (bf16[128,1152]{1,0:T(8,128)(2,1)S(1)}, bf16[128,1152]{1,0:T(8,128)(2,1)}, u32[]{:S(2)}, u32[]{:S(2)}) collective-permute-start(bf16[128,1152]{1,0:T(8,128)(2,1)S(1)} %bitcast.28), channel_id=1, source_target_pairs={{0,24},{4,28},{8,16},{12,20},{16,8},{20,12},{24,0},{28,4},{1,25},{... | collective-permute-start | bytes 884744 | tf_op jit(solution)/shard_map/ppermute | solution.py:17
  22.6 13.5 %collective-permute-start.7 = (bf16[128,1152]{1,0:T(8,128)(2,1)S(1)}, bf16[128,1152]{1,0:T(8,128)(2,1)}, u32[]{:S(2)}, u32[]{:S(2)}) collective-permute-start(bf16[128,1152]{1,0:T(8,128)(2,1)S(1)} %bitcast.29), channel_id=1, source_target_pairs={{0,4},{4,0},{8,12},{12,8},{16,20},{20,16},{24,28},{28,24},{1,5},{5... | collective-permute-start | bytes 884744 | tf_op jit(solution)/shard_map/ppermute | solution.py:17
  27.3 3.4 %copy-start.1 = (bf16[1024,1152]{1,0:T(8,128)(2,1)S(1)}, bf16[1024,1152]{1,0:T(8,128)(2,1)}, u32[]{:S(2)}) copy-start(bf16[1024,1152]{1,0:T(8,128)(2,1)} %constant_dynamic-update-slice_fusion.7) | copy-start | bytes 7077892
  29.0 8.7 %collective-permute-start.11 = (bf16[288,128]{0,1:T(8,128)(2,1)S(1)}, bf16[288,128]{0,1:T(8,128)(2,1)S(1)}, u32[]{:S(2)}, u32[]{:S(2)}) collective-permute-start(bf16[288,128]{0,1:T(8,128)(2,1)S(1)} %get-tuple-element.9), channel_id=1, source_target_pairs={{0,8},{4,12},{8,0},{12,4},{16,24},{20,28},{24,16},{28,20},{1,9},{5... | collective-permute-start | bytes 221192 | tf_op jit(solution)/shard_map/ppermute | solution.py:17
  29.1 8.7 %collective-permute-start.12 = (bf16[288,128]{0,1:T(8,128)(2,1)S(1)}, bf16[288,128]{0,1:T(8,128)(2,1)S(1)}, u32[]{:S(2)}, u32[]{:S(2)}) collective-permute-start(bf16[288,128]{0,1:T(8,128)(2,1)S(1)} %get-tuple-element.8), channel_id=1, source_target_pairs={{0,16},{4,20},{8,24},{12,28},{16,0},{20,4},{24,8},{28,12},{1,17},{... | collective-permute-start | bytes 221192 | tf_op jit(solution)/shard_map/ppermute | solution.py:17
  31.7 6.7 %collective-permute-start.13 = (bf16[288,128]{0,1:T(8,128)(2,1)S(1)}, bf16[288,128]{0,1:T(8,128)(2,1)S(1)}, u32[]{:S(2)}, u32[]{:S(2)}) collective-permute-start(bf16[288,128]{0,1:T(8,128)(2,1)S(1)} %get-tuple-element.7), channel_id=1, source_target_pairs={{0,24},{4,28},{8,16},{12,20},{16,8},{20,12},{24,0},{28,4},{1,25},{... | collective-permute-start | bytes 221192 | tf_op jit(solution)/shard_map/ppermute | solution.py:17
  35.0 3.5 %collective-permute-start.14 = (bf16[288,128]{0,1:T(8,128)(2,1)S(1)}, bf16[288,128]{0,1:T(8,128)(2,1)S(1)}, u32[]{:S(2)}, u32[]{:S(2)}) collective-permute-start(bf16[288,128]{0,1:T(8,128)(2,1)S(1)} %get-tuple-element.3), channel_id=1, source_target_pairs={{0,4},{4,0},{8,12},{12,8},{16,20},{20,16},{24,28},{28,24},{1,5},{5... | collective-permute-start | bytes 221192 | tf_op jit(solution)/shard_map/ppermute | solution.py:17
  36.1 5.1 %collective-permute-start.8 = (bf16[128,1152]{1,0:T(8,128)(2,1)}, bf16[128,1152]{1,0:T(8,128)(2,1)S(1)}, u32[]{:S(2)}, u32[]{:S(2)}) collective-permute-start(bf16[128,1152]{1,0:T(8,128)(2,1)} %collective-permute-done.4), channel_id=1, source_target_pairs={{0,4},{4,0},{8,12},{12,8},{16,20},{20,16},{24,28},{28,24},{1,5},{5... | collective-permute-start | bytes 884744 | tf_op jit(solution)/shard_map/ppermute | solution.py:17
  37.7 3.6 %collective-permute-start.9 = (bf16[128,1152]{1,0:T(8,128)(2,1)}, bf16[128,1152]{1,0:T(8,128)(2,1)S(1)}, u32[]{:S(2)}, u32[]{:S(2)}) collective-permute-start(bf16[128,1152]{1,0:T(8,128)(2,1)} %collective-permute-done.5), channel_id=1, source_target_pairs={{0,4},{4,0},{8,12},{12,8},{16,20},{20,16},{24,28},{28,24},{1,5},{5... | collective-permute-start | bytes 884744 | tf_op jit(solution)/shard_map/ppermute | solution.py:17
  37.8 3.5 %collective-permute-start.10 = (bf16[128,1152]{1,0:T(8,128)(2,1)}, bf16[128,1152]{1,0:T(8,128)(2,1)S(1)}, u32[]{:S(2)}, u32[]{:S(2)}) collective-permute-start(bf16[128,1152]{1,0:T(8,128)(2,1)} %collective-permute-done.6), channel_id=1, source_target_pairs={{0,4},{4,0},{8,12},{12,8},{16,20},{20,16},{24,28},{28,24},{1,5},{5... | collective-permute-start | bytes 884744 | tf_op jit(solution)/shard_map/ppermute | solution.py:17
  38.4 1.5 %collective-permute-start.15 = (bf16[288,128]{0,1:T(8,128)(2,1)S(1)}, bf16[288,128]{0,1:T(8,128)(2,1)S(1)}, u32[]{:S(2)}, u32[]{:S(2)}) collective-permute-start(bf16[288,128]{0,1:T(8,128)(2,1)S(1)} %collective-permute-done.11), channel_id=1, source_target_pairs={{0,4},{4,0},{8,12},{12,8},{16,20},{20,16},{24,28},{28,24},{1,5},{5... | collective-permute-start | bytes 221192 | tf_op jit(solution)/shard_map/ppermute | solution.py:17
  38.5 1.6 %collective-permute-start.16 = (bf16[288,128]{0,1:T(8,128)(2,1)S(1)}, bf16[288,128]{0,1:T(8,128)(2,1)S(1)}, u32[]{:S(2)}, u32[]{:S(2)}) collective-permute-start(bf16[288,128]{0,1:T(8,128)(2,1)S(1)} %collective-permute-done.12), channel_id=1, source_target_pairs={{0,4},{4,0},{8,12},{12,8},{16,20},{20,16},{24,28},{28,24},{1,5},{5... | collective-permute-start | bytes 221192 | tf_op jit(solution)/shard_map/ppermute | solution.py:17
  39.9 1.3 %collective-permute-start.17 = (bf16[288,128]{0,1:T(8,128)(2,1)S(1)}, bf16[288,128]{0,1:T(8,128)(2,1)S(1)}, u32[]{:S(2)}, u32[]{:S(2)}) collective-permute-start(bf16[288,128]{0,1:T(8,128)(2,1)S(1)} %collective-permute-done.13), channel_id=1, source_target_pairs={{0,4},{4,0},{8,12},{12,8},{16,20},{20,16},{24,28},{28,24},{1,5},{5... | collective-permute-start | bytes 221192 | tf_op jit(solution)/shard_map/ppermute | solution.py:17
  42.4 7.9 %collective-permute-start.20 = (bf16[288,144]{0,1:T(8,128)(2,1)S(1)}, bf16[288,144]{0,1:T(8,128)(2,1)S(1)}, u32[]{:S(2)}, u32[]{:S(2)}) collective-permute-start(bf16[288,144]{0,1:T(8,128)(2,1)S(1)} %get-tuple-element.5), channel_id=1, source_target_pairs={{0,3},{1,2},{2,1},{3,0},{4,7},{5,6},{6,5},{7,4},{8,11},{9,10},{10,... | collective-permute-start | bytes 248840 | tf_op jit(solution)/shard_map/ppermute | solution.py:17
  46.0 9.7 %collective-permute-start.19 = (bf16[288,144]{0,1:T(8,128)(2,1)S(1)}, bf16[288,144]{0,1:T(8,128)(2,1)S(1)}, u32[]{:S(2)}, u32[]{:S(2)}) collective-permute-start(bf16[288,144]{0,1:T(8,128)(2,1)S(1)} %get-tuple-element.6), channel_id=1, source_target_pairs={{0,2},{1,3},{2,0},{3,1},{4,6},{5,7},{6,4},{7,5},{8,10},{9,11},{10,... | collective-permute-start | bytes 248840 | tf_op jit(solution)/shard_map/ppermute | solution.py:17
  46.0 9.7 %collective-permute-start.18 = (bf16[288,144]{0,1:T(8,128)(2,1)S(1)}, bf16[288,144]{0,1:T(8,128)(2,1)S(1)}, u32[]{:S(2)}, u32[]{:S(2)}) collective-permute-start(bf16[288,144]{0,1:T(8,128)(2,1)S(1)} %get-tuple-element.4), channel_id=1, source_target_pairs={{0,1},{1,0},{2,3},{3,2},{4,5},{5,4},{6,7},{7,6},{8,9},{9,8},{10,11... | collective-permute-start | bytes 248840 | tf_op jit(solution)/shard_map/ppermute | solution.py:17

commit v2 on v1

--- a/solution.py
+++ b/solution.py
@@ -1,10 +1,22 @@
+import functools
+
 import jax
 import jax.numpy as jnp
 from jax import lax
+from jax.experimental import pallas as pl
+from jax.experimental.pallas import tpu as pltpu
 from jax.sharding import PartitionSpec as P
 
 HOPS = 3
 LOSS_SCALE = 2048.0
+LANES = 128
+VMEM = pl.BlockSpec(memory_space=pltpu.VMEM)
+SMEM = pl.BlockSpec(memory_space=pltpu.SMEM)
+NT = (((1,), (1,)), ((), ()))
+
+
+def grant(mib):
+    return pltpu.CompilerParams(vmem_limit_bytes=mib * 2**20)
 
 
 def rotated(x, axis, by):
@@ -17,7 +29,233 @@
     return lax.ppermute(x, axis, [(i, i ^ mask) for i in range(size)])
 
 
-def shards(image_emb, text_feat, head_w, log_scale, bias, pair_ids):
+def after(x, first):
+    return lax.optimization_barrier((x, first))[0]
+
+
+def in_order(core, own, other):
+    first = jnp.where(core == 0, own, other)
+    second = jnp.where(core == 0, other, own)
+    return jnp.concatenate([first, second], axis=0)
+
+
+def pair_term(factor, scale, shift_b, txt_bf, row_ids, images, image_ids, skip):
+    wide = images.astype(jnp.float32)
+    total = jnp.sum(wide * wide, axis=1, keepdims=True) + 1e-06
+    unit_img = (wide * (1.0 / jnp.sqrt(total))).astype(jnp.bfloat16)
+    sims = lax.dot_general(txt_bf, unit_img, NT, preferred_element_type=jnp.float32)
+    rows = sims.shape[0] // 2
+    match = (row_ids == image_ids).astype(jnp.float32)
+    grads = factor * (jax.nn.sigmoid(scale * sims + shift_b) - match)
+    row = lax.broadcasted_iota(jnp.int32, sims.shape, 0) >= rows
+    col = lax.broadcasted_iota(jnp.int32, sims.shape, 1) >= rows
+    away = (row == bool(skip[0])) & (col == bool(skip[1]))
+    grads = jnp.where(away, 0.0, grads).astype(jnp.bfloat16)
+    return jnp.dot(grads, unit_img, preferred_element_type=jnp.float32)
+
+
+def own_kernel(
+    factor, scalars, place, feats, feats2, head_w, img, img2, ids,
+    unit_out, inverse_out, ids_out, term_out,
+):
+    core = place[0]
+    both = in_order(core, feats[...], feats2[...])
+    text = jnp.dot(both, head_w[...], preferred_element_type=jnp.float32)
+    inverse = 1.0 / jnp.sqrt(jnp.sum(text * text, axis=1, keepdims=True) + 1e-06)
+    unit_txt = text * inverse
+    unit_out[...] = unit_txt
+    rows = text.shape[0]
+    inverse_out[...] = jnp.broadcast_to(inverse, (rows, LANES))
+    chip_ids = jnp.concatenate([ids[:1, :], ids[1:2, :]], axis=1)
+    row_ids = jnp.broadcast_to(chip_ids, (LANES, rows)).T
+    ids_out[...] = row_ids
+    row_ids = jnp.concatenate([row_ids, row_ids], axis=1)
+    txt_bf = unit_txt.astype(jnp.bfloat16)
+    images = in_order(core, img[...], img2[...])
+    term_out[...] = pair_term(
+        factor, scalars[0], scalars[1], txt_bf, row_ids, images, chip_ids, (1, 0)
+    )
+
+
+def loss_kernel(
+    factor, cols, scalars, place, far, far2, ids, unit, inverse, ids_in, term,
+    dz_out, *rest,
+):
+    core, chip = place[0], place[1]
+    *parts, straight, flipped = rest
+    unit_txt = unit[...]
+    txt_bf = unit_txt.astype(jnp.bfloat16)
+    chip_ids = jnp.concatenate([ids[:1, :], ids[1:2, :]], axis=1)
+    row_ids = jnp.concatenate([ids_in[...], ids_in[...]], axis=1)
+    images = in_order(core, far[...], far2[...])
+    scale = scalars[0]
+    dvec = term[...] + pair_term(
+        factor, scale, scalars[1], txt_bf, row_ids, images, chip_ids, (0, 1)
+    )
+    dvec = scale * dvec
+    along = jnp.sum(unit_txt * dvec, axis=1, keepdims=True)
+    dzed = ((dvec - unit_txt * along) * inverse[:, :1]).astype(jnp.bfloat16)
+    straight[...] = dzed
+    flipped[...] = dzed.T
+    rows = dz_out.shape[0]
+    dz_out[...] = straight[pl.ds(pl.multiple_of(core * rows, 16), rows), :]
+    for k, part in enumerate(parts):
+        start = pl.multiple_of((2 * (chip ^ k) + core) * cols, 16)
+        part[...] = flipped[pl.ds(start, cols), :]
+
+
+def packing(cols, depth):
+    full, rest = divmod(depth, LANES)
+    slots = 0
+    if rest:
+        slots = max(s for s in range(1, LANES // rest + 1) if cols % (16 * s) == 0)
+    return full, rest, slots, cols * full + (cols // slots if slots else 0)
+
+
+def product_kernel(chips, cols, depth, replica, place, *refs):
+    grads, feats = refs[:chips], refs[chips : 3 * chips]
+    outs = refs[3 * chips : 3 * chips + replica]
+    feats_all, packed, sem = refs[3 * chips + replica :]
+    core = place[0]
+    rows = feats[0].shape[0]
+    copies = []
+    for i, (mine, theirs) in enumerate(zip(feats[:chips], feats[chips:])):
+        for j, (block, slot) in enumerate(((mine, core), (theirs, 1 - core))):
+            start = pl.multiple_of((2 * i + slot) * rows, rows)
+            copies.append(
+                pltpu.make_async_copy(
+                    block, feats_all.at[pl.ds(start, rows), :], sem.at[2 * i + j]
+                )
+            )
+    for copy in copies:
+        copy.start()
+    left = jnp.concatenate([g[...] for g in grads], axis=1)
+    for copy in copies:
+        copy.wait()
+    full, rest, slots, _ = packing(cols, depth)
+    local = jnp.dot(left, feats_all[...], preferred_element_type=jnp.float32)
+    for r in range(replica):
+        block = local[:, r * depth : (r + 1) * depth]
+        for i in range(full):
+            packed[r, i * cols : (i + 1) * cols, :] = block[:, i * LANES : (i + 1) * LANES]
+        if slots:
+            tall = cols // slots
+            pieces = [block[s * tall : (s + 1) * tall, full * LANES :] for s in range(slots)]
+            pieces.append(jnp.zeros((tall, LANES - slots * rest), jnp.float32))
+            packed[r, full * cols :, :] = jnp.concatenate(pieces, axis=1)
+    for k, out in enumerate(outs):
+        out[...] = packed[place[2] ^ k].astype(out.dtype)
+
+
+def final_kernel(cols, depth, *refs):
+    out = refs[-1]
+    total = refs[0][...].astype(jnp.float32)
+    for ref in refs[1:-1]:
+        total = total + ref[...].astype(jnp.float32)
+    full, rest, slots, _ = packing(cols, depth)
+    for i in range(full):
+        out[:, i * LANES : (i + 1) * LANES] = total[i * cols : (i + 1) * cols, :]
+    if slots:
+        tall = cols // slots
+        for s in range(slots):
+            out[s * tall : (s + 1) * tall, full * LANES :] = total[
+                full * cols :, s * rest : (s + 1) * rest
+            ]
+
+
+def box_shards(image_emb, text_feat, head_w, log_scale, bias, pair_ids):
+    images = image_emb[0]
+    feats = text_feat[0]
+    rows, width = images.shape
+    dp, replica = lax.axis_size("dp"), lax.axis_size("replica")
+    chips = dp // 2
+    cols, depth = width // dp, head_w.shape[0] // replica
+    factor = LOSS_SCALE / (HOPS * rows)
+    scalars = jnp.concatenate([jnp.exp(log_scale), bias])
+    me, group = lax.axis_index("dp"), lax.axis_index("replica")
+    place = jnp.stack([me & 1, me >> 1, group])
+
+    def f32(*shape):
+        return jax.ShapeDtypeStruct(shape, jnp.float32)
+
+    def bf16(*shape):
+        return jax.ShapeDtypeStruct(shape, jnp.bfloat16)
+
+    far = rotated(images, "dp", -2)
+    feats2 = swapped(feats, "dp", 1)
+    images2 = swapped(images, "dp", 1)
+    chip_ids = in_order(me & 1, pair_ids, swapped(pair_ids, "dp", 1))
+    far_ids = rotated(jnp.tile(chip_ids, (1, 1)), "dp", -2)
+
+    unit_txt, inverse, row_ids, own_term = pl.pallas_call(
+        functools.partial(own_kernel, factor),
+        out_shape=[
+            f32(2 * rows, width),
+            f32(2 * rows, LANES),
+            jax.ShapeDtypeStruct((2 * rows, LANES), jnp.int32),
+            f32(2 * rows, width),
+        ],
+        in_specs=[SMEM] * 2 + [VMEM] * 6,
+        out_specs=[VMEM] * 4,
+        compiler_params=grant(24),
+        cost_estimate=pl.CostEstimate(flops=10000000000, bytes_accessed=1, transcendentals=0),
+        name="own",
+    )(scalars, place, feats, feats2, head_w, images, images2, chip_ids)
+
+    feats_soon = after(feats, feats2)
+    held = [swapped(feats_soon, "dp", 2 * k) for k in range(1, chips)]
+    far2 = swapped(far, "dp", 1)
+
+    dzed, *parts = pl.pallas_call(
+        functools.partial(loss_kernel, factor, cols),
+        out_shape=[bf16(rows, width)] + [bf16(cols, 2 * rows)] * chips,
+        in_specs=[SMEM] * 2 + [VMEM] * 7,
+        out_specs=[VMEM] * (1 + chips),
+        scratch_shapes=[
+            pltpu.VMEM((2 * rows, width), jnp.bfloat16),
+            pltpu.VMEM((width, 2 * rows), jnp.bfloat16),
+        ],
+        compiler_params=grant(24),
+        cost_estimate=pl.CostEstimate(flops=1, bytes_accessed=1, transcendentals=0),
+        name="loss",
+    )(scalars, place, far, far2, far_ids, unit_txt, inverse, row_ids, own_term)
+    got = [swapped(parts[k], "dp", 2 * k) for k in range(1, chips)]
+    held2 = [swapped(after(f, got[0]), "dp", 1) for f in held]
+    grad_feat = lax.dot_general(dzed, head_w, NT, preferred_element_type=jnp.float32).astype(
+        jnp.bfloat16
+    )
+    grad_feat, got = lax.optimization_barrier((grad_feat, got))
+
+    tall = packing(cols, depth)[3]
+    own, *pieces = pl.pallas_call(
+        functools.partial(product_kernel, chips, cols, depth, replica),
+        out_shape=[f32(tall, LANES)] + [bf16(tall, LANES)] * (replica - 1),
+        in_specs=[SMEM] + [VMEM] * chips + [pl.BlockSpec(memory_space=pl.ANY)] * dp,
+        out_specs=[VMEM] * replica,
+        scratch_shapes=[
+            pltpu.VMEM((dp * rows, head_w.shape[0]), jnp.bfloat16),
+            pltpu.VMEM((replica, tall, LANES), jnp.float32),
+            pltpu.SemaphoreType.DMA((dp,)),
+        ],
+        compiler_params=grant(24),
+        cost_estimate=pl.CostEstimate(flops=1, bytes_accessed=1, transcendentals=0),
+        name="product",
+    )(place, parts[0], *got, feats, *held, feats2, *held2)
+    order = sorted(range(1, replica), key=lambda k: (-(k & (replica // 2)), k))
+    sums = [swapped(pieces[k - 1], "replica", k) for k in order]
+    head_grad = pl.pallas_call(
+        functools.partial(final_kernel, cols, depth),
+        out_shape=f32(cols, depth),
+        in_specs=[VMEM] * replica,
+        out_specs=VMEM,
+        compiler_params=grant(8),
+        cost_estimate=pl.CostEstimate(flops=1, bytes_accessed=1, transcendentals=0),
+        name="final",
+    )(own, *sums)
+    return (grad_feat[None], head_grad.T)
+
+
+def general_shards(image_emb, text_feat, head_w, log_scale, bias, pair_ids):
     images = image_emb[0]
     feats = text_feat[0]
     ids = pair_ids[0]
@@ -83,6 +321,16 @@
     return (grad_feat[None], head_grad)
 
 
+def shards(image_emb, text_feat, head_w, log_scale, bias, pair_ids):
+    args = (image_emb, text_feat, head_w, log_scale, bias, pair_ids)
+    dp, replica = lax.axis_size("dp"), lax.axis_size("replica")
+    rows, width = image_emb.shape[1:]
+    cols, depth = width // dp, head_w.shape[0] // replica
+    if rows == LANES and cols % 16 == 0:
+        return box_shards(*args)
+    return general_shards(*args)
+
+
 def solution(mesh):
     return jax.shard_map(
         shards,

time: 56.9 us -> 42.8 us (0.75)
  Pallas kernels: 0 us -> 7.4 us
  matrix products: 7.26 us -> 1.63 us
  waiting for transfers between devices: 14.9 us -> 9.34 us
  starting transfers between devices: 20.8 us -> 17.3 us
  other arithmetic: 4.27 us -> 0.82 us
  local copies, waits for them, and re-layouts: 6.95 us -> 3.68 us
    pallas_call x0 -> x4, Pallas kernels: none -> 7.4 us  [the longest x1 2.57 us: box_shards(): pl.pallas_call(functools.partial(own_kernel, factor), out_shape=[f32(2 *...]
    dot_general x4 -> x1, matrix products: 7.26 us -> 1.63 us  [box_shards(): lax.dot_general(dzed, head_w, NT, preferred_element_type=jnp.float32)]
    ppermute x4 -> x2, waiting for transfers between devices: 5.75 us -> 0.95 us  [rotated(): return lax.ppermute(x, axis, [(i, (i + by) % size) for i in range(size)])]
    unnamed x24 -> x10, local copies, waits for them, and re-layouts: 6.51 us -> 3.68 us
    ppermute x17 -> x16, starting transfers between devices: 15.1 us -> 13.2 us  [swapped(): return lax.ppermute(x, axis, [(i, i ^ mask) for i in range(size)])]
    ppermute x4 -> x2, starting transfers between devices: 5.75 us -> 4.09 us  [rotated(): return lax.ppermute(x, axis, [(i, (i + by) % size) for i in range(size)])]
    reduce_sum x1 -> x0, other arithmetic: 1.39 us -> none  [shards(): jnp.sum(img32 * img32, axis=1, keepdims=True) + 1e-06]
    convert_element_type x1 -> x0, other arithmetic: 1.38 us -> none  [shards(): ((dvec - unit_txt * jnp.sum(unit_txt * dvec, axis=1, keepdims=True)) / no...]
  transfers between devices with their start and end apart: 21 -> 18, of which waited for: 5 -> 6; matrix products, arithmetic and copies ran while one was open for 29% -> 6% of each run, Pallas kernels for 0% -> 11%
where the time goes in v2:
time: 42.8 us; the launch traced here: 42.3 us
  starting transfers between devices  17.3 us (40%)
  waiting for transfers between devices  9.34 us (22%)
  Pallas kernels  7.4 us (17%)
  local copies, waits for them, and re-layouts  3.68 us (9%)
  between operations  2.05 us (5%)
  matrix products  1.63 us (4%)
  other arithmetic  0.82 us (2%)
    ppermute x16, starting transfers between devices, swapped(): return lax.ppermute(x, axis, [(i, i ^ mask) for i in range(size)])  13.2 us
    ppermute x16, waiting for transfers between devices, swapped(): return lax.ppermute(x, axis, [(i, i ^ mask) for i in range(size)])  8.4 us
    ppermute x2, starting transfers between devices, rotated(): return lax.ppermute(x, axis, [(i, (i + by) % size) for i in range(size)])  4.09 us
    unnamed x10, local copies, waits for them, and re-layouts  3.68 us
    pallas_call x1, Pallas kernels, box_shards(): pl.pallas_call(functools.partial(own_kernel, factor), out_shape=[f32(2 *...  2.57 us
    pallas_call x1, Pallas kernels, box_shards(): pl.pallas_call(functools.partial(loss_kernel, factor, cols), out_shape=[b...  2.2 us
    pallas_call x1, Pallas kernels, box_shards(): pl.pallas_call(functools.partial(product_kernel, chips, cols, depth, repl...  1.86 us
    dot_general x1, matrix products, box_shards(): lax.dot_general(dzed, head_w, NT, preferred_element_type=jnp.float32)  1.63 us
  transfers between devices with their start and end apart: 18, of which 6 were waited for; matrix products, arithmetic and copies ran while one was open for 6% of the time, Pallas kernels for 11%

profile of v2, /device:TPU:0, one launch (start us, length us, event | category | flops | bytes accessed | tf_op | source)
XLA Modules:
  0.0 42.3 jit_solution(18376050872634623808)
XLA Ops:
  0.6 0.5 %collective-permute-start.5 = (bf16[128,1152]{1,0:T(8,128)(2,1)}, bf16[128,1152]{1,0:T(8,128)(2,1)S(1)}, u32[]{:S(2)}, u32[]{:S(2)}) collective-permute-start(bf16[128,1152]{1,0:T(8,128)(2,1)} %bitcast.15), channel_id=1, source_target_pairs={{0,4},{4,0},{8,12},{12,8},{16,20},{20,16},{24,28},{28,24},{1,5},{5... | collective-permute-start | bytes 884744 | tf_op jit(solution)/shard_map/ppermute | solution.py:29
  1.1 3.5 %collective-permute-start = (bf16[128,1152]{1,0:T(8,128)(2,1)}, bf16[128,1152]{1,0:T(8,128)(2,1)S(1)}, u32[]{:S(2)}, u32[]{:S(2)}) collective-permute-start(bf16[128,1152]{1,0:T(8,128)(2,1)} %bitcast.16), channel_id=1, source_target_pairs={{0,24},{4,28},{8,0},{12,4},{16,8},{20,12},{24,16},{28,20},{1,25},{... | collective-permute-start | bytes 884744 | tf_op jit(solution)/shard_map/ppermute | solution.py:24
  4.7 0.2 collective-permute-start.2
  4.8 0.3 collective-permute-start.4
  6.5 0.1 pad_maximum_fusion.scalars
  6.6 0.1 pad_add_fusion.1.place
  6.7 0.0 collective-permute-done.2
  6.7 0.7 %broadcast_select_fusion.1 = (s32[1,128]{1,0:T(1,128)S(1)}, s32[1,128]{1,0:T(1,128)S(1)}) fusion(s32[1,128]{1,0:T(1,128)} %param.11, s32[1,128]{1,0:T(1,128)S(1)} %collective-permute-done.2, pred[]{:T(512)S(6)} %eq.4), kind=kLoop, calls=%fused_computation.3 | loop fusion | flops 256 | bytes 2049 | tf_op jit(solution)/shard_map/jit(_where)/select_n | solution.py:37
  7.3 0.6 %collective-permute-start.3 = (s32[2,128]{1,0:T(2,128)S(1)}, s32[2,128]{1,0:T(2,128)S(1)}, u32[]{:S(2)}, u32[]{:S(2)}) collective-permute-start(s32[2,128]{1,0:T(2,128)S(1)} %pad_add_fusion.ids), channel_id=1, source_target_pairs={{0,24},{4,28},{8,0},{12,4},{16,8},{20,12},{24,16},{28,20},{1,25},{... | collective-permute-start | bytes 3080 | tf_op jit(solution)/shard_map/ppermute | solution.py:24
  7.9 0.0 collective-permute-done.4.feats2.refs_8_
  7.9 1.5 %collective-permute-start.9 = (bf16[128,1152]{1,0:T(8,128)(2,1)}, bf16[128,1152]{1,0:T(8,128)(2,1)S(1)}, u32[]{:S(2)}, u32[]{:S(2)}) collective-permute-start(bf16[128,1152]{1,0:T(8,128)(2,1)} %bitcast.10), channel_id=1, source_target_pairs={{0,8},{4,12},{8,0},{12,4},{16,24},{20,28},{24,16},{28,20},{1,9},{5... | collective-permute-start | bytes 884744 | tf_op jit(solution)/shard_map/ppermute | solution.py:29
  9.4 0.5 %collective-permute-start.10 = (bf16[128,1152]{1,0:T(8,128)(2,1)}, bf16[128,1152]{1,0:T(8,128)(2,1)S(1)}, u32[]{:S(2)}, u32[]{:S(2)}) collective-permute-start(bf16[128,1152]{1,0:T(8,128)(2,1)} %bitcast.11), channel_id=1, source_target_pairs={{0,16},{4,20},{8,24},{12,28},{16,0},{20,4},{24,8},{28,12},{1,17},{... | collective-permute-start | bytes 884744 | tf_op jit(solution)/shard_map/ppermute | solution.py:29
  9.9 0.0 collective-permute-done.5.img2
  9.9 1.5 %collective-permute-start.11 = (bf16[128,1152]{1,0:T(8,128)(2,1)}, bf16[128,1152]{1,0:T(8,128)(2,1)S(1)}, u32[]{:S(2)}, u32[]{:S(2)}) collective-permute-start(bf16[128,1152]{1,0:T(8,128)(2,1)} %bitcast.12), channel_id=1, source_target_pairs={{0,24},{4,28},{8,16},{12,20},{16,8},{20,12},{24,0},{28,4},{1,25},{... | collective-permute-start | bytes 884744 | tf_op jit(solution)/shard_map/ppermute | solution.py:29
  11.4 0.9 %collective-permute-done.far = bf16[128,1152]{1,0:T(8,128)(2,1)S(1)} collective-permute-done((bf16[128,1152]{1,0:T(8,128)(2,1)}, bf16[128,1152]{1,0:T(8,128)(2,1)S(1)}, u32[]{:S(2)}, u32[]{:S(2)}) %collective-permute-start) | collective-permute-done | bytes 294944 | tf_op jit(solution)/shard_map/ppermute | solution.py:24
  12.4 0.0 collective-permute-start.1
  12.4 1.7 %copy-done = bf16[1152,1152]{1,0:T(8,128)(2,1)S(1)} copy-done((bf16[1152,1152]{1,0:T(8,128)(2,1)S(1)}, bf16[1152,1152]{1,0:T(8,128)(2,1)}, u32[]{:S(2)}) %copy-start) | copy-done | bytes 2654232
  14.1 1.0 %copy-done.2 = bf16[1,128,1152]{2,1,0:T(8,128)(2,1)S(1)} copy-done((bf16[1,128,1152]{2,1,0:T(8,128)(2,1)S(1)}, bf16[1,128,1152]{2,1,0:T(8,128)(2,1)}, u32[]{:S(2)}) %copy-start.2) | copy-done | bytes 294936
  15.1 1.0 %copy-done.4 = bf16[1,128,1152]{2,1,0:T(8,128)(2,1)S(1)} copy-done((bf16[1,128,1152]{2,1,0:T(8,128)(2,1)S(1)}, bf16[1,128,1152]{2,1,0:T(8,128)(2,1)}, u32[]{:S(2)}) %copy-start.4) | copy-done | bytes 294936
  16.0 2.6 %own.1 = (f32[256,1152]{1,0:T(8,128)S(1)}, f32[256,128]{1,0:T(8,128)S(1)}, s32[256,128]{1,0:T(8,128)S(1)}, f32[256,1152]{1,0:T(8,128)S(1)}) custom-call(f32[2]{0:T(128)S(1)} %pad_maximum_fusion.scalars, s32[3]{0:T(128)S(1)} %pad_add_fusion.1.place, bf16[128,1152]{1,0:T(8,128)(2,1)S(1)} %bitcast.13, ...), custom_call_target="tpu_custom_call" | custom-call | flops 10000000000 | bytes 1 | tf_op jit(solution)/shard_map/own/pallas_call | solution.py:190
  18.6 0.0 copy-start.1
  18.6 0.0 collective-permute-done.3.ids
  18.6 0.0 collective-permute-done.1.far2
  18.6 0.0 copy-start.3
  18.7 2.2 %loss.1 = (bf16[128,1152]{1,0:T(8,128)(2,1)S(1)}, bf16[144,256]{1,0:T(8,128)(2,1)S(1)}, bf16[144,256]{1,0:T(8,128)(2,1)S(1)}, bf16[144,256]{1,0:T(8,128)(2,1)S(1)}, bf16[144,256]{1,0:T(8,128)(2,1)S(1)}) custom-call(f32[2]{0:T(128)S(1)} %pad_maximum_fusion.scalars, s32[3]{0:T(128)S(1)} %pad_add_fusion.1.place, ...), custom_call_target="tpu_custom_call" | custom-call | flops 1 | bytes 1 | tf_op jit(solution)/shard_map/loss/pallas_call | solution.py:209
  20.9 2.3 %collective-permute-start.6 = (bf16[144,256]{1,0:T(8,128)(2,1)S(1)}, bf16[144,256]{1,0:T(8,128)(2,1)S(1)}, u32[]{:S(2)}, u32[]{:S(2)}) collective-permute-start(bf16[144,256]{1,0:T(8,128)(2,1)S(1)} %get-tuple-element.28), channel_id=1, source_target_pairs={{0,8},{4,12},{8,0},{12,4},{16,24},{20,28},{24,16},{28,20},{1,9},{5... | collective-permute-start | bytes 221192 | tf_op jit(solution)/shard_map/ppermute | solution.py:29
  23.2 1.6 %collective-permute-start.7 = (bf16[144,256]{1,0:T(8,128)(2,1)S(1)}, bf16[144,256]{1,0:T(8,128)(2,1)S(1)}, u32[]{:S(2)}, u32[]{:S(2)}) collective-permute-start(bf16[144,256]{1,0:T(8,128)(2,1)S(1)} %get-tuple-element.29), channel_id=1, source_target_pairs={{0,16},{4,20},{8,24},{12,28},{16,0},{20,4},{24,8},{28,12},{1,17},{... | collective-permute-start | bytes 221192 | tf_op jit(solution)/shard_map/ppermute | solution.py:29
  24.8 0.0 collective-permute-done.9.refs_5_
  24.8 0.0 collective-permute-start.8
  24.8 1.7 %collective-permute-done.6.refs_1_ = bf16[144,256]{1,0:T(8,128)(2,1)S(1)} collective-permute-done((bf16[144,256]{1,0:T(8,128)(2,1)S(1)}, bf16[144,256]{1,0:T(8,128)(2,1)S(1)}, u32[]{:S(2)}, u32[]{:S(2)}) %collective-permute-start.6) | collective-permute-done | bytes 73760 | tf_op jit(solution)/shard_map/ppermute | solution.py:29
  26.5 0.0 collective-permute-start.12
  26.5 0.0 collective-permute-done.10.refs_6_
  26.5 0.5 %collective-permute-start.13 = (bf16[128,1152]{1,0:T(8,128)(2,1)S(1)}, bf16[128,1152]{1,0:T(8,128)(2,1)S(1)}, u32[]{:S(2)}, u32[]{:S(2)}) collective-permute-start(bf16[128,1152]{1,0:T(8,128)(2,1)S(1)} %collective-permute-done.10.refs_6_), channel_id=1, source_target_pairs={{0,4},{4,0},{8,12},{12,8},{16,20},{20,16},{24,28},{28,24},{1,5},{5... | collective-permute-start | bytes 884744 | tf_op jit(solution)/shard_map/ppermute | solution.py:29
  27.0 0.0 collective-permute-done.11.refs_7_
  27.0 0.1 collective-permute-start.14
  27.1 1.6 %convolution_convert_fusion = bf16[128,1152]{1,0:T(8,128)(2,1)} fusion(bf16[128,1152]{1,0:T(8,128)(2,1)S(1)} %get-tuple-element.27, bf16[1152,1152]{1,0:T(8,128)(2,1)S(1)} %copy-done.1), kind=kOutput, calls=%fused_computation | convolution fusion | flops 339886080 | bytes 3244032 | tf_op jit(solution)/shard_map/dot_general | solution.py:224
  28.7 1.3 %collective-permute-done.8.refs_3_ = bf16[144,256]{1,0:T(8,128)(2,1)S(1)} collective-permute-done((bf16[144,256]{1,0:T(8,128)(2,1)S(1)}, bf16[144,256]{1,0:T(8,128)(2,1)S(1)}, u32[]{:S(2)}, u32[]{:S(2)}) %collective-permute-start.8) | collective-permute-done | bytes 73760 | tf_op jit(solution)/shard_map/ppermute | solution.py:29
  30.0 0.0 collective-permute-done.12.refs_9_
  30.0 0.0 collective-permute-done.13.refs_10_
  30.0 0.0 collective-permute-done.14.refs_11_
  30.0 1.9 %product.1 = (f32[336,128]{1,0:T(8,128)S(1)}, bf16[336,128]{1,0:T(8,128)(2,1)S(1)}, bf16[336,128]{1,0:T(8,128)(2,1)S(1)}, bf16[336,128]{1,0:T(8,128)(2,1)S(1)}) custom-call(s32[3]{0:T(128)S(1)} %pad_add_fusion.1.place, bf16[144,256]{1,0:T(8,128)(2,1)S(1)} %get-tuple-element.32.refs_0_, bf16[144,256]{1,0:T(8,128)(2,1)S(1)} %collective-permute-done.6.refs_1_, ...), custom_call_target="tpu_custom_call" | custom-call | flops 1 | bytes 1 | tf_op jit(solution)/shard_map/product/pallas_call | solution.py:230
  31.9 2.7 %collective-permute-start.15 = (bf16[336,128]{1,0:T(8,128)(2,1)S(1)}, bf16[336,128]{1,0:T(8,128)(2,1)S(1)}, u32[]{:S(2)}, u32[]{:S(2)}) collective-permute-start(bf16[336,128]{1,0:T(8,128)(2,1)S(1)} %get-tuple-element.41), channel_id=1, source_target_pairs={{0,2},{1,3},{2,0},{3,1},{4,6},{5,7},{6,4},{7,5},{8,10},{9,11},{10,... | collective-permute-start | bytes 258056 | tf_op jit(solution)/shard_map/ppermute | solution.py:29
  34.6 1.4 %collective-permute-start.16 = (bf16[336,128]{1,0:T(8,128)(2,1)S(1)}, bf16[336,128]{1,0:T(8,128)(2,1)S(1)}, u32[]{:S(2)}, u32[]{:S(2)}) collective-permute-start(bf16[336,128]{1,0:T(8,128)(2,1)S(1)} %get-tuple-element.42), channel_id=1, source_target_pairs={{0,3},{1,2},{2,1},{3,0},{4,7},{5,6},{6,5},{7,4},{8,11},{9,10},{10,... | collective-permute-start | bytes 258056 | tf_op jit(solution)/shard_map/ppermute | solution.py:29
  35.9 0.2 collective-permute-start.17
  36.2 3.7 %collective-permute-done.15.refs_1_ = bf16[336,128]{1,0:T(8,128)(2,1)S(1)} collective-permute-done((bf16[336,128]{1,0:T(8,128)(2,1)S(1)}, bf16[336,128]{1,0:T(8,128)(2,1)S(1)}, u32[]{:S(2)}, u32[]{:S(2)}) %collective-permute-start.15) | collective-permute-done | bytes 86048 | tf_op jit(solution)/shard_map/ppermute | solution.py:29
  39.8 1.5 %collective-permute-done.16.refs_2_ = bf16[336,128]{1,0:T(8,128)(2,1)S(1)} collective-permute-done((bf16[336,128]{1,0:T(8,128)(2,1)S(1)}, bf16[336,128]{1,0:T(8,128)(2,1)S(1)}, u32[]{:S(2)}, u32[]{:S(2)}) %collective-permute-start.16) | collective-permute-done | bytes 86048 | tf_op jit(solution)/shard_map/ppermute | solution.py:29
  41.3 0.2 collective-permute-done.17.refs_3_
  41.5 0.8 %final.1 = f32[144,288]{1,0:T(8,128)} custom-call(f32[336,128]{1,0:T(8,128)S(1)} %get-tuple-element.40.refs_0_, bf16[336,128]{1,0:T(8,128)(2,1)S(1)} %collective-permute-done.15.refs_1_, bf16[336,128]{1,0:T(8,128)(2,1)S(1)} %collective-permute-done.16.refs_2_, bf16[336,128]{1,0:T(8,128)(2,1)S(1)} %collective-permute-done.17.refs_3_), custom_call_target="tpu_custom_call" | custom-call | flops 1 | bytes 1 | tf_op jit(solution)/shard_map/final/pallas_call | solution.py:246
  (7 shorter events, 0.0 us)
Async XLA Ops:
  0.6 9.3 %collective-permute-start.5 = (bf16[128,1152]{1,0:T(8,128)(2,1)}, bf16[128,1152]{1,0:T(8,128)(2,1)S(1)}, u32[]{:S(2)}, u32[]{:S(2)}) collective-permute-start(bf16[128,1152]{1,0:T(8,128)(2,1)} %bitcast.15), channel_id=1, source_target_pairs={{0,4},{4,0},{8,12},{12,8},{16,20},{20,16},{24,28},{28,24},{1,5},{5... | collective-permute-start | bytes 884744 | tf_op jit(solution)/shard_map/ppermute | solution.py:29
  1.1 11.2 %collective-permute-start = (bf16[128,1152]{1,0:T(8,128)(2,1)}, bf16[128,1152]{1,0:T(8,128)(2,1)S(1)}, u32[]{:S(2)}, u32[]{:S(2)}) collective-permute-start(bf16[128,1152]{1,0:T(8,128)(2,1)} %bitcast.16), channel_id=1, source_target_pairs={{0,24},{4,28},{8,0},{12,4},{16,8},{20,12},{24,16},{28,20},{1,25},{... | collective-permute-start | bytes 884744 | tf_op jit(solution)/shard_map/ppermute | solution.py:24
  4.7 2.0 %collective-permute-start.2 = (s32[1,128]{1,0:T(1,128)}, s32[1,128]{1,0:T(1,128)S(1)}, u32[]{:S(2)}, u32[]{:S(2)}) collective-permute-start(s32[1,128]{1,0:T(1,128)} %param.11), channel_id=1, source_target_pairs={{0,4},{4,0},{8,12},{12,8},{16,20},{20,16},{24,28},{28,24},{1,5},{5... | collective-permute-start | bytes 1544 | tf_op jit(solution)/shard_map/ppermute | solution.py:29
  4.8 3.1 %collective-permute-start.4 = (bf16[128,1152]{1,0:T(8,128)(2,1)}, bf16[128,1152]{1,0:T(8,128)(2,1)S(1)}, u32[]{:S(2)}, u32[]{:S(2)}) collective-permute-start(bf16[128,1152]{1,0:T(8,128)(2,1)} %bitcast.9), channel_id=1, source_target_pairs={{0,4},{4,0},{8,12},{12,8},{16,20},{20,16},{24,28},{28,24},{1,5},{5... | collective-permute-start | bytes 884744 | tf_op jit(solution)/shard_map/ppermute | solution.py:29
  7.3 11.3 %collective-permute-start.3 = (s32[2,128]{1,0:T(2,128)S(1)}, s32[2,128]{1,0:T(2,128)S(1)}, u32[]{:S(2)}, u32[]{:S(2)}) collective-permute-start(s32[2,128]{1,0:T(2,128)S(1)} %pad_add_fusion.ids), channel_id=1, source_target_pairs={{0,24},{4,28},{8,0},{12,4},{16,8},{20,12},{24,16},{28,20},{1,25},{... | collective-permute-start | bytes 3080 | tf_op jit(solution)/shard_map/ppermute | solution.py:24
  7.9 16.9 %collective-permute-start.9 = (bf16[128,1152]{1,0:T(8,128)(2,1)}, bf16[128,1152]{1,0:T(8,128)(2,1)S(1)}, u32[]{:S(2)}, u32[]{:S(2)}) collective-permute-start(bf16[128,1152]{1,0:T(8,128)(2,1)} %bitcast.10), channel_id=1, source_target_pairs={{0,8},{4,12},{8,0},{12,4},{16,24},{20,28},{24,16},{28,20},{1,9},{5... | collective-permute-start | bytes 884744 | tf_op jit(solution)/shard_map/ppermute | solution.py:29
  9.4 17.1 %collective-permute-start.10 = (bf16[128,1152]{1,0:T(8,128)(2,1)}, bf16[128,1152]{1,0:T(8,128)(2,1)S(1)}, u32[]{:S(2)}, u32[]{:S(2)}) collective-permute-start(bf16[128,1152]{1,0:T(8,128)(2,1)} %bitcast.11), channel_id=1, source_target_pairs={{0,16},{4,20},{8,24},{12,28},{16,0},{20,4},{24,8},{28,12},{1,17},{... | collective-permute-start | bytes 884744 | tf_op jit(solution)/shard_map/ppermute | solution.py:29
  9.9 17.1 %collective-permute-start.11 = (bf16[128,1152]{1,0:T(8,128)(2,1)}, bf16[128,1152]{1,0:T(8,128)(2,1)S(1)}, u32[]{:S(2)}, u32[]{:S(2)}) collective-permute-start(bf16[128,1152]{1,0:T(8,128)(2,1)} %bitcast.12), channel_id=1, source_target_pairs={{0,24},{4,28},{8,16},{12,20},{16,8},{20,12},{24,0},{28,4},{1,25},{... | collective-permute-start | bytes 884744 | tf_op jit(solution)/shard_map/ppermute | solution.py:29
  12.4 6.3 %collective-permute-start.1 = (bf16[128,1152]{1,0:T(8,128)(2,1)S(1)}, bf16[128,1152]{1,0:T(8,128)(2,1)S(1)}, u32[]{:S(2)}, u32[]{:S(2)}) collective-permute-start(bf16[128,1152]{1,0:T(8,128)(2,1)S(1)} %collective-permute-done.far), channel_id=1, source_target_pairs={{0,4},{4,0},{8,12},{12,8},{16,20},{20,16},{24,28},{28,24},{1,5},{5... | collective-permute-start | bytes 884744 | tf_op jit(solution)/shard_map/ppermute | solution.py:29
  12.4 1.8 %copy-start = (bf16[1152,1152]{1,0:T(8,128)(2,1)S(1)}, bf16[1152,1152]{1,0:T(8,128)(2,1)}, u32[]{:S(2)}) copy-start(bf16[1152,1152]{1,0:T(8,128)(2,1)} %head_w.1) | copy-start | bytes 7962628
  14.1 1.0 %copy-start.2 = (bf16[1,128,1152]{2,1,0:T(8,128)(2,1)S(1)}, bf16[1,128,1152]{2,1,0:T(8,128)(2,1)}, u32[]{:S(2)}) copy-start(bf16[1,128,1152]{2,1,0:T(8,128)(2,1)} %param.7) | copy-start | bytes 884740
  15.1 1.0 %copy-start.4 = (bf16[1,128,1152]{2,1,0:T(8,128)(2,1)S(1)}, bf16[1,128,1152]{2,1,0:T(8,128)(2,1)}, u32[]{:S(2)}) copy-start(bf16[1,128,1152]{2,1,0:T(8,128)(2,1)} %param.6) | copy-start | bytes 884740
  18.6 8.5 %copy-start.1 = (bf16[1152,1152]{1,0:T(8,128)(2,1)S(1)}, bf16[1152,1152]{1,0:T(8,128)(2,1)}, u32[]{:S(2)}) copy-start(bf16[1152,1152]{1,0:T(8,128)(2,1)} %head_w.1) | copy-start | bytes 7962628
  18.6 11.4 %copy-start.3 = (bf16[1,128,1152]{2,1,0:T(8,128)(2,1)S(1)}, bf16[1,128,1152]{2,1,0:T(8,128)(2,1)}, u32[]{:S(2)}) copy-start(bf16[1,128,1152]{2,1,0:T(8,128)(2,1)} %param.7) | copy-start | bytes 884740
  20.9 5.6 %collective-permute-start.6 = (bf16[144,256]{1,0:T(8,128)(2,1)S(1)}, bf16[144,256]{1,0:T(8,128)(2,1)S(1)}, u32[]{:S(2)}, u32[]{:S(2)}) collective-permute-start(bf16[144,256]{1,0:T(8,128)(2,1)S(1)} %get-tuple-element.28), channel_id=1, source_target_pairs={{0,8},{4,12},{8,0},{12,4},{16,24},{20,28},{24,16},{28,20},{1,9},{5... | collective-permute-start | bytes 221192 | tf_op jit(solution)/shard_map/ppermute | solution.py:29
  23.2 5.5 %collective-permute-start.7 = (bf16[144,256]{1,0:T(8,128)(2,1)S(1)}, bf16[144,256]{1,0:T(8,128)(2,1)S(1)}, u32[]{:S(2)}, u32[]{:S(2)}) collective-permute-start(bf16[144,256]{1,0:T(8,128)(2,1)S(1)} %get-tuple-element.29), channel_id=1, source_target_pairs={{0,16},{4,20},{8,24},{12,28},{16,0},{20,4},{24,8},{28,12},{1,17},{... | collective-permute-start | bytes 221192 | tf_op jit(solution)/shard_map/ppermute | solution.py:29
  24.8 5.3 %collective-permute-start.8 = (bf16[144,256]{1,0:T(8,128)(2,1)S(1)}, bf16[144,256]{1,0:T(8,128)(2,1)S(1)}, u32[]{:S(2)}, u32[]{:S(2)}) collective-permute-start(bf16[144,256]{1,0:T(8,128)(2,1)S(1)} %get-tuple-element.30), channel_id=1, source_target_pairs={{0,24},{4,28},{8,16},{12,20},{16,8},{20,12},{24,0},{28,4},{1,25},{... | collective-permute-start | bytes 221192 | tf_op jit(solution)/shard_map/ppermute | solution.py:29
  26.5 3.5 %collective-permute-start.12 = (bf16[128,1152]{1,0:T(8,128)(2,1)S(1)}, bf16[128,1152]{1,0:T(8,128)(2,1)S(1)}, u32[]{:S(2)}, u32[]{:S(2)}) collective-permute-start(bf16[128,1152]{1,0:T(8,128)(2,1)S(1)} %collective-permute-done.9.refs_5_), channel_id=1, source_target_pairs={{0,4},{4,0},{8,12},{12,8},{16,20},{20,16},{24,28},{28,24},{1,5},{5... | collective-permute-start | bytes 884744 | tf_op jit(solution)/shard_map/ppermute | solution.py:29
  26.5 3.5 %collective-permute-start.13 = (bf16[128,1152]{1,0:T(8,128)(2,1)S(1)}, bf16[128,1152]{1,0:T(8,128)(2,1)S(1)}, u32[]{:S(2)}, u32[]{:S(2)}) collective-permute-start(bf16[128,1152]{1,0:T(8,128)(2,1)S(1)} %collective-permute-done.10.refs_6_), channel_id=1, source_target_pairs={{0,4},{4,0},{8,12},{12,8},{16,20},{20,16},{24,28},{28,24},{1,5},{5... | collective-permute-start | bytes 884744 | tf_op jit(solution)/shard_map/ppermute | solution.py:29
  27.0 3.0 %collective-permute-start.14 = (bf16[128,1152]{1,0:T(8,128)(2,1)S(1)}, bf16[128,1152]{1,0:T(8,128)(2,1)S(1)}, u32[]{:S(2)}, u32[]{:S(2)}) collective-permute-start(bf16[128,1152]{1,0:T(8,128)(2,1)S(1)} %collective-permute-done.11.refs_7_), channel_id=1, source_target_pairs={{0,4},{4,0},{8,12},{12,8},{16,20},{20,16},{24,28},{28,24},{1,5},{5... | collective-permute-start | bytes 884744 | tf_op jit(solution)/shard_map/ppermute | solution.py:29
  31.9 7.9 %collective-permute-start.15 = (bf16[336,128]{1,0:T(8,128)(2,1)S(1)}, bf16[336,128]{1,0:T(8,128)(2,1)S(1)}, u32[]{:S(2)}, u32[]{:S(2)}) collective-permute-start(bf16[336,128]{1,0:T(8,128)(2,1)S(1)} %get-tuple-element.41), channel_id=1, source_target_pairs={{0,2},{1,3},{2,0},{3,1},{4,6},{5,7},{6,4},{7,5},{8,10},{9,11},{10,... | collective-permute-start | bytes 258056 | tf_op jit(solution)/shard_map/ppermute | solution.py:29
  34.6 6.8 %collective-permute-start.16 = (bf16[336,128]{1,0:T(8,128)(2,1)S(1)}, bf16[336,128]{1,0:T(8,128)(2,1)S(1)}, u32[]{:S(2)}, u32[]{:S(2)}) collective-permute-start(bf16[336,128]{1,0:T(8,128)(2,1)S(1)} %get-tuple-element.42), channel_id=1, source_target_pairs={{0,3},{1,2},{2,1},{3,0},{4,7},{5,6},{6,5},{7,4},{8,11},{9,10},{10,... | collective-permute-start | bytes 258056 | tf_op jit(solution)/shard_map/ppermute | solution.py:29
  35.9 5.6 %collective-permute-start.17 = (bf16[336,128]{1,0:T(8,128)(2,1)S(1)}, bf16[336,128]{1,0:T(8,128)(2,1)S(1)}, u32[]{:S(2)}, u32[]{:S(2)}) collective-permute-start(bf16[336,128]{1,0:T(8,128)(2,1)S(1)} %get-tuple-element.43), channel_id=1, source_target_pairs={{0,1},{1,0},{2,3},{3,2},{4,5},{5,4},{6,7},{7,6},{8,9},{9,8},{10,11... | collective-permute-start | bytes 258056 | tf_op jit(solution)/shard_map/ppermute | solution.py:29

commit v3 on v2

--- a/solution.py
+++ b/solution.py
@@ -12,6 +12,7 @@
 LANES = 128
 VMEM = pl.BlockSpec(memory_space=pltpu.VMEM)
 SMEM = pl.BlockSpec(memory_space=pltpu.SMEM)
+ANY = pl.BlockSpec(memory_space=pl.ANY)
 NT = (((1,), (1,)), ((), ()))
 
 
@@ -33,72 +34,68 @@
     return lax.optimization_barrier((x, first))[0]
 
 
-def in_order(core, own, other):
-    first = jnp.where(core == 0, own, other)
-    second = jnp.where(core == 0, other, own)
-    return jnp.concatenate([first, second], axis=0)
-
-
-def pair_term(factor, scale, shift_b, txt_bf, row_ids, images, image_ids, skip):
+def unit_rows(images):
     wide = images.astype(jnp.float32)
     total = jnp.sum(wide * wide, axis=1, keepdims=True) + 1e-06
-    unit_img = (wide * (1.0 / jnp.sqrt(total))).astype(jnp.bfloat16)
+    return (wide * (1.0 / jnp.sqrt(total))).astype(jnp.bfloat16)
+
+
+def pair_term(factor, log_scale, shift_b, txt_bf, row_ids, unit_img, image_ids, skip):
+    scale = jnp.exp(jnp.full((1, txt_bf.shape[0]), log_scale, jnp.float32))
     sims = lax.dot_general(txt_bf, unit_img, NT, preferred_element_type=jnp.float32)
     rows = sims.shape[0] // 2
     match = (row_ids == image_ids).astype(jnp.float32)
     grads = factor * (jax.nn.sigmoid(scale * sims + shift_b) - match)
     row = lax.broadcasted_iota(jnp.int32, sims.shape, 0) >= rows
     col = lax.broadcasted_iota(jnp.int32, sims.shape, 1) >= rows
-    away = (row == bool(skip[0])) & (col == bool(skip[1]))
+    away = (row.astype(jnp.int32) == skip) & (col.astype(jnp.int32) == 1 - skip)
     grads = jnp.where(away, 0.0, grads).astype(jnp.bfloat16)
     return jnp.dot(grads, unit_img, preferred_element_type=jnp.float32)
 
 
 def own_kernel(
-    factor, scalars, place, feats, feats2, head_w, img, img2, ids,
+    factor, log_scale, bias, ids, ids2, raw, raw2, img, img2,
     unit_out, inverse_out, ids_out, term_out,
 ):
-    core = place[0]
-    both = in_order(core, feats[...], feats2[...])
-    text = jnp.dot(both, head_w[...], preferred_element_type=jnp.float32)
+    core = lax.axis_index("dp") % 2
+    text = jnp.concatenate([raw[...], raw2[...]], axis=0)
+    rows = text.shape[0]
+    chip_ids = jnp.concatenate([ids[...], ids2[...]], axis=1)
+    row_ids = jnp.broadcast_to(chip_ids, (LANES, rows)).T
+    ids_out[...] = row_ids
+    row_ids = jnp.concatenate([row_ids, row_ids], axis=1)
+    unit_img = unit_rows(jnp.concatenate([img[...], img2[...]], axis=0))
     inverse = 1.0 / jnp.sqrt(jnp.sum(text * text, axis=1, keepdims=True) + 1e-06)
     unit_txt = text * inverse
     unit_out[...] = unit_txt
-    rows = text.shape[0]
     inverse_out[...] = jnp.broadcast_to(inverse, (rows, LANES))
-    chip_ids = jnp.concatenate([ids[:1, :], ids[1:2, :]], axis=1)
-    row_ids = jnp.broadcast_to(chip_ids, (LANES, rows)).T
-    ids_out[...] = row_ids
-    row_ids = jnp.concatenate([row_ids, row_ids], axis=1)
     txt_bf = unit_txt.astype(jnp.bfloat16)
-    images = in_order(core, img[...], img2[...])
     term_out[...] = pair_term(
-        factor, scalars[0], scalars[1], txt_bf, row_ids, images, chip_ids, (1, 0)
+        factor, log_scale[0], bias[0], txt_bf, row_ids, unit_img, chip_ids, 1 - core
     )
 
 
 def loss_kernel(
-    factor, cols, scalars, place, far, far2, ids, unit, inverse, ids_in, term,
+    factor, cols, log_scale, bias, far, far2, ids, ids2, unit, inverse, ids_in, term,
     dz_out, *rest,
 ):
-    core, chip = place[0], place[1]
-    *parts, straight, flipped = rest
+    me = lax.axis_index("dp")
+    core, chip = me % 2, me // 2
+    *parts, flipped = rest
     unit_txt = unit[...]
     txt_bf = unit_txt.astype(jnp.bfloat16)
-    chip_ids = jnp.concatenate([ids[:1, :], ids[1:2, :]], axis=1)
+    chip_ids = jnp.concatenate([ids[...], ids2[...]], axis=1)
     row_ids = jnp.concatenate([ids_in[...], ids_in[...]], axis=1)
-    images = in_order(core, far[...], far2[...])
-    scale = scalars[0]
+    unit_img = unit_rows(jnp.concatenate([far[...], far2[...]], axis=0))
     dvec = term[...] + pair_term(
-        factor, scale, scalars[1], txt_bf, row_ids, images, chip_ids, (0, 1)
-    )
+        factor, log_scale[0], bias[0], txt_bf, row_ids, unit_img, chip_ids, core
+    )
+    scale = jnp.exp(jnp.full((1, dvec.shape[1]), log_scale[0], jnp.float32))
     dvec = scale * dvec
     along = jnp.sum(unit_txt * dvec, axis=1, keepdims=True)
     dzed = ((dvec - unit_txt * along) * inverse[:, :1]).astype(jnp.bfloat16)
-    straight[...] = dzed
+    dz_out[...] = dzed[: dz_out.shape[0]]
     flipped[...] = dzed.T
-    rows = dz_out.shape[0]
-    dz_out[...] = straight[pl.ds(pl.multiple_of(core * rows, 16), rows), :]
     for k, part in enumerate(parts):
         start = pl.multiple_of((2 * (chip ^ k) + core) * cols, 16)
         part[...] = flipped[pl.ds(start, cols), :]
@@ -112,28 +109,39 @@
     return full, rest, slots, cols * full + (cols // slots if slots else 0)
 
 
-def product_kernel(chips, cols, depth, replica, place, *refs):
-    grads, feats = refs[:chips], refs[chips : 3 * chips]
-    outs = refs[3 * chips : 3 * chips + replica]
-    feats_all, packed, sem = refs[3 * chips + replica :]
-    core = place[0]
-    rows = feats[0].shape[0]
-    copies = []
-    for i, (mine, theirs) in enumerate(zip(feats[:chips], feats[chips:])):
-        for j, (block, slot) in enumerate(((mine, core), (theirs, 1 - core))):
-            start = pl.multiple_of((2 * i + slot) * rows, rows)
-            copies.append(
-                pltpu.make_async_copy(
-                    block, feats_all.at[pl.ds(start, rows), :], sem.at[2 * i + j]
-                )
-            )
+def gathered(blocks, held, sem):
+    rows = blocks[0].shape[0]
+    copies = [
+        pltpu.make_async_copy(block, held.at[pl.ds(i * rows, rows), :], sem.at[i])
+        for i, block in enumerate(blocks)
+    ]
     for copy in copies:
         copy.start()
-    left = jnp.concatenate([g[...] for g in grads], axis=1)
+    return copies
+
+
+def near_kernel(chips, *refs):
+    grads, feats, (out, held, sem) = refs[:chips], refs[chips : 2 * chips + 1], refs[2 * chips + 1 :]
+    copies = gathered(feats, held, sem)
+    rows = feats[0].shape[0]
+    left = [g[:, :rows] for g in grads] + [grads[0][:, rows:]]
+    left = jnp.concatenate(left, axis=1)
     for copy in copies:
         copy.wait()
+    out[...] = jnp.dot(left, held[...], preferred_element_type=jnp.float32)
+
+
+def product_kernel(chips, cols, depth, replica, near, *refs):
+    grads, feats = refs[: chips - 1], refs[chips - 1 : 2 * chips - 2]
+    outs = refs[2 * chips - 2 : 2 * chips - 2 + replica]
+    held, packed, sem = refs[2 * chips - 2 + replica :]
+    copies = gathered(feats, held, sem)
+    rows = feats[0].shape[0]
+    left = jnp.concatenate([g[:, rows:] for g in grads], axis=1)
+    for copy in copies:
+        copy.wait()
+    local = near[...] + jnp.dot(left, held[...], preferred_element_type=jnp.float32)
     full, rest, slots, _ = packing(cols, depth)
-    local = jnp.dot(left, feats_all[...], preferred_element_type=jnp.float32)
     for r in range(replica):
         block = local[:, r * depth : (r + 1) * depth]
         for i in range(full):
@@ -144,7 +152,7 @@
             pieces.append(jnp.zeros((tall, LANES - slots * rest), jnp.float32))
             packed[r, full * cols :, :] = jnp.concatenate(pieces, axis=1)
     for k, out in enumerate(outs):
-        out[...] = packed[place[2] ^ k].astype(out.dtype)
+        out[...] = packed[lax.axis_index("replica") ^ k].astype(out.dtype)
 
 
 def final_kernel(cols, depth, *refs):
@@ -171,9 +179,6 @@
     chips = dp // 2
     cols, depth = width // dp, head_w.shape[0] // replica
     factor = LOSS_SCALE / (HOPS * rows)
-    scalars = jnp.concatenate([jnp.exp(log_scale), bias])
-    me, group = lax.axis_index("dp"), lax.axis_index("replica")
-    place = jnp.stack([me & 1, me >> 1, group])
 
     def f32(*shape):
         return jax.ShapeDtypeStruct(shape, jnp.float32)
@@ -182,11 +187,16 @@
         return jax.ShapeDtypeStruct(shape, jnp.bfloat16)
 
     far = rotated(images, "dp", -2)
+    far_ids = rotated(pair_ids, "dp", -2)
     feats2 = swapped(feats, "dp", 1)
     images2 = swapped(images, "dp", 1)
-    chip_ids = in_order(me & 1, pair_ids, swapped(pair_ids, "dp", 1))
-    far_ids = rotated(jnp.tile(chip_ids, (1, 1)), "dp", -2)
-
+    pair_ids2 = swapped(pair_ids, "dp", 1)
+
+    feats_in, feats2, images2, pair_ids2 = lax.optimization_barrier(
+        (feats, feats2, images2, pair_ids2)
+    )
+    raw = jnp.dot(feats, head_w, preferred_element_type=jnp.float32)
+    raw2 = jnp.dot(feats2, head_w, preferred_element_type=jnp.float32)
     unit_txt, inverse, row_ids, own_term = pl.pallas_call(
         functools.partial(own_kernel, factor),
         out_shape=[
@@ -200,47 +210,57 @@
         compiler_params=grant(24),
         cost_estimate=pl.CostEstimate(flops=10000000000, bytes_accessed=1, transcendentals=0),
         name="own",
-    )(scalars, place, feats, feats2, head_w, images, images2, chip_ids)
-
-    feats_soon = after(feats, feats2)
+    )(log_scale, bias, pair_ids, pair_ids2, raw, raw2, images, images2)
+
+    feats_soon = feats
     held = [swapped(feats_soon, "dp", 2 * k) for k in range(1, chips)]
-    far2 = swapped(far, "dp", 1)
+    far2 = swapped(after(far, (raw, raw2)), "dp", 1)
+    far_ids2 = swapped(after(far_ids, far), "dp", 1)
 
     dzed, *parts = pl.pallas_call(
         functools.partial(loss_kernel, factor, cols),
         out_shape=[bf16(rows, width)] + [bf16(cols, 2 * rows)] * chips,
-        in_specs=[SMEM] * 2 + [VMEM] * 7,
+        in_specs=[SMEM] * 2 + [VMEM] * 8,
         out_specs=[VMEM] * (1 + chips),
-        scratch_shapes=[
-            pltpu.VMEM((2 * rows, width), jnp.bfloat16),
-            pltpu.VMEM((width, 2 * rows), jnp.bfloat16),
-        ],
+        scratch_shapes=[pltpu.VMEM((width, 2 * rows), jnp.bfloat16)],
         compiler_params=grant(24),
         cost_estimate=pl.CostEstimate(flops=1, bytes_accessed=1, transcendentals=0),
         name="loss",
-    )(scalars, place, far, far2, far_ids, unit_txt, inverse, row_ids, own_term)
+    )(log_scale, bias, far, far2, far_ids, far_ids2, unit_txt, inverse, row_ids, own_term)
     got = [swapped(parts[k], "dp", 2 * k) for k in range(1, chips)]
-    held2 = [swapped(after(f, got[0]), "dp", 1) for f in held]
     grad_feat = lax.dot_general(dzed, head_w, NT, preferred_element_type=jnp.float32).astype(
         jnp.bfloat16
     )
-    grad_feat, got = lax.optimization_barrier((grad_feat, got))
-
+    held2 = [swapped(after(f, grad_feat), "dp", 1) for f in held]
+
+    near = pl.pallas_call(
+        functools.partial(near_kernel, chips),
+        out_shape=f32(cols, head_w.shape[0]),
+        in_specs=[VMEM] * chips + [ANY] * (chips + 1),
+        out_specs=VMEM,
+        scratch_shapes=[
+            pltpu.VMEM(((chips + 1) * rows, head_w.shape[0]), jnp.bfloat16),
+            pltpu.SemaphoreType.DMA((chips + 1,)),
+        ],
+        compiler_params=grant(24),
+        cost_estimate=pl.CostEstimate(flops=10000000000, bytes_accessed=1, transcendentals=0),
+        name="near",
+    )(parts[0], *got, feats, *held, feats2)
     tall = packing(cols, depth)[3]
     own, *pieces = pl.pallas_call(
         functools.partial(product_kernel, chips, cols, depth, replica),
         out_shape=[f32(tall, LANES)] + [bf16(tall, LANES)] * (replica - 1),
-        in_specs=[SMEM] + [VMEM] * chips + [pl.BlockSpec(memory_space=pl.ANY)] * dp,
+        in_specs=[VMEM] * chips + [ANY] * (chips - 1),
         out_specs=[VMEM] * replica,
         scratch_shapes=[
-            pltpu.VMEM((dp * rows, head_w.shape[0]), jnp.bfloat16),
+            pltpu.VMEM(((chips - 1) * rows, head_w.shape[0]), jnp.bfloat16),
             pltpu.VMEM((replica, tall, LANES), jnp.float32),
-            pltpu.SemaphoreType.DMA((dp,)),
+            pltpu.SemaphoreType.DMA((chips - 1,)),
         ],
         compiler_params=grant(24),
         cost_estimate=pl.CostEstimate(flops=1, bytes_accessed=1, transcendentals=0),
         name="product",
-    )(place, parts[0], *got, feats, *held, feats2, *held2)
+    )(near, *got, *held2)
     order = sorted(range(1, replica), key=lambda k: (-(k & (replica // 2)), k))
     sums = [swapped(pieces[k - 1], "replica", k) for k in order]
     head_grad = pl.pallas_call(

time: 42.8 us -> 41.1 us (0.960)
  local copies, waits for them, and re-layouts: 3.68 us -> 0.03 us
  Pallas kernels: 7.4 us -> 4.91 us
  waiting for transfers between devices: 9.34 us -> 11.7 us
  matrix products: 1.63 us -> 3.78 us
  starting transfers between devices: 17.3 us -> 18.4 us
  other arithmetic: 0.82 us -> 0 us
    unnamed x10 -> x8, local copies, waits for them, and re-layouts: 3.68 us -> 0.03 us
    ppermute x16 -> x17, waiting for transfers between devices: 8.4 us -> 11.7 us  [swapped(): return lax.ppermute(x, axis, [(i, i ^ mask) for i in range(size)])]
    dot_general x0 -> x2, matrix products: none -> 2.14 us  [the longest x1 1.55 us: box_shards(): raw = jnp.dot(feats, head_w, preferred_element_type=jnp.float32)]
    pallas_call x1, Pallas kernels: 2.57 us -> 1.12 us  [box_shards(): pl.pallas_call(functools.partial(own_kernel, factor), out_shape=[f32(2 *...]
    ppermute x16 -> x17, starting transfers between devices: 13.2 us -> 14.4 us  [swapped(): return lax.ppermute(x, axis, [(i, i ^ mask) for i in range(size)])]
    pallas_call x1, Pallas kernels: 1.86 us -> 0.77 us  [box_shards(): pl.pallas_call(functools.partial(product_kernel, chips, cols, depth, repl...]
    ppermute x2, waiting for transfers between devices: 0.95 us -> 0.01 us  [rotated(): return lax.ppermute(x, axis, [(i, (i + by) % size) for i in range(size)])]
    pallas_call x0 -> x1, Pallas kernels: none -> 0.81 us  [box_shards(): pl.pallas_call(functools.partial(near_kernel, chips), out_shape=f32(cols,...]
  transfers between devices with their start and end apart: 18 -> 19, of which waited for: 6 -> 6; matrix products, arithmetic and copies ran while one was open for 6% -> 9% of each run, Pallas kernels for 11% -> 8%
where the time goes in v3:
time: 41.1 us; the launch traced here: 41 us
  starting transfers between devices  18.4 us (45%)
  waiting for transfers between devices  11.7 us (28%)
  Pallas kernels  4.91 us (12%)
  matrix products  3.78 us (9%)
  between operations  2.14 us (5%)
    ppermute x17, starting transfers between devices, swapped(): return lax.ppermute(x, axis, [(i, i ^ mask) for i in range(size)])  14.4 us
    ppermute x17, waiting for transfers between devices, swapped(): return lax.ppermute(x, axis, [(i, i ^ mask) for i in range(size)])  11.7 us
    ppermute x2, starting transfers between devices, rotated(): return lax.ppermute(x, axis, [(i, (i + by) % size) for i in range(size)])  4.04 us
    dot_general x1, matrix products, box_shards(): lax.dot_general(dzed, head_w, NT, preferred_element_type=jnp.float32)  1.64 us
    dot_general x1, matrix products, box_shards(): raw = jnp.dot(feats, head_w, preferred_element_type=jnp.float32)  1.55 us
    pallas_call x1, Pallas kernels, box_shards(): pl.pallas_call(functools.partial(loss_kernel, factor, cols), out_shape=[b...  1.43 us
    pallas_call x1, Pallas kernels, box_shards(): pl.pallas_call(functools.partial(own_kernel, factor), out_shape=[f32(2 *...  1.12 us
  transfers between devices with their start and end apart: 19, of which 6 were waited for; matrix products, arithmetic and copies ran while one was open for 9% of the time, Pallas kernels for 8%

profile of v3, /device:TPU:0, one launch (start us, length us, event | category | flops | bytes accessed | tf_op | source)
XLA Modules:
  0.0 41.0 jit_solution(7705304708301792268)
XLA Ops:
  0.6 0.0 copy-start
  0.7 0.5 %collective-permute-start.2 = (bf16[128,1152]{1,0:T(8,128)(2,1)}, bf16[128,1152]{1,0:T(8,128)(2,1)S(1)}, u32[]{:S(2)}, u32[]{:S(2)}) collective-permute-start(bf16[128,1152]{1,0:T(8,128)(2,1)} %bitcast.16), channel_id=1, source_target_pairs={{0,4},{4,0},{8,12},{12,8},{16,20},{20,16},{24,28},{28,24},{1,5},{5... | collective-permute-start | bytes 884744 | tf_op jit(solution)/shard_map/ppermute | solution.py:30
  1.2 3.5 %collective-permute-start = (bf16[128,1152]{1,0:T(8,128)(2,1)}, bf16[128,1152]{1,0:T(8,128)(2,1)S(1)}, u32[]{:S(2)}, u32[]{:S(2)}) collective-permute-start(bf16[128,1152]{1,0:T(8,128)(2,1)} %bitcast.17), channel_id=1, source_target_pairs={{0,24},{4,28},{8,0},{12,4},{16,8},{20,12},{24,16},{28,20},{1,25},{... | collective-permute-start | bytes 884744 | tf_op jit(solution)/shard_map/ppermute | solution.py:25
  4.7 0.2 collective-permute-start.3
  4.8 0.5 %collective-permute-start.5 = (s32[1,128]{1,0:T(1,128)}, s32[1,128]{1,0:T(1,128)S(1)}, u32[]{:S(2)}, u32[]{:S(2)}) collective-permute-start(s32[1,128]{1,0:T(1,128)} %ids.1), channel_id=1, source_target_pairs={{0,24},{4,28},{8,0},{12,4},{16,8},{20,12},{24,16},{28,20},{1,25},{... | collective-permute-start | bytes 1544 | tf_op jit(solution)/shard_map/ppermute | solution.py:25
  5.4 0.1 collective-permute-start.1
  5.5 1.5 %fusion.raw = f32[128,1152]{1,0:T(8,128)S(1)} fusion(bf16[1152,1152]{1,0:T(8,128)(2,1)S(1)} %copy-done, bf16[1,128,1152]{2,1,0:T(8,128)(2,1)} %param.7), kind=kOutput, calls=%fused_computation.1 | convolution fusion | flops 339738624 | bytes 3538944 | tf_op jit(solution)/shard_map/dot_general | solution.py:198
  7.0 0.0 copy-start.2
  7.0 0.0 copy-start.3
  8.4 0.0 collective-permute-done.3.ids2
  8.4 1.6 %collective-permute-start.10 = (bf16[128,1152]{1,0:T(8,128)(2,1)S(1)}, bf16[128,1152]{1,0:T(8,128)(2,1)S(1)}, u32[]{:S(2)}, u32[]{:S(2)}) collective-permute-start(bf16[128,1152]{1,0:T(8,128)(2,1)S(1)} %bitcast.12), channel_id=1, source_target_pairs={{0,8},{4,12},{8,0},{12,4},{16,24},{20,28},{24,16},{28,20},{1,9},{5... | collective-permute-start | bytes 884744 | tf_op jit(solution)/shard_map/ppermute | solution.py:30
  9.9 0.0 collective-permute-done.1.refs_8_
  9.9 0.5 %collective-permute-start.11 = (bf16[128,1152]{1,0:T(8,128)(2,1)S(1)}, bf16[128,1152]{1,0:T(8,128)(2,1)S(1)}, u32[]{:S(2)}, u32[]{:S(2)}) collective-permute-start(bf16[128,1152]{1,0:T(8,128)(2,1)S(1)} %bitcast.13), channel_id=1, source_target_pairs={{0,16},{4,20},{8,24},{12,28},{16,0},{20,4},{24,8},{28,12},{1,17},{... | collective-permute-start | bytes 884744 | tf_op jit(solution)/shard_map/ppermute | solution.py:30
  10.5 0.0 collective-permute-done.2.img2
  10.5 1.5 %collective-permute-start.12 = (bf16[128,1152]{1,0:T(8,128)(2,1)S(1)}, bf16[128,1152]{1,0:T(8,128)(2,1)S(1)}, u32[]{:S(2)}, u32[]{:S(2)}) collective-permute-start(bf16[128,1152]{1,0:T(8,128)(2,1)S(1)} %bitcast.14), channel_id=1, source_target_pairs={{0,24},{4,28},{8,16},{12,20},{16,8},{20,12},{24,0},{28,4},{1,25},{... | collective-permute-start | bytes 884744 | tf_op jit(solution)/shard_map/ppermute | solution.py:30
  12.0 0.6 %fusion.2.raw2 = f32[128,1152]{1,0:T(8,128)S(1)} fusion(bf16[128,1152]{1,0:T(8,128)(2,1)S(1)} %collective-permute-done.1.refs_8_, bf16[1152,1152]{1,0:T(8,128)(2,1)S(1)} %copy-done), kind=kOutput, calls=%fused_computation.3 | convolution fusion | flops 339738624 | bytes 3538944 | tf_op jit(solution)/shard_map/dot_general | solution.py:199
  12.6 0.0 collective-permute-done.far
  12.6 0.1 collective-permute-start.4
  12.6 0.0 collective-permute-done.5.ids
  12.7 0.5 %collective-permute-start.6 = (s32[1,128]{1,0:T(1,128)S(1)}, s32[1,128]{1,0:T(1,128)S(1)}, u32[]{:S(2)}, u32[]{:S(2)}) collective-permute-start(s32[1,128]{1,0:T(1,128)S(1)} %collective-permute-done.5.ids), channel_id=1, source_target_pairs={{0,4},{4,0},{8,12},{12,8},{16,20},{20,16},{24,28},{28,24},{1,5},{5... | collective-permute-start | bytes 1544 | tf_op jit(solution)/shard_map/ppermute | solution.py:30
  13.1 1.1 %own.1 = (f32[256,1152]{1,0:T(8,128)S(1)}, f32[256,128]{1,0:T(8,128)S(1)}, s32[256,128]{1,0:T(8,128)S(1)}, f32[256,1152]{1,0:T(8,128)S(1)}) custom-call(f32[1]{0:T(128)S(6)} %copy.8.log_scale, f32[1]{0:T(128)S(6)} %copy.9.bias, s32[1,128]{1,0:T(1,128)S(1)} %copy-done.3, s32[1,128]{1,0:T(1,128)S(1)} %collective-permute-done.3.ids2, f32[128,1152]{1,0:T(8,128)S(1)} %fusion.raw, ...), custom_call_target="tpu_custom_call" | custom-call | flops 10000000000 | bytes 1 | tf_op jit(solution)/shard_map/own/pallas_call | solution.py:200
  14.3 0.0 collective-permute-done.6.ids2
  14.3 0.0 collective-permute-done.4.far2
  14.3 1.4 %loss.1 = (bf16[128,1152]{1,0:T(8,128)(2,1)S(1)}, bf16[144,256]{1,0:T(8,128)(2,1)S(1)}, bf16[144,256]{1,0:T(8,128)(2,1)S(1)}, bf16[144,256]{1,0:T(8,128)(2,1)S(1)}, bf16[144,256]{1,0:T(8,128)(2,1)S(1)}) custom-call(f32[1]{0:T(128)S(6)} %copy.8.log_scale, f32[1]{0:T(128)S(6)} %copy.9.bias, bf16[128,1152]{1,0:T(8,128)(2,1)S(1)} %collective-permute-done.far, ...), custom_call_target="tpu_custom_call" | custom-call | flops 1 | bytes 1 | tf_op jit(solution)/shard_map/loss/pallas_call | solution.py:220
  15.7 2.1 %collective-permute-start.7 = (bf16[144,256]{1,0:T(8,128)(2,1)S(1)}, bf16[144,256]{1,0:T(8,128)(2,1)S(1)}, u32[]{:S(2)}, u32[]{:S(2)}) collective-permute-start(bf16[144,256]{1,0:T(8,128)(2,1)S(1)} %get-tuple-element.34), channel_id=1, source_target_pairs={{0,8},{4,12},{8,0},{12,4},{16,24},{20,28},{24,16},{28,20},{1,9},{5... | collective-permute-start | bytes 221192 | tf_op jit(solution)/shard_map/ppermute | solution.py:30
  17.8 1.5 %collective-permute-start.8 = (bf16[144,256]{1,0:T(8,128)(2,1)S(1)}, bf16[144,256]{1,0:T(8,128)(2,1)S(1)}, u32[]{:S(2)}, u32[]{:S(2)}) collective-permute-start(bf16[144,256]{1,0:T(8,128)(2,1)S(1)} %get-tuple-element.35), channel_id=1, source_target_pairs={{0,16},{4,20},{8,24},{12,28},{16,0},{20,4},{24,8},{28,12},{1,17},{... | collective-permute-start | bytes 221192 | tf_op jit(solution)/shard_map/ppermute | solution.py:30
  19.4 0.0 collective-permute-done.10.refs_5_
  19.4 1.6 %collective-permute-start.9 = (bf16[144,256]{1,0:T(8,128)(2,1)S(1)}, bf16[144,256]{1,0:T(8,128)(2,1)S(1)}, u32[]{:S(2)}, u32[]{:S(2)}) collective-permute-start(bf16[144,256]{1,0:T(8,128)(2,1)S(1)} %get-tuple-element.36), channel_id=1, source_target_pairs={{0,24},{4,28},{8,16},{12,20},{16,8},{20,12},{24,0},{28,4},{1,25},{... | collective-permute-start | bytes 221192 | tf_op jit(solution)/shard_map/ppermute | solution.py:30
  21.0 1.6 %convolution_convert_fusion = bf16[128,1152]{1,0:T(8,128)(2,1)} fusion(bf16[128,1152]{1,0:T(8,128)(2,1)S(1)} %get-tuple-element.32, bf16[1152,1152]{1,0:T(8,128)(2,1)S(1)} %copy-done), kind=kOutput, calls=%fused_computation | convolution fusion | flops 339886080 | bytes 3244032 | tf_op jit(solution)/shard_map/dot_general | solution.py:231
  22.6 0.0 collective-permute-done.11.refs_6_
  22.6 0.0 collective-permute-start.13
  22.6 3.3 %collective-permute-done.12.refs_7_ = bf16[128,1152]{1,0:T(8,128)(2,1)S(1)} collective-permute-done((bf16[128,1152]{1,0:T(8,128)(2,1)S(1)}, bf16[128,1152]{1,0:T(8,128)(2,1)S(1)}, u32[]{:S(2)}, u32[]{:S(2)}) %collective-permute-start.12) | collective-permute-done | bytes 294944 | tf_op jit(solution)/shard_map/ppermute | solution.py:30
  25.9 0.0 collective-permute-start.14
  25.9 0.6 %collective-permute-done.7.refs_1_.refs_0_ = bf16[144,256]{1,0:T(8,128)(2,1)S(1)} collective-permute-done((bf16[144,256]{1,0:T(8,128)(2,1)S(1)}, bf16[144,256]{1,0:T(8,128)(2,1)S(1)}, u32[]{:S(2)}, u32[]{:S(2)}) %collective-permute-start.7) | collective-permute-done | bytes 73760 | tf_op jit(solution)/shard_map/ppermute | solution.py:30
  26.5 0.0 collective-permute-start.15
  26.5 0.9 %collective-permute-done.8.refs_2_.refs_1_ = bf16[144,256]{1,0:T(8,128)(2,1)S(1)} collective-permute-done((bf16[144,256]{1,0:T(8,128)(2,1)S(1)}, bf16[144,256]{1,0:T(8,128)(2,1)S(1)}, u32[]{:S(2)}, u32[]{:S(2)}) %collective-permute-start.8) | collective-permute-done | bytes 73760 | tf_op jit(solution)/shard_map/ppermute | solution.py:30
  27.4 1.2 %collective-permute-done.9.refs_3_.refs_2_ = bf16[144,256]{1,0:T(8,128)(2,1)S(1)} collective-permute-done((bf16[144,256]{1,0:T(8,128)(2,1)S(1)}, bf16[144,256]{1,0:T(8,128)(2,1)S(1)}, u32[]{:S(2)}, u32[]{:S(2)}) %collective-permute-start.9) | collective-permute-done | bytes 73760 | tf_op jit(solution)/shard_map/ppermute | solution.py:30
  28.6 0.8 %near.1 = f32[144,1152]{1,0:T(8,128)S(1)} custom-call(bf16[144,256]{1,0:T(8,128)(2,1)S(1)} %get-tuple-element.33.refs_0_, bf16[144,256]{1,0:T(8,128)(2,1)S(1)} %collective-permute-done.7.refs_1_.refs_0_, bf16[144,256]{1,0:T(8,128)(2,1)S(1)} %collective-permute-done.8.refs_2_.refs_1_, bf16[144,256]{1,0:T(8,128)(2,1)S(1)} %collective-permute-done.9.refs_3_.refs_2_, ...), custom_call_target="tpu_custom_call" | custom-call | flops 10000000000 | bytes 1 | tf_op jit(solution)/shard_map/near/pallas_call | solution.py:236
  29.4 0.0 collective-permute-done.13.refs_3_
  29.4 0.0 collective-permute-done.14.refs_4_
  29.5 0.0 collective-permute-done.15.refs_5_
  29.5 0.8 %product.1 = (f32[336,128]{1,0:T(8,128)S(1)}, bf16[336,128]{1,0:T(8,128)(2,1)S(1)}, bf16[336,128]{1,0:T(8,128)(2,1)S(1)}, bf16[336,128]{1,0:T(8,128)(2,1)S(1)}) custom-call(f32[144,1152]{1,0:T(8,128)S(1)} %near.1, bf16[144,256]{1,0:T(8,128)(2,1)S(1)} %collective-permute-done.7.refs_1_.refs_0_, bf16[144,256]{1,0:T(8,128)(2,1)S(1)} %collective-permute-done.8.refs_2_.refs_1_, ...), custom_call_target="tpu_custom_call" | custom-call | flops 1 | bytes 1 | tf_op jit(solution)/shard_map/product/pallas_call | solution.py:250
  30.2 2.7 %collective-permute-start.16 = (bf16[336,128]{1,0:T(8,128)(2,1)S(1)}, bf16[336,128]{1,0:T(8,128)(2,1)S(1)}, u32[]{:S(2)}, u32[]{:S(2)}) collective-permute-start(bf16[336,128]{1,0:T(8,128)(2,1)S(1)} %get-tuple-element.41), channel_id=1, source_target_pairs={{0,2},{1,3},{2,0},{3,1},{4,6},{5,7},{6,4},{7,5},{8,10},{9,11},{10,... | collective-permute-start | bytes 258056 | tf_op jit(solution)/shard_map/ppermute | solution.py:30
  32.9 1.3 %collective-permute-start.17 = (bf16[336,128]{1,0:T(8,128)(2,1)S(1)}, bf16[336,128]{1,0:T(8,128)(2,1)S(1)}, u32[]{:S(2)}, u32[]{:S(2)}) collective-permute-start(bf16[336,128]{1,0:T(8,128)(2,1)S(1)} %get-tuple-element.42), channel_id=1, source_target_pairs={{0,3},{1,2},{2,1},{3,0},{4,7},{5,6},{6,5},{7,4},{8,11},{9,10},{10,... | collective-permute-start | bytes 258056 | tf_op jit(solution)/shard_map/ppermute | solution.py:30
  34.3 0.3 collective-permute-start.18
  34.5 5.1 %collective-permute-done.16.refs_1_ = bf16[336,128]{1,0:T(8,128)(2,1)S(1)} collective-permute-done((bf16[336,128]{1,0:T(8,128)(2,1)S(1)}, bf16[336,128]{1,0:T(8,128)(2,1)S(1)}, u32[]{:S(2)}, u32[]{:S(2)}) %collective-permute-start.16) | collective-permute-done | bytes 86048 | tf_op jit(solution)/shard_map/ppermute | solution.py:30
  39.6 0.6 %collective-permute-done.18.refs_3_ = bf16[336,128]{1,0:T(8,128)(2,1)S(1)} collective-permute-done((bf16[336,128]{1,0:T(8,128)(2,1)S(1)}, bf16[336,128]{1,0:T(8,128)(2,1)S(1)}, u32[]{:S(2)}, u32[]{:S(2)}) %collective-permute-start.18) | collective-permute-done | bytes 86048 | tf_op jit(solution)/shard_map/ppermute | solution.py:30
  40.2 0.8 %final.1 = f32[144,288]{1,0:T(8,128)} custom-call(f32[336,128]{1,0:T(8,128)S(1)} %get-tuple-element.40.refs_0_, bf16[336,128]{1,0:T(8,128)(2,1)S(1)} %collective-permute-done.16.refs_1_, bf16[336,128]{1,0:T(8,128)(2,1)S(1)} %collective-permute-done.17.refs_2_, bf16[336,128]{1,0:T(8,128)(2,1)S(1)} %collective-permute-done.18.refs_3_), custom_call_target="tpu_custom_call" | custom-call | flops 1 | bytes 1 | tf_op jit(solution)/shard_map/final/pallas_call | solution.py:266
  (6 shorter events, 0.0 us)
Async XLA Ops:
  0.6 4.8 %copy-start = (bf16[1152,1152]{1,0:T(8,128)(2,1)S(1)}, bf16[1152,1152]{1,0:T(8,128)(2,1)}, u32[]{:S(2)}) copy-start(bf16[1152,1152]{1,0:T(8,128)(2,1)} %param.8) | copy-start | bytes 7962628
  0.6 7.7 %copy-start.1 = (bf16[1,128,1152]{2,1,0:T(8,128)(2,1)S(1)}, bf16[1,128,1152]{2,1,0:T(8,128)(2,1)}, u32[]{:S(2)}) copy-start(bf16[1,128,1152]{2,1,0:T(8,128)(2,1)} %param.7) | copy-start | bytes 884740
  0.7 9.8 %collective-permute-start.2 = (bf16[128,1152]{1,0:T(8,128)(2,1)}, bf16[128,1152]{1,0:T(8,128)(2,1)S(1)}, u32[]{:S(2)}, u32[]{:S(2)}) collective-permute-start(bf16[128,1152]{1,0:T(8,128)(2,1)} %bitcast.16), channel_id=1, source_target_pairs={{0,4},{4,0},{8,12},{12,8},{16,20},{20,16},{24,28},{28,24},{1,5},{5... | collective-permute-start | bytes 884744 | tf_op jit(solution)/shard_map/ppermute | solution.py:30
  1.2 11.4 %collective-permute-start = (bf16[128,1152]{1,0:T(8,128)(2,1)}, bf16[128,1152]{1,0:T(8,128)(2,1)S(1)}, u32[]{:S(2)}, u32[]{:S(2)}) collective-permute-start(bf16[128,1152]{1,0:T(8,128)(2,1)} %bitcast.17), channel_id=1, source_target_pairs={{0,24},{4,28},{8,0},{12,4},{16,8},{20,12},{24,16},{28,20},{1,25},{... | collective-permute-start | bytes 884744 | tf_op jit(solution)/shard_map/ppermute | solution.py:25
  4.7 3.7 %collective-permute-start.3 = (s32[1,128]{1,0:T(1,128)}, s32[1,128]{1,0:T(1,128)S(1)}, u32[]{:S(2)}, u32[]{:S(2)}) collective-permute-start(s32[1,128]{1,0:T(1,128)} %ids.1), channel_id=1, source_target_pairs={{0,4},{4,0},{8,12},{12,8},{16,20},{20,16},{24,28},{28,24},{1,5},{5... | collective-permute-start | bytes 1544 | tf_op jit(solution)/shard_map/ppermute | solution.py:30
  4.8 7.8 %collective-permute-start.5 = (s32[1,128]{1,0:T(1,128)}, s32[1,128]{1,0:T(1,128)S(1)}, u32[]{:S(2)}, u32[]{:S(2)}) collective-permute-start(s32[1,128]{1,0:T(1,128)} %ids.1), channel_id=1, source_target_pairs={{0,24},{4,28},{8,0},{12,4},{16,8},{20,12},{24,16},{28,20},{1,25},{... | collective-permute-start | bytes 1544 | tf_op jit(solution)/shard_map/ppermute | solution.py:25
  5.4 4.6 %collective-permute-start.1 = (bf16[128,1152]{1,0:T(8,128)(2,1)}, bf16[128,1152]{1,0:T(8,128)(2,1)S(1)}, u32[]{:S(2)}, u32[]{:S(2)}) collective-permute-start(bf16[128,1152]{1,0:T(8,128)(2,1)} %bitcast.11), channel_id=1, source_target_pairs={{0,4},{4,0},{8,12},{12,8},{16,20},{20,16},{24,28},{28,24},{1,5},{5... | collective-permute-start | bytes 884744 | tf_op jit(solution)/shard_map/ppermute | solution.py:30
  7.0 6.1 %copy-start.2 = (bf16[1,128,1152]{2,1,0:T(8,128)(2,1)S(1)}, bf16[1,128,1152]{2,1,0:T(8,128)(2,1)}, u32[]{:S(2)}) copy-start(bf16[1,128,1152]{2,1,0:T(8,128)(2,1)} %param.6) | copy-start | bytes 884740
  7.0 6.1 %copy-start.3 = (s32[1,128]{1,0:T(1,128)S(1)}, s32[1,128]{1,0:T(1,128)}, u32[]{:S(2)}) copy-start(s32[1,128]{1,0:T(1,128)} %ids.1) | copy-start | bytes 1540
  8.4 11.0 %collective-permute-start.10 = (bf16[128,1152]{1,0:T(8,128)(2,1)S(1)}, bf16[128,1152]{1,0:T(8,128)(2,1)S(1)}, u32[]{:S(2)}, u32[]{:S(2)}) collective-permute-start(bf16[128,1152]{1,0:T(8,128)(2,1)S(1)} %bitcast.12), channel_id=1, source_target_pairs={{0,8},{4,12},{8,0},{12,4},{16,24},{20,28},{24,16},{28,20},{1,9},{5... | collective-permute-start | bytes 884744 | tf_op jit(solution)/shard_map/ppermute | solution.py:30
  9.9 12.7 %collective-permute-start.11 = (bf16[128,1152]{1,0:T(8,128)(2,1)S(1)}, bf16[128,1152]{1,0:T(8,128)(2,1)S(1)}, u32[]{:S(2)}, u32[]{:S(2)}) collective-permute-start(bf16[128,1152]{1,0:T(8,128)(2,1)S(1)} %bitcast.13), channel_id=1, source_target_pairs={{0,16},{4,20},{8,24},{12,28},{16,0},{20,4},{24,8},{28,12},{1,17},{... | collective-permute-start | bytes 884744 | tf_op jit(solution)/shard_map/ppermute | solution.py:30
  10.5 15.5 %collective-permute-start.12 = (bf16[128,1152]{1,0:T(8,128)(2,1)S(1)}, bf16[128,1152]{1,0:T(8,128)(2,1)S(1)}, u32[]{:S(2)}, u32[]{:S(2)}) collective-permute-start(bf16[128,1152]{1,0:T(8,128)(2,1)S(1)} %bitcast.14), channel_id=1, source_target_pairs={{0,24},{4,28},{8,16},{12,20},{16,8},{20,12},{24,0},{28,4},{1,25},{... | collective-permute-start | bytes 884744 | tf_op jit(solution)/shard_map/ppermute | solution.py:30
  12.6 1.7 %collective-permute-start.4 = (bf16[128,1152]{1,0:T(8,128)(2,1)S(1)}, bf16[128,1152]{1,0:T(8,128)(2,1)S(1)}, u32[]{:S(2)}, u32[]{:S(2)}) collective-permute-start(bf16[128,1152]{1,0:T(8,128)(2,1)S(1)} %collective-permute-done.far), channel_id=1, source_target_pairs={{0,4},{4,0},{8,12},{12,8},{16,20},{20,16},{24,28},{28,24},{1,5},{5... | collective-permute-start | bytes 884744 | tf_op jit(solution)/shard_map/ppermute | solution.py:30
  12.7 1.6 %collective-permute-start.6 = (s32[1,128]{1,0:T(1,128)S(1)}, s32[1,128]{1,0:T(1,128)S(1)}, u32[]{:S(2)}, u32[]{:S(2)}) collective-permute-start(s32[1,128]{1,0:T(1,128)S(1)} %collective-permute-done.5.ids), channel_id=1, source_target_pairs={{0,4},{4,0},{8,12},{12,8},{16,20},{20,16},{24,28},{28,24},{1,5},{5... | collective-permute-start | bytes 1544 | tf_op jit(solution)/shard_map/ppermute | solution.py:30
  15.7 10.8 %collective-permute-start.7 = (bf16[144,256]{1,0:T(8,128)(2,1)S(1)}, bf16[144,256]{1,0:T(8,128)(2,1)S(1)}, u32[]{:S(2)}, u32[]{:S(2)}) collective-permute-start(bf16[144,256]{1,0:T(8,128)(2,1)S(1)} %get-tuple-element.34), channel_id=1, source_target_pairs={{0,8},{4,12},{8,0},{12,4},{16,24},{20,28},{24,16},{28,20},{1,9},{5... | collective-permute-start | bytes 221192 | tf_op jit(solution)/shard_map/ppermute | solution.py:30
  17.8 9.6 %collective-permute-start.8 = (bf16[144,256]{1,0:T(8,128)(2,1)S(1)}, bf16[144,256]{1,0:T(8,128)(2,1)S(1)}, u32[]{:S(2)}, u32[]{:S(2)}) collective-permute-start(bf16[144,256]{1,0:T(8,128)(2,1)S(1)} %get-tuple-element.35), channel_id=1, source_target_pairs={{0,16},{4,20},{8,24},{12,28},{16,0},{20,4},{24,8},{28,12},{1,17},{... | collective-permute-start | bytes 221192 | tf_op jit(solution)/shard_map/ppermute | solution.py:30
  19.4 9.2 %collective-permute-start.9 = (bf16[144,256]{1,0:T(8,128)(2,1)S(1)}, bf16[144,256]{1,0:T(8,128)(2,1)S(1)}, u32[]{:S(2)}, u32[]{:S(2)}) collective-permute-start(bf16[144,256]{1,0:T(8,128)(2,1)S(1)} %get-tuple-element.36), channel_id=1, source_target_pairs={{0,24},{4,28},{8,16},{12,20},{16,8},{20,12},{24,0},{28,4},{1,25},{... | collective-permute-start | bytes 221192 | tf_op jit(solution)/shard_map/ppermute | solution.py:30
  22.6 6.8 %collective-permute-start.13 = (bf16[128,1152]{1,0:T(8,128)(2,1)S(1)}, bf16[128,1152]{1,0:T(8,128)(2,1)S(1)}, u32[]{:S(2)}, u32[]{:S(2)}) collective-permute-start(bf16[128,1152]{1,0:T(8,128)(2,1)S(1)} %collective-permute-done.10.refs_5_), channel_id=1, source_target_pairs={{0,4},{4,0},{8,12},{12,8},{16,20},{20,16},{24,28},{28,24},{1,5},{5... | collective-permute-start | bytes 884744 | tf_op jit(solution)/shard_map/ppermute | solution.py:30
  25.9 3.5 %collective-permute-start.14 = (bf16[128,1152]{1,0:T(8,128)(2,1)S(1)}, bf16[128,1152]{1,0:T(8,128)(2,1)S(1)}, u32[]{:S(2)}, u32[]{:S(2)}) collective-permute-start(bf16[128,1152]{1,0:T(8,128)(2,1)S(1)} %collective-permute-done.11.refs_6_), channel_id=1, source_target_pairs={{0,4},{4,0},{8,12},{12,8},{16,20},{20,16},{24,28},{28,24},{1,5},{5... | collective-permute-start | bytes 884744 | tf_op jit(solution)/shard_map/ppermute | solution.py:30
  26.5 2.9 %collective-permute-start.15 = (bf16[128,1152]{1,0:T(8,128)(2,1)S(1)}, bf16[128,1152]{1,0:T(8,128)(2,1)S(1)}, u32[]{:S(2)}, u32[]{:S(2)}) collective-permute-start(bf16[128,1152]{1,0:T(8,128)(2,1)S(1)} %collective-permute-done.12.refs_7_), channel_id=1, source_target_pairs={{0,4},{4,0},{8,12},{12,8},{16,20},{20,16},{24,28},{28,24},{1,5},{5... | collective-permute-start | bytes 884744 | tf_op jit(solution)/shard_map/ppermute | solution.py:30
  30.2 9.4 %collective-permute-start.16 = (bf16[336,128]{1,0:T(8,128)(2,1)S(1)}, bf16[336,128]{1,0:T(8,128)(2,1)S(1)}, u32[]{:S(2)}, u32[]{:S(2)}) collective-permute-start(bf16[336,128]{1,0:T(8,128)(2,1)S(1)} %get-tuple-element.41), channel_id=1, source_target_pairs={{0,2},{1,3},{2,0},{3,1},{4,6},{5,7},{6,4},{7,5},{8,10},{9,11},{10,... | collective-permute-start | bytes 258056 | tf_op jit(solution)/shard_map/ppermute | solution.py:30
  32.9 6.7 %collective-permute-start.17 = (bf16[336,128]{1,0:T(8,128)(2,1)S(1)}, bf16[336,128]{1,0:T(8,128)(2,1)S(1)}, u32[]{:S(2)}, u32[]{:S(2)}) collective-permute-start(bf16[336,128]{1,0:T(8,128)(2,1)S(1)} %get-tuple-element.42), channel_id=1, source_target_pairs={{0,3},{1,2},{2,1},{3,0},{4,7},{5,6},{6,5},{7,4},{8,11},{9,10},{10,... | collective-permute-start | bytes 258056 | tf_op jit(solution)/shard_map/ppermute | solution.py:30
  34.3 5.9 %collective-permute-start.18 = (bf16[336,128]{1,0:T(8,128)(2,1)S(1)}, bf16[336,128]{1,0:T(8,128)(2,1)S(1)}, u32[]{:S(2)}, u32[]{:S(2)}) collective-permute-start(bf16[336,128]{1,0:T(8,128)(2,1)S(1)} %get-tuple-element.43), channel_id=1, source_target_pairs={{0,1},{1,0},{2,3},{3,2},{4,5},{5,4},{6,7},{7,6},{8,9},{9,8},{10,11... | collective-permute-start | bytes 258056 | tf_op jit(solution)/shard_map/ppermute | solution.py:30

commit v4 on v3

--- a/solution.py
+++ b/solution.py
@@ -96,9 +96,10 @@
     dzed = ((dvec - unit_txt * along) * inverse[:, :1]).astype(jnp.bfloat16)
     dz_out[...] = dzed[: dz_out.shape[0]]
     flipped[...] = dzed.T
-    for k, part in enumerate(parts):
-        start = pl.multiple_of((2 * (chip ^ k) + core) * cols, 16)
-        part[...] = flipped[pl.ds(start, cols), :]
+    for east, part in enumerate(parts):
+        for north in range(2):
+            start = pl.multiple_of((2 * (chip ^ east ^ (2 * north)) + core) * cols, 16)
+            part[north * cols : (north + 1) * cols, :] = flipped[pl.ds(start, cols), :]
 
 
 def packing(cols, depth):
@@ -120,39 +121,38 @@
     return copies
 
 
-def near_kernel(chips, *refs):
-    grads, feats, (out, held, sem) = refs[:chips], refs[chips : 2 * chips + 1], refs[2 * chips + 1 :]
+def near_kernel(own, east, *refs):
+    feats, (out, held, sem) = refs[:3], refs[3:]
     copies = gathered(feats, held, sem)
-    rows = feats[0].shape[0]
-    left = [g[:, :rows] for g in grads] + [grads[0][:, rows:]]
-    left = jnp.concatenate(left, axis=1)
+    left = jnp.concatenate([own[...], east[:, : feats[0].shape[0]]], axis=1)
     for copy in copies:
         copy.wait()
     out[...] = jnp.dot(left, held[...], preferred_element_type=jnp.float32)
 
 
-def product_kernel(chips, cols, depth, replica, near, *refs):
-    grads, feats = refs[: chips - 1], refs[chips - 1 : 2 * chips - 2]
-    outs = refs[2 * chips - 2 : 2 * chips - 2 + replica]
-    held, packed, sem = refs[2 * chips - 2 + replica :]
-    copies = gathered(feats, held, sem)
-    rows = feats[0].shape[0]
-    left = jnp.concatenate([g[:, rows:] for g in grads], axis=1)
-    for copy in copies:
-        copy.wait()
-    local = near[...] + jnp.dot(left, held[...], preferred_element_type=jnp.float32)
-    full, rest, slots, _ = packing(cols, depth)
-    for r in range(replica):
-        block = local[:, r * depth : (r + 1) * depth]
-        for i in range(full):
-            packed[r, i * cols : (i + 1) * cols, :] = block[:, i * LANES : (i + 1) * LANES]
-        if slots:
-            tall = cols // slots
-            pieces = [block[s * tall : (s + 1) * tall, full * LANES :] for s in range(slots)]
-            pieces.append(jnp.zeros((tall, LANES - slots * rest), jnp.float32))
-            packed[r, full * cols :, :] = jnp.concatenate(pieces, axis=1)
-    for k, out in enumerate(outs):
-        out[...] = packed[lax.axis_index("replica") ^ k].astype(out.dtype)
+def product_kernel(cols, depth, replica, near, east, feats, *refs):
+    keeps, sends, packed = refs[:replica], refs[replica : 2 * replica - 1], refs[-1]
+    local = near[...] + jnp.dot(
+        east[:, feats.shape[0] :], feats[...], preferred_element_type=jnp.float32
+    )
+    full, rest, slots, tall = packing(cols, depth)
+    for north in range(2):
+        for r in range(replica):
+            block = local[north * cols : (north + 1) * cols, r * depth : (r + 1) * depth]
+            for i in range(full):
+                packed[north, r, i * cols : (i + 1) * cols, :] = block[:, i * LANES : (i + 1) * LANES]
+            if slots:
+                high = cols // slots
+                pieces = [block[s * high : (s + 1) * high, full * LANES :] for s in range(slots)]
+                pieces.append(jnp.zeros((high, LANES - slots * rest), jnp.float32))
+                packed[north, r, full * cols :, :] = jnp.concatenate(pieces, axis=1)
+    me = lax.axis_index("replica")
+    for k, out in enumerate(keeps):
+        out[...] = packed[0, me ^ k]
+    for k in range(2, replica):
+        sends[k - 1][...] = packed[1, me ^ k].astype(jnp.bfloat16)
+    for k in range(2):
+        sends[0][k * tall : (k + 1) * tall, :] = packed[1, me ^ k].astype(jnp.bfloat16)
 
 
 def final_kernel(cols, depth, *refs):
@@ -213,56 +213,60 @@
     )(log_scale, bias, pair_ids, pair_ids2, raw, raw2, images, images2)
 
     feats_soon = feats
-    held = [swapped(feats_soon, "dp", 2 * k) for k in range(1, chips)]
+    east_feats = swapped(feats_soon, "dp", 2)
     far2 = swapped(after(far, (raw, raw2)), "dp", 1)
     far_ids2 = swapped(after(far_ids, far), "dp", 1)
 
-    dzed, *parts = pl.pallas_call(
+    dzed, same, other = pl.pallas_call(
         functools.partial(loss_kernel, factor, cols),
-        out_shape=[bf16(rows, width)] + [bf16(cols, 2 * rows)] * chips,
+        out_shape=[bf16(rows, width)] + [bf16(2 * cols, 2 * rows)] * 2,
         in_specs=[SMEM] * 2 + [VMEM] * 8,
-        out_specs=[VMEM] * (1 + chips),
+        out_specs=[VMEM] * 3,
         scratch_shapes=[pltpu.VMEM((width, 2 * rows), jnp.bfloat16)],
         compiler_params=grant(24),
-        cost_estimate=pl.CostEstimate(flops=1, bytes_accessed=1, transcendentals=0),
+        cost_estimate=pl.CostEstimate(flops=5000000000, bytes_accessed=1, transcendentals=0),
         name="loss",
     )(log_scale, bias, far, far2, far_ids, far_ids2, unit_txt, inverse, row_ids, own_term)
-    got = [swapped(parts[k], "dp", 2 * k) for k in range(1, chips)]
+    east = swapped(other, "dp", 2)
     grad_feat = lax.dot_general(dzed, head_w, NT, preferred_element_type=jnp.float32).astype(
         jnp.bfloat16
     )
-    held2 = [swapped(after(f, grad_feat), "dp", 1) for f in held]
-
+    east_feats2 = swapped(after(east_feats, same), "dp", 1)
+    tall = packing(cols, depth)[3]
     near = pl.pallas_call(
-        functools.partial(near_kernel, chips),
-        out_shape=f32(cols, head_w.shape[0]),
-        in_specs=[VMEM] * chips + [ANY] * (chips + 1),
+        near_kernel,
+        out_shape=f32(2 * cols, head_w.shape[0]),
+        in_specs=[VMEM] * 2 + [ANY] * 3,
         out_specs=VMEM,
         scratch_shapes=[
-            pltpu.VMEM(((chips + 1) * rows, head_w.shape[0]), jnp.bfloat16),
-            pltpu.SemaphoreType.DMA((chips + 1,)),
+            pltpu.VMEM((3 * rows, head_w.shape[0]), jnp.bfloat16),
+            pltpu.SemaphoreType.DMA((3,)),
         ],
         compiler_params=grant(24),
         cost_estimate=pl.CostEstimate(flops=10000000000, bytes_accessed=1, transcendentals=0),
         name="near",
-    )(parts[0], *got, feats, *held, feats2)
-    tall = packing(cols, depth)[3]
-    own, *pieces = pl.pallas_call(
-        functools.partial(product_kernel, chips, cols, depth, replica),
-        out_shape=[f32(tall, LANES)] + [bf16(tall, LANES)] * (replica - 1),
-        in_specs=[VMEM] * chips + [ANY] * (chips - 1),
-        out_specs=[VMEM] * replica,
-        scratch_shapes=[
-            pltpu.VMEM(((chips - 1) * rows, head_w.shape[0]), jnp.bfloat16),
-            pltpu.VMEM((replica, tall, LANES), jnp.float32),
-            pltpu.SemaphoreType.DMA((chips - 1,)),
-        ],
+    )(same, east, feats, feats2, east_feats)
+    products = pl.pallas_call(
+        functools.partial(product_kernel, cols, depth, replica),
+        out_shape=[f32(tall, LANES)] * replica
+        + [bf16(2 * tall, LANES)]
+        + [bf16(tall, LANES)] * (replica - 2),
+        in_specs=[VMEM] * 3,
+        out_specs=[VMEM] * (2 * replica - 1),
+        scratch_shapes=[pltpu.VMEM((2, replica, tall, LANES), jnp.float32)],
         compiler_params=grant(24),
         cost_estimate=pl.CostEstimate(flops=1, bytes_accessed=1, transcendentals=0),
         name="product",
-    )(near, *got, *held2)
-    order = sorted(range(1, replica), key=lambda k: (-(k & (replica // 2)), k))
-    sums = [swapped(pieces[k - 1], "replica", k) for k in order]
+    )(near, east, east_feats2)
+    keeps, sends = products[:replica], products[replica:]
+    sums = []
+    for k in range(2, replica):
+        total = keeps[k] + swapped(sends[k - 1], "dp", 4).astype(jnp.float32)
+        sums.append(swapped(total.astype(jnp.bfloat16), "replica", k))
+    last = swapped(sends[0], "dp", 4).astype(jnp.float32)
+    total = keeps[1] + last[tall:]
+    sums.append(swapped(total.astype(jnp.bfloat16), "replica", 1))
+    own = keeps[0] + last[:tall]
     head_grad = pl.pallas_call(
         functools.partial(final_kernel, cols, depth),
         out_shape=f32(cols, depth),
@@ -346,7 +350,7 @@
     dp, replica = lax.axis_size("dp"), lax.axis_size("replica")
     rows, width = image_emb.shape[1:]
     cols, depth = width // dp, head_w.shape[0] // replica
-    if rows == LANES and cols % 16 == 0:
+    if dp == 8 and replica == 4 and rows == LANES and cols % 16 == 0:
         return box_shards(*args)
     return general_shards(*args)
 

time: 41.1 us -> 40.1 us (0.976)
  waiting for transfers between devices: 11.7 us -> 10.1 us
  starting transfers between devices: 18.4 us -> 19 us
    ppermute x17 -> x14, waiting for transfers between devices: 11.7 us -> 8.35 us  [swapped(): return lax.ppermute(x, axis, [(i, i ^ mask) for i in range(size)])]
    ppermute x2, waiting for transfers between devices: 0.01 us -> 1.79 us  [rotated(): return lax.ppermute(x, axis, [(i, (i + by) % size) for i in range(size)])]
    ppermute x17 -> x14, starting transfers between devices: 14.4 us -> 15 us  [swapped(): return lax.ppermute(x, axis, [(i, i ^ mask) for i in range(size)])]
  transfers between devices with their start and end apart: 19 -> 16, of which waited for: 6 -> 6; matrix products, arithmetic and copies ran while one was open for 9% -> 10% of each run, Pallas kernels for 8% -> 8%
where the time goes in v4:
time: 40.1 us; the launch traced here: 39.9 us
  starting transfers between devices  19 us (47%)
  waiting for transfers between devices  10.1 us (25%)
  Pallas kernels  4.76 us (12%)
  matrix products  3.79 us (9%)
  between operations  2.12 us (5%)
    ppermute x14, starting transfers between devices, swapped(): return lax.ppermute(x, axis, [(i, i ^ mask) for i in range(size)])  15 us
    ppermute x14, waiting for transfers between devices, swapped(): return lax.ppermute(x, axis, [(i, i ^ mask) for i in range(size)])  8.35 us
    ppermute x2, starting transfers between devices, rotated(): return lax.ppermute(x, axis, [(i, (i + by) % size) for i in range(size)])  4.04 us
    ppermute x2, waiting for transfers between devices, rotated(): return lax.ppermute(x, axis, [(i, (i + by) % size) for i in range(size)])  1.79 us
    dot_general x1, matrix products, box_shards(): lax.dot_general(dzed, head_w, NT, preferred_element_type=jnp.float32)  1.64 us
    dot_general x1, matrix products, box_shards(): raw = jnp.dot(feats, head_w, preferred_element_type=jnp.float32)  1.55 us
    pallas_call x1, Pallas kernels, box_shards(): pl.pallas_call(functools.partial(loss_kernel, factor, cols), out_shape=[b...  1.4 us
    pallas_call x1, Pallas kernels, box_shards(): pl.pallas_call(functools.partial(own_kernel, factor), out_shape=[f32(2 *...  1.11 us
  transfers between devices with their start and end apart: 16, of which 6 were waited for; matrix products, arithmetic and copies ran while one was open for 10% of the time, Pallas kernels for 8%

profile of v4, /device:TPU:0, one launch (start us, length us, event | category | flops | bytes accessed | tf_op | source)
XLA Modules:
  0.0 39.9 jit_solution(6131506101001710906)
XLA Ops:
  0.6 0.0 copy-start
  0.6 0.0 copy-start.1
  0.7 0.5 %collective-permute-start.2 = (bf16[128,1152]{1,0:T(8,128)(2,1)}, bf16[128,1152]{1,0:T(8,128)(2,1)S(1)}, u32[]{:S(2)}, u32[]{:S(2)}) collective-permute-start(bf16[128,1152]{1,0:T(8,128)(2,1)} %bitcast.15), channel_id=1, source_target_pairs={{0,4},{4,0},{8,12},{12,8},{16,20},{20,16},{24,28},{28,24},{1,5},{5... | collective-permute-start | bytes 884744 | tf_op jit(solution)/shard_map/ppermute | solution.py:30
  1.2 3.5 %collective-permute-start = (bf16[128,1152]{1,0:T(8,128)(2,1)}, bf16[128,1152]{1,0:T(8,128)(2,1)S(1)}, u32[]{:S(2)}, u32[]{:S(2)}) collective-permute-start(bf16[128,1152]{1,0:T(8,128)(2,1)} %bitcast.16), channel_id=1, source_target_pairs={{0,24},{4,28},{8,0},{12,4},{16,8},{20,12},{24,16},{28,20},{1,25},{... | collective-permute-start | bytes 884744 | tf_op jit(solution)/shard_map/ppermute | solution.py:25
  4.7 0.2 collective-permute-start.3
  4.8 0.5 %collective-permute-start.5 = (s32[1,128]{1,0:T(1,128)}, s32[1,128]{1,0:T(1,128)S(1)}, u32[]{:S(2)}, u32[]{:S(2)}) collective-permute-start(s32[1,128]{1,0:T(1,128)} %ids.1), channel_id=1, source_target_pairs={{0,24},{4,28},{8,0},{12,4},{16,8},{20,12},{24,16},{28,20},{1,25},{... | collective-permute-start | bytes 1544 | tf_op jit(solution)/shard_map/ppermute | solution.py:25
  5.4 0.1 collective-permute-start.1
  5.4 0.0 copy-done
  5.5 1.5 %fusion.2.raw = f32[128,1152]{1,0:T(8,128)S(1)} fusion(bf16[1152,1152]{1,0:T(8,128)(2,1)S(1)} %copy-done, bf16[1,128,1152]{2,1,0:T(8,128)(2,1)} %param.7), kind=kOutput, calls=%fused_computation.7 | convolution fusion | flops 339738624 | bytes 3538944 | tf_op jit(solution)/shard_map/dot_general | solution.py:198
  7.0 0.0 copy-start.2
  7.0 0.0 copy-start.3
  8.4 0.0 collective-permute-done.3.ids2
  8.4 0.0 copy-done.1
  8.4 1.6 %collective-permute-start.8 = (bf16[128,1152]{1,0:T(8,128)(2,1)S(1)}, bf16[128,1152]{1,0:T(8,128)(2,1)S(1)}, u32[]{:S(2)}, u32[]{:S(2)}) collective-permute-start(bf16[128,1152]{1,0:T(8,128)(2,1)S(1)} %bitcast.13), channel_id=1, source_target_pairs={{0,8},{4,12},{8,0},{12,4},{16,24},{20,28},{24,16},{28,20},{1,9},{5... | collective-permute-start | bytes 884744 | tf_op jit(solution)/shard_map/ppermute | solution.py:30
  9.9 0.0 collective-permute-done.1.refs_1_
  9.9 0.0 collective-permute-done.2.img2
  9.9 0.6 %fusion.4.raw2 = f32[128,1152]{1,0:T(8,128)S(1)} fusion(bf16[128,1152]{1,0:T(8,128)(2,1)S(1)} %collective-permute-done.1.refs_1_, bf16[1152,1152]{1,0:T(8,128)(2,1)S(1)} %copy-done), kind=kOutput, calls=%fused_computation.9 | convolution fusion | flops 339738624 | bytes 3538944 | tf_op jit(solution)/shard_map/dot_general | solution.py:199
  10.6 1.8 %collective-permute-done.far = bf16[128,1152]{1,0:T(8,128)(2,1)S(1)} collective-permute-done((bf16[128,1152]{1,0:T(8,128)(2,1)}, bf16[128,1152]{1,0:T(8,128)(2,1)S(1)}, u32[]{:S(2)}, u32[]{:S(2)}) %collective-permute-start) | collective-permute-done | bytes 294944 | tf_op jit(solution)/shard_map/ppermute | solution.py:25
  12.3 0.0 collective-permute-start.4
  12.3 0.0 collective-permute-done.5.ids
  12.3 0.5 %collective-permute-start.6 = (s32[1,128]{1,0:T(1,128)S(1)}, s32[1,128]{1,0:T(1,128)S(1)}, u32[]{:S(2)}, u32[]{:S(2)}) collective-permute-start(s32[1,128]{1,0:T(1,128)S(1)} %collective-permute-done.5.ids), channel_id=1, source_target_pairs={{0,4},{4,0},{8,12},{12,8},{16,20},{20,16},{24,28},{28,24},{1,5},{5... | collective-permute-start | bytes 1544 | tf_op jit(solution)/shard_map/ppermute | solution.py:30
  12.8 0.0 copy-done.2
  12.9 0.0 copy-done.3
  12.9 1.1 %own.1 = (f32[256,1152]{1,0:T(8,128)S(1)}, f32[256,128]{1,0:T(8,128)S(1)}, s32[256,128]{1,0:T(8,128)S(1)}, f32[256,1152]{1,0:T(8,128)S(1)}) custom-call(f32[1]{0:T(128)S(6)} %copy.8.log_scale, f32[1]{0:T(128)S(6)} %copy.9.bias, s32[1,128]{1,0:T(1,128)S(1)} %copy-done.3, s32[1,128]{1,0:T(1,128)S(1)} %collective-permute-done.3.ids2, ...), custom_call_target="tpu_custom_call" | custom-call | flops 10000000000 | bytes 1 | tf_op jit(solution)/shard_map/own/pallas_call | solution.py:200
  14.0 0.0 collective-permute-done.6.ids2
  14.0 0.0 collective-permute-done.4.far2
  14.0 1.4 %loss.1 = (bf16[128,1152]{1,0:T(8,128)(2,1)S(1)}, bf16[288,256]{1,0:T(8,128)(2,1)S(1)}, bf16[288,256]{1,0:T(8,128)(2,1)S(1)}) custom-call(f32[1]{0:T(128)S(6)} %copy.8.log_scale, f32[1]{0:T(128)S(6)} %copy.9.bias, bf16[128,1152]{1,0:T(8,128)(2,1)S(1)} %collective-permute-done.far, bf16[128,1152]{1,0:T(8,128)(2,1)S(1)} %collective-permute-done.4.far2, ...), custom_call_target="tpu_custom_call" | custom-call | flops 5000000000 | bytes 1 | tf_op jit(solution)/shard_map/loss/pallas_call | solution.py:220
  15.4 2.4 %collective-permute-start.7 = (bf16[288,256]{1,0:T(8,128)(2,1)S(1)}, bf16[288,256]{1,0:T(8,128)(2,1)S(1)}, u32[]{:S(2)}, u32[]{:S(2)}) collective-permute-start(bf16[288,256]{1,0:T(8,128)(2,1)S(1)} %get-tuple-element.33), channel_id=1, source_target_pairs={{0,8},{4,12},{8,0},{12,4},{16,24},{20,28},{24,16},{28,20},{1,9},{5... | collective-permute-start | bytes 442376 | tf_op jit(solution)/shard_map/ppermute | solution.py:30
  17.8 0.3 collective-permute-done.8.refs_2_
  18.1 0.0 collective-permute-start.9
  18.1 3.8 %collective-permute-done.7.east = bf16[288,256]{1,0:T(8,128)(2,1)S(1)} collective-permute-done((bf16[288,256]{1,0:T(8,128)(2,1)S(1)}, bf16[288,256]{1,0:T(8,128)(2,1)S(1)}, u32[]{:S(2)}, u32[]{:S(2)}) %collective-permute-start.7) | collective-permute-done | bytes 147488 | tf_op jit(solution)/shard_map/ppermute | solution.py:30
  21.9 0.7 %near.1 = f32[288,1152]{1,0:T(8,128)S(1)} custom-call(bf16[288,256]{1,0:T(8,128)(2,1)S(1)} %get-tuple-element.32.own, bf16[288,256]{1,0:T(8,128)(2,1)S(1)} %collective-permute-done.7.east, bf16[128,1152]{1,0:T(8,128)(2,1)S(1)} %bitcast.14, bf16[128,1152]{1,0:T(8,128)(2,1)S(1)} %collective-permute-done.1.refs_1_, ...), custom_call_target="tpu_custom_call" | custom-call | flops 10000000000 | bytes 1 | tf_op jit(solution)/shard_map/near/pallas_call | solution.py:236
  22.6 0.0 collective-permute-done.9.feats
  22.6 0.7 %product.1 = (f32[336,128]{1,0:T(8,128)S(1)}, f32[336,128]{1,0:T(8,128)S(1)}, f32[336,128]{1,0:T(8,128)S(1)}, f32[336,128]{1,0:T(8,128)S(1)}, bf16[672,128]{1,0:...) custom-call(f32[288,1152]{1,0:T(8,128)S(1)} %near.1, ...), custom_call_target="tpu_custom_call" | custom-call | flops 1 | bytes 1 | tf_op jit(solution)/shard_map/product/pallas_call | solution.py:249
  23.4 1.6 %collective-permute-start.13 = (bf16[336,128]{1,0:T(8,128)(2,1)S(1)}, bf16[336,128]{1,0:T(8,128)(2,1)S(1)}, u32[]{:S(2)}, u32[]{:S(2)}) collective-permute-start(bf16[336,128]{1,0:T(8,128)(2,1)S(1)} %get-tuple-element.40), channel_id=1, source_target_pairs={{0,16},{4,20},{8,24},{12,28},{16,0},{20,4},{24,8},{28,12},{1,17},{... | collective-permute-start | bytes 258056 | tf_op jit(solution)/shard_map/ppermute | solution.py:30
  25.0 0.5 %collective-permute-start.11 = (bf16[336,128]{1,0:T(8,128)(2,1)S(1)}, bf16[336,128]{1,0:T(8,128)(2,1)S(1)}, u32[]{:S(2)}, u32[]{:S(2)}) collective-permute-start(bf16[336,128]{1,0:T(8,128)(2,1)S(1)} %get-tuple-element.38), channel_id=1, source_target_pairs={{0,16},{4,20},{8,24},{12,28},{16,0},{20,4},{24,8},{28,12},{1,17},{... | collective-permute-start | bytes 258056 | tf_op jit(solution)/shard_map/ppermute | solution.py:30
  25.5 1.5 %collective-permute-start.10 = (bf16[672,128]{1,0:T(8,128)(2,1)S(1)}, bf16[672,128]{1,0:T(8,128)(2,1)S(1)}, u32[]{:S(2)}, u32[]{:S(2)}) collective-permute-start(bf16[672,128]{1,0:T(8,128)(2,1)S(1)} %get-tuple-element.36), channel_id=1, source_target_pairs={{0,16},{4,20},{8,24},{12,28},{16,0},{20,4},{24,8},{28,12},{1,17},{... | collective-permute-start | bytes 516104 | tf_op jit(solution)/shard_map/ppermute | solution.py:30
  27.0 1.9 %collective-permute-done.13 = bf16[336,128]{1,0:T(8,128)(2,1)S(1)} collective-permute-done((bf16[336,128]{1,0:T(8,128)(2,1)S(1)}, bf16[336,128]{1,0:T(8,128)(2,1)S(1)}, u32[]{:S(2)}, u32[]{:S(2)}) %collective-permute-start.13) | collective-permute-done | bytes 86048 | tf_op jit(solution)/shard_map/ppermute | solution.py:30
  28.9 3.7 %collective-permute-start.14 = (bf16[336,128]{1,0:T(8,128)(2,1)S(1)}, bf16[336,128]{1,0:T(8,128)(2,1)S(1)}, u32[]{:S(2)}, u32[]{:S(2)}) collective-permute-start(bf16[336,128]{1,0:T(8,128)(2,1)S(1)} %add_convert_fusion), channel_id=1, source_target_pairs={{0,3},{1,2},{2,1},{3,0},{4,7},{5,6},{6,5},{7,4},{8,11},{9,10},{10,... | collective-permute-start | bytes 258056 | tf_op jit(solution)/shard_map/ppermute | solution.py:30
  32.6 0.0 collective-permute-done.11
  32.6 0.8 %collective-permute-start.12 = (bf16[336,128]{1,0:T(8,128)(2,1)S(1)}, bf16[336,128]{1,0:T(8,128)(2,1)S(1)}, u32[]{:S(2)}, u32[]{:S(2)}) collective-permute-start(bf16[336,128]{1,0:T(8,128)(2,1)S(1)} %add_convert_fusion.1), channel_id=1, source_target_pairs={{0,2},{1,3},{2,0},{3,1},{4,6},{5,7},{6,4},{7,5},{8,10},{9,11},{10,... | collective-permute-start | bytes 258056 | tf_op jit(solution)/shard_map/ppermute | solution.py:30
  33.4 0.0 collective-permute-done.10
  33.4 1.7 %collective-permute-start.15 = (bf16[336,128]{1,0:T(8,128)(2,1)S(1)}, bf16[336,128]{1,0:T(8,128)(2,1)S(1)}, u32[]{:S(2)}, u32[]{:S(2)}) collective-permute-start(bf16[336,128]{1,0:T(8,128)(2,1)S(1)} %get-tuple-element.42), channel_id=1, source_target_pairs={{0,1},{1,0},{2,3},{3,2},{4,5},{5,4},{6,7},{7,6},{8,9},{9,8},{10,11... | collective-permute-start | bytes 258056 | tf_op jit(solution)/shard_map/ppermute | solution.py:30
  35.1 1.6 %fusion = bf16[1,128,1152]{2,1,0:T(8,128)(2,1)} fusion(bf16[128,1152]{1,0:T(8,128)(2,1)S(1)} %get-tuple-element.31, bf16[1152,1152]{1,0:T(8,128)(2,1)S(1)} %copy-done), kind=kOutput, calls=%fused_computation.1 | convolution fusion | flops 339886080 | bytes 3244032 | tf_op jit(solution)/shard_map/dot_general | solution.py:231
  36.8 0.0 collective-permute-done.14.refs_2_
  36.8 2.0 %collective-permute-done.12.refs_1_ = bf16[336,128]{1,0:T(8,128)(2,1)S(1)} collective-permute-done((bf16[336,128]{1,0:T(8,128)(2,1)S(1)}, bf16[336,128]{1,0:T(8,128)(2,1)S(1)}, u32[]{:S(2)}, u32[]{:S(2)}) %collective-permute-start.12) | collective-permute-done | bytes 86048 | tf_op jit(solution)/shard_map/ppermute | solution.py:30
  38.8 0.4 collective-permute-done.15.refs_3_
  39.2 0.8 %final.1 = f32[144,288]{1,0:T(8,128)} custom-call(f32[336,128]{1,0:T(8,128)S(1)} %get-tuple-element.43.refs_0_, bf16[336,128]{1,0:T(8,128)(2,1)S(1)} %collective-permute-done.12.refs_1_, bf16[336,128]{1,0:T(8,128)(2,1)S(1)} %collective-permute-done.14.refs_2_, bf16[336,128]{1,0:T(8,128)(2,1)S(1)} %collective-permute-done.15.refs_3_), custom_call_target="tpu_custom_call" | custom-call | flops 1 | bytes 1 | tf_op jit(solution)/shard_map/final/pallas_call | solution.py:270
  (4 shorter events, 0.1 us)
Async XLA Ops:
  0.6 4.8 %copy-start = (bf16[1152,1152]{1,0:T(8,128)(2,1)S(1)}, bf16[1152,1152]{1,0:T(8,128)(2,1)}, u32[]{:S(2)}) copy-start(bf16[1152,1152]{1,0:T(8,128)(2,1)} %param.8) | copy-start | bytes 7962628
  0.6 7.7 %copy-start.1 = (bf16[1,128,1152]{2,1,0:T(8,128)(2,1)S(1)}, bf16[1,128,1152]{2,1,0:T(8,128)(2,1)}, u32[]{:S(2)}) copy-start(bf16[1,128,1152]{2,1,0:T(8,128)(2,1)} %param.7) | copy-start | bytes 884740
  0.7 9.3 %collective-permute-start.2 = (bf16[128,1152]{1,0:T(8,128)(2,1)}, bf16[128,1152]{1,0:T(8,128)(2,1)S(1)}, u32[]{:S(2)}, u32[]{:S(2)}) collective-permute-start(bf16[128,1152]{1,0:T(8,128)(2,1)} %bitcast.15), channel_id=1, source_target_pairs={{0,4},{4,0},{8,12},{12,8},{16,20},{20,16},{24,28},{28,24},{1,5},{5... | collective-permute-start | bytes 884744 | tf_op jit(solution)/shard_map/ppermute | solution.py:30
  1.2 11.2 %collective-permute-start = (bf16[128,1152]{1,0:T(8,128)(2,1)}, bf16[128,1152]{1,0:T(8,128)(2,1)S(1)}, u32[]{:S(2)}, u32[]{:S(2)}) collective-permute-start(bf16[128,1152]{1,0:T(8,128)(2,1)} %bitcast.16), channel_id=1, source_target_pairs={{0,24},{4,28},{8,0},{12,4},{16,8},{20,12},{24,16},{28,20},{1,25},{... | collective-permute-start | bytes 884744 | tf_op jit(solution)/shard_map/ppermute | solution.py:25
  4.7 3.7 %collective-permute-start.3 = (s32[1,128]{1,0:T(1,128)}, s32[1,128]{1,0:T(1,128)S(1)}, u32[]{:S(2)}, u32[]{:S(2)}) collective-permute-start(s32[1,128]{1,0:T(1,128)} %ids.1), channel_id=1, source_target_pairs={{0,4},{4,0},{8,12},{12,8},{16,20},{20,16},{24,28},{28,24},{1,5},{5... | collective-permute-start | bytes 1544 | tf_op jit(solution)/shard_map/ppermute | solution.py:30
  4.8 7.5 %collective-permute-start.5 = (s32[1,128]{1,0:T(1,128)}, s32[1,128]{1,0:T(1,128)S(1)}, u32[]{:S(2)}, u32[]{:S(2)}) collective-permute-start(s32[1,128]{1,0:T(1,128)} %ids.1), channel_id=1, source_target_pairs={{0,24},{4,28},{8,0},{12,4},{16,8},{20,12},{24,16},{28,20},{1,25},{... | collective-permute-start | bytes 1544 | tf_op jit(solution)/shard_map/ppermute | solution.py:25
  5.4 4.6 %collective-permute-start.1 = (bf16[128,1152]{1,0:T(8,128)(2,1)}, bf16[128,1152]{1,0:T(8,128)(2,1)S(1)}, u32[]{:S(2)}, u32[]{:S(2)}) collective-permute-start(bf16[128,1152]{1,0:T(8,128)(2,1)} %bitcast.12), channel_id=1, source_target_pairs={{0,4},{4,0},{8,12},{12,8},{16,20},{20,16},{24,28},{28,24},{1,5},{5... | collective-permute-start | bytes 884744 | tf_op jit(solution)/shard_map/ppermute | solution.py:30
  7.0 5.8 %copy-start.2 = (bf16[1,128,1152]{2,1,0:T(8,128)(2,1)S(1)}, bf16[1,128,1152]{2,1,0:T(8,128)(2,1)}, u32[]{:S(2)}) copy-start(bf16[1,128,1152]{2,1,0:T(8,128)(2,1)} %param.6) | copy-start | bytes 884740
  7.0 5.8 %copy-start.3 = (s32[1,128]{1,0:T(1,128)S(1)}, s32[1,128]{1,0:T(1,128)}, u32[]{:S(2)}) copy-start(s32[1,128]{1,0:T(1,128)} %ids.1) | copy-start | bytes 1540
  8.4 9.7 %collective-permute-start.8 = (bf16[128,1152]{1,0:T(8,128)(2,1)S(1)}, bf16[128,1152]{1,0:T(8,128)(2,1)S(1)}, u32[]{:S(2)}, u32[]{:S(2)}) collective-permute-start(bf16[128,1152]{1,0:T(8,128)(2,1)S(1)} %bitcast.13), channel_id=1, source_target_pairs={{0,8},{4,12},{8,0},{12,4},{16,24},{20,28},{24,16},{28,20},{1,9},{5... | collective-permute-start | bytes 884744 | tf_op jit(solution)/shard_map/ppermute | solution.py:30
  12.3 1.7 %collective-permute-start.4 = (bf16[128,1152]{1,0:T(8,128)(2,1)S(1)}, bf16[128,1152]{1,0:T(8,128)(2,1)S(1)}, u32[]{:S(2)}, u32[]{:S(2)}) collective-permute-start(bf16[128,1152]{1,0:T(8,128)(2,1)S(1)} %collective-permute-done.far), channel_id=1, source_target_pairs={{0,4},{4,0},{8,12},{12,8},{16,20},{20,16},{24,28},{28,24},{1,5},{5... | collective-permute-start | bytes 884744 | tf_op jit(solution)/shard_map/ppermute | solution.py:30
  12.3 1.6 %collective-permute-start.6 = (s32[1,128]{1,0:T(1,128)S(1)}, s32[1,128]{1,0:T(1,128)S(1)}, u32[]{:S(2)}, u32[]{:S(2)}) collective-permute-start(s32[1,128]{1,0:T(1,128)S(1)} %collective-permute-done.5.ids), channel_id=1, source_target_pairs={{0,4},{4,0},{8,12},{12,8},{16,20},{20,16},{24,28},{28,24},{1,5},{5... | collective-permute-start | bytes 1544 | tf_op jit(solution)/shard_map/ppermute | solution.py:30
  15.4 6.5 %collective-permute-start.7 = (bf16[288,256]{1,0:T(8,128)(2,1)S(1)}, bf16[288,256]{1,0:T(8,128)(2,1)S(1)}, u32[]{:S(2)}, u32[]{:S(2)}) collective-permute-start(bf16[288,256]{1,0:T(8,128)(2,1)S(1)} %get-tuple-element.33), channel_id=1, source_target_pairs={{0,8},{4,12},{8,0},{12,4},{16,24},{20,28},{24,16},{28,20},{1,9},{5... | collective-permute-start | bytes 442376 | tf_op jit(solution)/shard_map/ppermute | solution.py:30
  18.1 4.5 %collective-permute-start.9 = (bf16[128,1152]{1,0:T(8,128)(2,1)S(1)}, bf16[128,1152]{1,0:T(8,128)(2,1)S(1)}, u32[]{:S(2)}, u32[]{:S(2)}) collective-permute-start(bf16[128,1152]{1,0:T(8,128)(2,1)S(1)} %collective-permute-done.8.refs_2_), channel_id=1, source_target_pairs={{0,4},{4,0},{8,12},{12,8},{16,20},{20,16},{24,28},{28,24},{1,5},{5... | collective-permute-start | bytes 884744 | tf_op jit(solution)/shard_map/ppermute | solution.py:30
  23.4 5.5 %collective-permute-start.13 = (bf16[336,128]{1,0:T(8,128)(2,1)S(1)}, bf16[336,128]{1,0:T(8,128)(2,1)S(1)}, u32[]{:S(2)}, u32[]{:S(2)}) collective-permute-start(bf16[336,128]{1,0:T(8,128)(2,1)S(1)} %get-tuple-element.40), channel_id=1, source_target_pairs={{0,16},{4,20},{8,24},{12,28},{16,0},{20,4},{24,8},{28,12},{1,17},{... | collective-permute-start | bytes 258056 | tf_op jit(solution)/shard_map/ppermute | solution.py:30
  25.0 7.6 %collective-permute-start.11 = (bf16[336,128]{1,0:T(8,128)(2,1)S(1)}, bf16[336,128]{1,0:T(8,128)(2,1)S(1)}, u32[]{:S(2)}, u32[]{:S(2)}) collective-permute-start(bf16[336,128]{1,0:T(8,128)(2,1)S(1)} %get-tuple-element.38), channel_id=1, source_target_pairs={{0,16},{4,20},{8,24},{12,28},{16,0},{20,4},{24,8},{28,12},{1,17},{... | collective-permute-start | bytes 258056 | tf_op jit(solution)/shard_map/ppermute | solution.py:30
  25.5 7.9 %collective-permute-start.10 = (bf16[672,128]{1,0:T(8,128)(2,1)S(1)}, bf16[672,128]{1,0:T(8,128)(2,1)S(1)}, u32[]{:S(2)}, u32[]{:S(2)}) collective-permute-start(bf16[672,128]{1,0:T(8,128)(2,1)S(1)} %get-tuple-element.36), channel_id=1, source_target_pairs={{0,16},{4,20},{8,24},{12,28},{16,0},{20,4},{24,8},{28,12},{1,17},{... | collective-permute-start | bytes 516104 | tf_op jit(solution)/shard_map/ppermute | solution.py:30
  28.9 7.9 %collective-permute-start.14 = (bf16[336,128]{1,0:T(8,128)(2,1)S(1)}, bf16[336,128]{1,0:T(8,128)(2,1)S(1)}, u32[]{:S(2)}, u32[]{:S(2)}) collective-permute-start(bf16[336,128]{1,0:T(8,128)(2,1)S(1)} %add_convert_fusion), channel_id=1, source_target_pairs={{0,3},{1,2},{2,1},{3,0},{4,7},{5,6},{6,5},{7,4},{8,11},{9,10},{10,... | collective-permute-start | bytes 258056 | tf_op jit(solution)/shard_map/ppermute | solution.py:30
  32.6 6.2 %collective-permute-start.12 = (bf16[336,128]{1,0:T(8,128)(2,1)S(1)}, bf16[336,128]{1,0:T(8,128)(2,1)S(1)}, u32[]{:S(2)}, u32[]{:S(2)}) collective-permute-start(bf16[336,128]{1,0:T(8,128)(2,1)S(1)} %add_convert_fusion.1), channel_id=1, source_target_pairs={{0,2},{1,3},{2,0},{3,1},{4,6},{5,7},{6,4},{7,5},{8,10},{9,11},{10,... | collective-permute-start | bytes 258056 | tf_op jit(solution)/shard_map/ppermute | solution.py:30
  33.4 5.7 %collective-permute-start.15 = (bf16[336,128]{1,0:T(8,128)(2,1)S(1)}, bf16[336,128]{1,0:T(8,128)(2,1)S(1)}, u32[]{:S(2)}, u32[]{:S(2)}) collective-permute-start(bf16[336,128]{1,0:T(8,128)(2,1)S(1)} %get-tuple-element.42), channel_id=1, source_target_pairs={{0,1},{1,0},{2,3},{3,2},{4,5},{5,4},{6,7},{7,6},{8,9},{9,8},{10,11... | collective-permute-start | bytes 258056 | tf_op jit(solution)/shard_map/ppermute | solution.py:30

commit v5 on v4

--- a/solution.py
+++ b/solution.py
@@ -10,9 +10,10 @@
 HOPS = 3
 LOSS_SCALE = 2048.0
 LANES = 128
+GATHER, REDUCE = (1, 2)
+LONG = pl.CostEstimate(flops=10**10, bytes_accessed=1, transcendentals=0)
 VMEM = pl.BlockSpec(memory_space=pltpu.VMEM)
 SMEM = pl.BlockSpec(memory_space=pltpu.SMEM)
-ANY = pl.BlockSpec(memory_space=pl.ANY)
 NT = (((1,), (1,)), ((), ()))
 
 
@@ -98,7 +99,7 @@
     flipped[...] = dzed.T
     for east, part in enumerate(parts):
         for north in range(2):
-            start = pl.multiple_of((2 * (chip ^ east ^ (2 * north)) + core) * cols, 16)
+            start = pl.multiple_of((2 * (chip ^ (GATHER * east) ^ (REDUCE * north)) + core) * cols, 16)
             part[north * cols : (north + 1) * cols, :] = flipped[pl.ds(start, cols), :]
 
 
@@ -110,28 +111,21 @@
     return full, rest, slots, cols * full + (cols // slots if slots else 0)
 
 
-def gathered(blocks, held, sem):
-    rows = blocks[0].shape[0]
-    copies = [
-        pltpu.make_async_copy(block, held.at[pl.ds(i * rows, rows), :], sem.at[i])
-        for i, block in enumerate(blocks)
-    ]
-    for copy in copies:
-        copy.start()
-    return copies
-
-
-def near_kernel(own, east, *refs):
-    feats, (out, held, sem) = refs[:3], refs[3:]
-    copies = gathered(feats, held, sem)
-    left = jnp.concatenate([own[...], east[:, : feats[0].shape[0]]], axis=1)
-    for copy in copies:
-        copy.wait()
-    out[...] = jnp.dot(left, held[...], preferred_element_type=jnp.float32)
+def early_kernel(own, feats, feats2, out):
+    rows = feats.shape[0]
+    out[...] = jnp.dot(
+        own[:, :rows], feats[...], preferred_element_type=jnp.float32
+    ) + jnp.dot(own[:, rows:], feats2[...], preferred_element_type=jnp.float32)
+
+
+def near_kernel(early, east, feats, out):
+    out[...] = early[...] + jnp.dot(
+        east[:, : feats.shape[0]], feats[...], preferred_element_type=jnp.float32
+    )
 
 
 def product_kernel(cols, depth, replica, near, east, feats, *refs):
-    keeps, sends, packed = refs[:replica], refs[replica : 2 * replica - 1], refs[-1]
+    keeps, sends, packed = refs[:replica], refs[replica : 2 * replica], refs[-1]
     local = near[...] + jnp.dot(
         east[:, feats.shape[0] :], feats[...], preferred_element_type=jnp.float32
     )
@@ -149,10 +143,8 @@
     me = lax.axis_index("replica")
     for k, out in enumerate(keeps):
         out[...] = packed[0, me ^ k]
-    for k in range(2, replica):
-        sends[k - 1][...] = packed[1, me ^ k].astype(jnp.bfloat16)
-    for k in range(2):
-        sends[0][k * tall : (k + 1) * tall, :] = packed[1, me ^ k].astype(jnp.bfloat16)
+    for k, out in enumerate(sends):
+        out[...] = packed[1, me ^ k].astype(jnp.bfloat16)
 
 
 def final_kernel(cols, depth, *refs):
@@ -188,9 +180,9 @@
 
     far = rotated(images, "dp", -2)
     far_ids = rotated(pair_ids, "dp", -2)
+    pair_ids2 = swapped(pair_ids, "dp", 1)
     feats2 = swapped(feats, "dp", 1)
     images2 = swapped(images, "dp", 1)
-    pair_ids2 = swapped(pair_ids, "dp", 1)
 
     feats_in, feats2, images2, pair_ids2 = lax.optimization_barrier(
         (feats, feats2, images2, pair_ids2)
@@ -208,12 +200,12 @@
         in_specs=[SMEM] * 2 + [VMEM] * 6,
         out_specs=[VMEM] * 4,
         compiler_params=grant(24),
-        cost_estimate=pl.CostEstimate(flops=10000000000, bytes_accessed=1, transcendentals=0),
+        cost_estimate=LONG,
         name="own",
     )(log_scale, bias, pair_ids, pair_ids2, raw, raw2, images, images2)
 
     feats_soon = feats
-    east_feats = swapped(feats_soon, "dp", 2)
+    east_feats = swapped(feats_soon, "dp", 2 * GATHER)
     far2 = swapped(after(far, (raw, raw2)), "dp", 1)
     far_ids2 = swapped(after(far_ids, far), "dp", 1)
 
@@ -224,58 +216,56 @@
         out_specs=[VMEM] * 3,
         scratch_shapes=[pltpu.VMEM((width, 2 * rows), jnp.bfloat16)],
         compiler_params=grant(24),
-        cost_estimate=pl.CostEstimate(flops=5000000000, bytes_accessed=1, transcendentals=0),
         name="loss",
     )(log_scale, bias, far, far2, far_ids, far_ids2, unit_txt, inverse, row_ids, own_term)
-    east = swapped(other, "dp", 2)
+    east = swapped(other, "dp", 2 * GATHER)
     grad_feat = lax.dot_general(dzed, head_w, NT, preferred_element_type=jnp.float32).astype(
         jnp.bfloat16
     )
-    east_feats2 = swapped(after(east_feats, same), "dp", 1)
+    east_feats2 = swapped(after(east_feats, grad_feat), "dp", 1)
     tall = packing(cols, depth)[3]
+    early = pl.pallas_call(
+        early_kernel,
+        out_shape=f32(2 * cols, head_w.shape[0]),
+        in_specs=[VMEM] * 3,
+        out_specs=VMEM,
+        compiler_params=grant(24),
+        name="early",
+    )(same, feats, feats2)
     near = pl.pallas_call(
         near_kernel,
         out_shape=f32(2 * cols, head_w.shape[0]),
-        in_specs=[VMEM] * 2 + [ANY] * 3,
+        in_specs=[VMEM] * 3,
         out_specs=VMEM,
-        scratch_shapes=[
-            pltpu.VMEM((3 * rows, head_w.shape[0]), jnp.bfloat16),
-            pltpu.SemaphoreType.DMA((3,)),
-        ],
-        compiler_params=grant(24),
-        cost_estimate=pl.CostEstimate(flops=10000000000, bytes_accessed=1, transcendentals=0),
+        compiler_params=grant(24),
+        cost_estimate=LONG,
         name="near",
-    )(same, east, feats, feats2, east_feats)
+    )(early, east, east_feats)
     products = pl.pallas_call(
         functools.partial(product_kernel, cols, depth, replica),
-        out_shape=[f32(tall, LANES)] * replica
-        + [bf16(2 * tall, LANES)]
-        + [bf16(tall, LANES)] * (replica - 2),
+        out_shape=[f32(tall, LANES)] * replica + [bf16(tall, LANES)] * replica,
         in_specs=[VMEM] * 3,
-        out_specs=[VMEM] * (2 * replica - 1),
+        out_specs=[VMEM] * (2 * replica),
         scratch_shapes=[pltpu.VMEM((2, replica, tall, LANES), jnp.float32)],
         compiler_params=grant(24),
-        cost_estimate=pl.CostEstimate(flops=1, bytes_accessed=1, transcendentals=0),
         name="product",
     )(near, east, east_feats2)
     keeps, sends = products[:replica], products[replica:]
+    got = {}
+    for k in (1, 2, 3, 0):
+        got[k] = swapped(after(sends[k], got[{}[k]]) if k in {} else sends[k], "dp", 2 * REDUCE)
     sums = []
-    for k in range(2, replica):
-        total = keeps[k] + swapped(sends[k - 1], "dp", 4).astype(jnp.float32)
+    for k in (1, 3, 2):
+        total = keeps[k] + got[k].astype(jnp.float32)
         sums.append(swapped(total.astype(jnp.bfloat16), "replica", k))
-    last = swapped(sends[0], "dp", 4).astype(jnp.float32)
-    total = keeps[1] + last[tall:]
-    sums.append(swapped(total.astype(jnp.bfloat16), "replica", 1))
-    own = keeps[0] + last[:tall]
     head_grad = pl.pallas_call(
         functools.partial(final_kernel, cols, depth),
         out_shape=f32(cols, depth),
-        in_specs=[VMEM] * replica,
+        in_specs=[VMEM] * (replica + 1),
         out_specs=VMEM,
         compiler_params=grant(8),
-        cost_estimate=pl.CostEstimate(flops=1, bytes_accessed=1, transcendentals=0),
         name="final",
-    )(own, *sums)
+    )(keeps[0], got[0], *sums)
     return (grad_feat[None], head_grad.T)
 
 

time: 40.1 us -> 39.5 us (0.985)
  waiting for transfers between devices: 10.1 us -> 9.49 us
    ppermute x14 -> x15, waiting for transfers between devices: 8.35 us -> 7.7 us  [swapped(): return lax.ppermute(x, axis, [(i, i ^ mask) for i in range(size)])]
    pallas_call x0 -> x1, Pallas kernels: none -> 0.49 us  [box_shards(): pl.pallas_call(early_kernel, out_shape=f32(2 * cols, head_w.shape[0]), in...]
    pallas_call x1, Pallas kernels: 0.75 us -> 0.32 us  [box_shards(): pl.pallas_call(near_kernel, out_shape=f32(2 * cols, head_w.shape[0]), in_...]
    ppermute x14 -> x15, starting transfers between devices: 15 us -> 15 us  [swapped(): return lax.ppermute(x, axis, [(i, i ^ mask) for i in range(size)])]
  transfers between devices with their start and end apart: 16 -> 17, of which waited for: 6 -> 6; matrix products, arithmetic and copies ran while one was open for 10% -> 10% of each run, Pallas kernels for 8% -> 8%
where the time goes in v5:
time: 39.5 us; the launch traced here: 39.4 us
  starting transfers between devices  19 us (48%)
  waiting for transfers between devices  9.49 us (24%)
  Pallas kernels  4.85 us (12%)
  matrix products  3.77 us (10%)
  between operations  2.14 us (5%)
    ppermute x15, starting transfers between devices, swapped(): return lax.ppermute(x, axis, [(i, i ^ mask) for i in range(size)])  15 us
    ppermute x15, waiting for transfers between devices, swapped(): return lax.ppermute(x, axis, [(i, i ^ mask) for i in range(size)])  7.7 us
    ppermute x2, starting transfers between devices, rotated(): return lax.ppermute(x, axis, [(i, (i + by) % size) for i in range(size)])  4.04 us
    ppermute x2, waiting for transfers between devices, rotated(): return lax.ppermute(x, axis, [(i, (i + by) % size) for i in range(size)])  1.8 us
    dot_general x1, matrix products, box_shards(): lax.dot_general(dzed, head_w, NT, preferred_element_type=jnp.float32)  1.63 us
    dot_general x1, matrix products, box_shards(): raw = jnp.dot(feats, head_w, preferred_element_type=jnp.float32)  1.55 us
    pallas_call x1, Pallas kernels, box_shards(): pl.pallas_call(functools.partial(loss_kernel, factor, cols), out_shape=[b...  1.41 us
    pallas_call x1, Pallas kernels, box_shards(): pl.pallas_call(functools.partial(own_kernel, factor), out_shape=[f32(2 *...  1.11 us
  transfers between devices with their start and end apart: 17, of which 6 were waited for; matrix products, arithmetic and copies ran while one was open for 10% of the time, Pallas kernels for 8%

profile of v5, /device:TPU:0, one launch (start us, length us, event | category | flops | bytes accessed | tf_op | source)
XLA Modules:
  0.0 39.4 jit_solution(14149014033698556351)
XLA Ops:
  0.6 0.0 copy-start
  0.6 0.0 copy-start.1
  0.7 0.5 %collective-permute-start.2 = (bf16[128,1152]{1,0:T(8,128)(2,1)}, bf16[128,1152]{1,0:T(8,128)(2,1)S(1)}, u32[]{:S(2)}, u32[]{:S(2)}) collective-permute-start(bf16[128,1152]{1,0:T(8,128)(2,1)} %bitcast.14), channel_id=1, source_target_pairs={{0,4},{4,0},{8,12},{12,8},{16,20},{20,16},{24,28},{28,24},{1,5},{5... | collective-permute-start | bytes 884744 | tf_op jit(solution)/shard_map/ppermute | solution.py:31
  1.2 3.5 %collective-permute-start = (bf16[128,1152]{1,0:T(8,128)(2,1)}, bf16[128,1152]{1,0:T(8,128)(2,1)S(1)}, u32[]{:S(2)}, u32[]{:S(2)}) collective-permute-start(bf16[128,1152]{1,0:T(8,128)(2,1)} %bitcast.15), channel_id=1, source_target_pairs={{0,24},{4,28},{8,0},{12,4},{16,8},{20,12},{24,16},{28,20},{1,25},{... | collective-permute-start | bytes 884744 | tf_op jit(solution)/shard_map/ppermute | solution.py:26
  4.7 0.2 collective-permute-start.3
  4.8 0.5 %collective-permute-start.5 = (s32[1,128]{1,0:T(1,128)}, s32[1,128]{1,0:T(1,128)S(1)}, u32[]{:S(2)}, u32[]{:S(2)}) collective-permute-start(s32[1,128]{1,0:T(1,128)} %ids.1), channel_id=1, source_target_pairs={{0,24},{4,28},{8,0},{12,4},{16,8},{20,12},{24,16},{28,20},{1,25},{... | collective-permute-start | bytes 1544 | tf_op jit(solution)/shard_map/ppermute | solution.py:26
  5.4 0.1 collective-permute-start.1
  5.4 0.0 copy-done
  5.5 1.5 %fusion.raw = f32[128,1152]{1,0:T(8,128)S(1)} fusion(bf16[1152,1152]{1,0:T(8,128)(2,1)S(1)} %copy-done, bf16[1,128,1152]{2,1,0:T(8,128)(2,1)} %param.7), kind=kOutput, calls=%fused_computation.4 | convolution fusion | flops 339738624 | bytes 3538944 | tf_op jit(solution)/shard_map/dot_general | solution.py:190
  7.0 0.0 copy-start.2
  7.0 0.0 copy-start.3
  8.4 0.0 collective-permute-done.3.ids2
  8.4 1.6 %collective-permute-start.8 = (bf16[128,1152]{1,0:T(8,128)(2,1)S(1)}, bf16[128,1152]{1,0:T(8,128)(2,1)S(1)}, u32[]{:S(2)}, u32[]{:S(2)}) collective-permute-start(bf16[128,1152]{1,0:T(8,128)(2,1)S(1)} %bitcast.12), channel_id=1, source_target_pairs={{0,8},{4,12},{8,0},{12,4},{16,24},{20,28},{24,16},{28,20},{1,9},{5... | collective-permute-start | bytes 884744 | tf_op jit(solution)/shard_map/ppermute | solution.py:31
  9.9 0.0 collective-permute-done.1.feats2
  9.9 0.0 collective-permute-done.2.img2
  9.9 0.6 %fusion.2.raw2 = f32[128,1152]{1,0:T(8,128)S(1)} fusion(bf16[128,1152]{1,0:T(8,128)(2,1)S(1)} %collective-permute-done.1.feats2, bf16[1152,1152]{1,0:T(8,128)(2,1)S(1)} %copy-done), kind=kOutput, calls=%fused_computation.6 | convolution fusion | flops 339738624 | bytes 3538944 | tf_op jit(solution)/shard_map/dot_general | solution.py:191
  10.5 1.8 %collective-permute-done.far = bf16[128,1152]{1,0:T(8,128)(2,1)S(1)} collective-permute-done((bf16[128,1152]{1,0:T(8,128)(2,1)}, bf16[128,1152]{1,0:T(8,128)(2,1)S(1)}, u32[]{:S(2)}, u32[]{:S(2)}) %collective-permute-start) | collective-permute-done | bytes 294944 | tf_op jit(solution)/shard_map/ppermute | solution.py:26
  12.3 0.0 collective-permute-start.4
  12.3 0.0 collective-permute-done.5.ids
  12.3 0.5 %collective-permute-start.6 = (s32[1,128]{1,0:T(1,128)S(1)}, s32[1,128]{1,0:T(1,128)S(1)}, u32[]{:S(2)}, u32[]{:S(2)}) collective-permute-start(s32[1,128]{1,0:T(1,128)S(1)} %collective-permute-done.5.ids), channel_id=1, source_target_pairs={{0,4},{4,0},{8,12},{12,8},{16,20},{20,16},{24,28},{28,24},{1,5},{5... | collective-permute-start | bytes 1544 | tf_op jit(solution)/shard_map/ppermute | solution.py:31
  12.9 1.1 %own.1 = (f32[256,1152]{1,0:T(8,128)S(1)}, f32[256,128]{1,0:T(8,128)S(1)}, s32[256,128]{1,0:T(8,128)S(1)}, f32[256,1152]{1,0:T(8,128)S(1)}) custom-call(f32[1]{0:T(128)S(6)} %copy.8.log_scale, f32[1]{0:T(128)S(6)} %copy.9.bias, s32[1,128]{1,0:T(1,128)S(1)} %copy-done.3, s32[1,128]{1,0:T(1,128)S(1)} %collective-permute-done.3.ids2, f32[128,1152]{1,0:T(8,128)S(1)} %fusion.raw, ...), custom_call_target="tpu_custom_call" | custom-call | flops 10000000000 | bytes 1 | tf_op jit(solution)/shard_map/own/pallas_call | solution.py:192
  14.0 0.0 collective-permute-done.6.ids2
  14.0 0.0 collective-permute-done.4.far2
  14.0 1.4 %loss.1 = (bf16[128,1152]{1,0:T(8,128)(2,1)S(1)}, bf16[288,256]{1,0:T(8,128)(2,1)S(1)}, bf16[288,256]{1,0:T(8,128)(2,1)S(1)}) custom-call(f32[1]{0:T(128)S(6)} %copy.8.log_scale, f32[1]{0:T(128)S(6)} %copy.9.bias, bf16[128,1152]{1,0:T(8,128)(2,1)S(1)} %collective-permute-done.far, bf16[128,1152]{1,0:T(8,128)(2,1)S(1)} %collective-permute-done.4.far2, ...), custom_call_target="tpu_custom_call" | custom-call | tf_op jit(solution)/shard_map/loss/pallas_call | solution.py:212
  15.4 2.4 %collective-permute-start.7 = (bf16[288,256]{1,0:T(8,128)(2,1)S(1)}, bf16[288,256]{1,0:T(8,128)(2,1)S(1)}, u32[]{:S(2)}, u32[]{:S(2)}) collective-permute-start(bf16[288,256]{1,0:T(8,128)(2,1)S(1)} %get-tuple-element.34), channel_id=1, source_target_pairs={{0,8},{4,12},{8,0},{12,4},{16,24},{20,28},{24,16},{28,20},{1,9},{5... | collective-permute-start | bytes 442376 | tf_op jit(solution)/shard_map/ppermute | solution.py:31
  17.8 1.6 %convolution_convert_fusion = bf16[128,1152]{1,0:T(8,128)(2,1)} fusion(bf16[128,1152]{1,0:T(8,128)(2,1)S(1)} %get-tuple-element.32, bf16[1152,1152]{1,0:T(8,128)(2,1)S(1)} %copy-done), kind=kOutput, calls=%fused_computation | convolution fusion | flops 339886080 | bytes 3244032 | tf_op jit(solution)/shard_map/dot_general | solution.py:222
  19.4 0.5 %early.1 = f32[288,1152]{1,0:T(8,128)S(1)} custom-call(bf16[288,256]{1,0:T(8,128)(2,1)S(1)} %get-tuple-element.33.own, bf16[128,1152]{1,0:T(8,128)(2,1)S(1)} %bitcast.13, bf16[128,1152]{1,0:T(8,128)(2,1)S(1)} %collective-permute-done.1.feats2), custom_call_target="tpu_custom_call" | custom-call | tf_op jit(solution)/shard_map/early/pallas_call | solution.py:227
  19.9 0.0 collective-permute-done.8.feats
  19.9 0.1 collective-permute-start.9
  20.0 1.9 %collective-permute-done.7.east = bf16[288,256]{1,0:T(8,128)(2,1)S(1)} collective-permute-done((bf16[288,256]{1,0:T(8,128)(2,1)S(1)}, bf16[288,256]{1,0:T(8,128)(2,1)S(1)}, u32[]{:S(2)}, u32[]{:S(2)}) %collective-permute-start.7) | collective-permute-done | bytes 147488 | tf_op jit(solution)/shard_map/ppermute | solution.py:31
  21.9 0.3 near.1
  22.2 0.0 collective-permute-done.9.feats
  22.2 0.7 %product.1 = (f32[336,128]{1,0:T(8,128)S(1)}, f32[336,128]{1,0:T(8,128)S(1)}, f32[336,128]{1,0:T(8,128)S(1)}, f32[336,128]{1,0:T(8,128)S(1)}, bf16[336,128]{1,0:...) custom-call(f32[288,1152]{1,0:T(8,128)S(1)} %near.1, ...), custom_call_target="tpu_custom_call" | custom-call | tf_op jit(solution)/shard_map/product/pallas_call | solution.py:244
  23.0 1.6 %collective-permute-start.15 = (bf16[336,128]{1,0:T(8,128)(2,1)S(1)}, bf16[336,128]{1,0:T(8,128)(2,1)S(1)}, u32[]{:S(2)}, u32[]{:S(2)}) collective-permute-start(bf16[336,128]{1,0:T(8,128)(2,1)S(1)} %get-tuple-element.43), channel_id=1, source_target_pairs={{0,16},{4,20},{8,24},{12,28},{16,0},{20,4},{24,8},{28,12},{1,17},{... | collective-permute-start | bytes 258056 | tf_op jit(solution)/shard_map/ppermute | solution.py:31
  24.5 0.5 %collective-permute-start.13 = (bf16[336,128]{1,0:T(8,128)(2,1)S(1)}, bf16[336,128]{1,0:T(8,128)(2,1)S(1)}, u32[]{:S(2)}, u32[]{:S(2)}) collective-permute-start(bf16[336,128]{1,0:T(8,128)(2,1)S(1)} %get-tuple-element.41), channel_id=1, source_target_pairs={{0,16},{4,20},{8,24},{12,28},{16,0},{20,4},{24,8},{28,12},{1,17},{... | collective-permute-start | bytes 258056 | tf_op jit(solution)/shard_map/ppermute | solution.py:31
  25.0 1.5 %collective-permute-start.11 = (bf16[336,128]{1,0:T(8,128)(2,1)S(1)}, bf16[336,128]{1,0:T(8,128)(2,1)S(1)}, u32[]{:S(2)}, u32[]{:S(2)}) collective-permute-start(bf16[336,128]{1,0:T(8,128)(2,1)S(1)} %get-tuple-element.39), channel_id=1, source_target_pairs={{0,16},{4,20},{8,24},{12,28},{16,0},{20,4},{24,8},{28,12},{1,17},{... | collective-permute-start | bytes 258056 | tf_op jit(solution)/shard_map/ppermute | solution.py:31
  26.6 0.5 %collective-permute-start.10 = (bf16[336,128]{1,0:T(8,128)(2,1)S(1)}, bf16[336,128]{1,0:T(8,128)(2,1)S(1)}, u32[]{:S(2)}, u32[]{:S(2)}) collective-permute-start(bf16[336,128]{1,0:T(8,128)(2,1)S(1)} %get-tuple-element.37), channel_id=1, source_target_pairs={{0,16},{4,20},{8,24},{12,28},{16,0},{20,4},{24,8},{28,12},{1,17},{... | collective-permute-start | bytes 258056 | tf_op jit(solution)/shard_map/ppermute | solution.py:31
  27.1 1.4 %collective-permute-done.15 = bf16[336,128]{1,0:T(8,128)(2,1)S(1)} collective-permute-done((bf16[336,128]{1,0:T(8,128)(2,1)S(1)}, bf16[336,128]{1,0:T(8,128)(2,1)S(1)}, u32[]{:S(2)}, u32[]{:S(2)}) %collective-permute-start.15) | collective-permute-done | bytes 86048 | tf_op jit(solution)/shard_map/ppermute | solution.py:31
  28.5 2.7 %collective-permute-start.16 = (bf16[336,128]{1,0:T(8,128)(2,1)S(1)}, bf16[336,128]{1,0:T(8,128)(2,1)S(1)}, u32[]{:S(2)}, u32[]{:S(2)}) collective-permute-start(bf16[336,128]{1,0:T(8,128)(2,1)S(1)} %add_convert_fusion), channel_id=1, source_target_pairs={{0,2},{1,3},{2,0},{3,1},{4,6},{5,7},{6,4},{7,5},{8,10},{9,11},{10,... | collective-permute-start | bytes 258056 | tf_op jit(solution)/shard_map/ppermute | solution.py:31
  31.1 0.0 collective-permute-done.13
  31.1 2.9 %collective-permute-start.14 = (bf16[336,128]{1,0:T(8,128)(2,1)S(1)}, bf16[336,128]{1,0:T(8,128)(2,1)S(1)}, u32[]{:S(2)}, u32[]{:S(2)}) collective-permute-start(bf16[336,128]{1,0:T(8,128)(2,1)S(1)} %add_convert_fusion.1), channel_id=1, source_target_pairs={{0,3},{1,2},{2,1},{3,0},{4,7},{5,6},{6,5},{7,4},{8,11},{9,10},{10,... | collective-permute-start | bytes 258056 | tf_op jit(solution)/shard_map/ppermute | solution.py:31
  34.0 0.0 collective-permute-done.11
  34.0 0.1 collective-permute-start.12
  34.1 0.0 collective-permute-done.10.refs_1_
  34.1 1.7 %collective-permute-done.16.refs_4_ = bf16[336,128]{1,0:T(8,128)(2,1)S(1)} collective-permute-done((bf16[336,128]{1,0:T(8,128)(2,1)S(1)}, bf16[336,128]{1,0:T(8,128)(2,1)S(1)}, u32[]{:S(2)}, u32[]{:S(2)}) %collective-permute-start.16) | collective-permute-done | bytes 86048 | tf_op jit(solution)/shard_map/ppermute | solution.py:31
  35.8 1.8 %collective-permute-done.14.refs_3_ = bf16[336,128]{1,0:T(8,128)(2,1)S(1)} collective-permute-done((bf16[336,128]{1,0:T(8,128)(2,1)S(1)}, bf16[336,128]{1,0:T(8,128)(2,1)S(1)}, u32[]{:S(2)}, u32[]{:S(2)}) %collective-permute-start.14) | collective-permute-done | bytes 86048 | tf_op jit(solution)/shard_map/ppermute | solution.py:31
  37.6 1.0 %collective-permute-done.12.refs_2_ = bf16[336,128]{1,0:T(8,128)(2,1)S(1)} collective-permute-done((bf16[336,128]{1,0:T(8,128)(2,1)S(1)}, bf16[336,128]{1,0:T(8,128)(2,1)S(1)}, u32[]{:S(2)}, u32[]{:S(2)}) %collective-permute-start.12) | collective-permute-done | bytes 86048 | tf_op jit(solution)/shard_map/ppermute | solution.py:31
  38.6 0.8 %final.1 = f32[144,288]{1,0:T(8,128)} custom-call(f32[336,128]{1,0:T(8,128)S(1)} %get-tuple-element.36.refs_0_, bf16[336,128]{1,0:T(8,128)(2,1)S(1)} %collective-permute-done.10.refs_1_, bf16[336,128]{1,0:T(8,128)(2,1)S(1)} %collective-permute-done.12.refs_2_, bf16[336,128]{1,0:T(8,128)(2,1)S(1)} %collective-permute-done.14.refs_3_, ...), custom_call_target="tpu_custom_call" | custom-call | tf_op jit(solution)/shard_map/final/pallas_call | solution.py:261
  (6 shorter events, 0.1 us)
Async XLA Ops:
  0.6 4.8 %copy-start = (bf16[1152,1152]{1,0:T(8,128)(2,1)S(1)}, bf16[1152,1152]{1,0:T(8,128)(2,1)}, u32[]{:S(2)}) copy-start(bf16[1152,1152]{1,0:T(8,128)(2,1)} %param.8) | copy-start | bytes 7962628
  0.6 7.7 %copy-start.1 = (bf16[1,128,1152]{2,1,0:T(8,128)(2,1)S(1)}, bf16[1,128,1152]{2,1,0:T(8,128)(2,1)}, u32[]{:S(2)}) copy-start(bf16[1,128,1152]{2,1,0:T(8,128)(2,1)} %param.7) | copy-start | bytes 884740
  0.7 9.3 %collective-permute-start.2 = (bf16[128,1152]{1,0:T(8,128)(2,1)}, bf16[128,1152]{1,0:T(8,128)(2,1)S(1)}, u32[]{:S(2)}, u32[]{:S(2)}) collective-permute-start(bf16[128,1152]{1,0:T(8,128)(2,1)} %bitcast.14), channel_id=1, source_target_pairs={{0,4},{4,0},{8,12},{12,8},{16,20},{20,16},{24,28},{28,24},{1,5},{5... | collective-permute-start | bytes 884744 | tf_op jit(solution)/shard_map/ppermute | solution.py:31
  1.2 11.2 %collective-permute-start = (bf16[128,1152]{1,0:T(8,128)(2,1)}, bf16[128,1152]{1,0:T(8,128)(2,1)S(1)}, u32[]{:S(2)}, u32[]{:S(2)}) collective-permute-start(bf16[128,1152]{1,0:T(8,128)(2,1)} %bitcast.15), channel_id=1, source_target_pairs={{0,24},{4,28},{8,0},{12,4},{16,8},{20,12},{24,16},{28,20},{1,25},{... | collective-permute-start | bytes 884744 | tf_op jit(solution)/shard_map/ppermute | solution.py:26
  4.7 3.7 %collective-permute-start.3 = (s32[1,128]{1,0:T(1,128)}, s32[1,128]{1,0:T(1,128)S(1)}, u32[]{:S(2)}, u32[]{:S(2)}) collective-permute-start(s32[1,128]{1,0:T(1,128)} %ids.1), channel_id=1, source_target_pairs={{0,4},{4,0},{8,12},{12,8},{16,20},{20,16},{24,28},{28,24},{1,5},{5... | collective-permute-start | bytes 1544 | tf_op jit(solution)/shard_map/ppermute | solution.py:31
  4.8 7.5 %collective-permute-start.5 = (s32[1,128]{1,0:T(1,128)}, s32[1,128]{1,0:T(1,128)S(1)}, u32[]{:S(2)}, u32[]{:S(2)}) collective-permute-start(s32[1,128]{1,0:T(1,128)} %ids.1), channel_id=1, source_target_pairs={{0,24},{4,28},{8,0},{12,4},{16,8},{20,12},{24,16},{28,20},{1,25},{... | collective-permute-start | bytes 1544 | tf_op jit(solution)/shard_map/ppermute | solution.py:26
  5.4 4.6 %collective-permute-start.1 = (bf16[128,1152]{1,0:T(8,128)(2,1)}, bf16[128,1152]{1,0:T(8,128)(2,1)S(1)}, u32[]{:S(2)}, u32[]{:S(2)}) collective-permute-start(bf16[128,1152]{1,0:T(8,128)(2,1)} %bitcast.11), channel_id=1, source_target_pairs={{0,4},{4,0},{8,12},{12,8},{16,20},{20,16},{24,28},{28,24},{1,5},{5... | collective-permute-start | bytes 884744 | tf_op jit(solution)/shard_map/ppermute | solution.py:31
  7.0 5.8 %copy-start.2 = (bf16[1,128,1152]{2,1,0:T(8,128)(2,1)S(1)}, bf16[1,128,1152]{2,1,0:T(8,128)(2,1)}, u32[]{:S(2)}) copy-start(bf16[1,128,1152]{2,1,0:T(8,128)(2,1)} %param.6) | copy-start | bytes 884740
  7.0 5.8 %copy-start.3 = (s32[1,128]{1,0:T(1,128)S(1)}, s32[1,128]{1,0:T(1,128)}, u32[]{:S(2)}) copy-start(s32[1,128]{1,0:T(1,128)} %ids.1) | copy-start | bytes 1540
  8.4 11.5 %collective-permute-start.8 = (bf16[128,1152]{1,0:T(8,128)(2,1)S(1)}, bf16[128,1152]{1,0:T(8,128)(2,1)S(1)}, u32[]{:S(2)}, u32[]{:S(2)}) collective-permute-start(bf16[128,1152]{1,0:T(8,128)(2,1)S(1)} %bitcast.12), channel_id=1, source_target_pairs={{0,8},{4,12},{8,0},{12,4},{16,24},{20,28},{24,16},{28,20},{1,9},{5... | collective-permute-start | bytes 884744 | tf_op jit(solution)/shard_map/ppermute | solution.py:31
  12.3 1.6 %collective-permute-start.4 = (bf16[128,1152]{1,0:T(8,128)(2,1)S(1)}, bf16[128,1152]{1,0:T(8,128)(2,1)S(1)}, u32[]{:S(2)}, u32[]{:S(2)}) collective-permute-start(bf16[128,1152]{1,0:T(8,128)(2,1)S(1)} %collective-permute-done.far), channel_id=1, source_target_pairs={{0,4},{4,0},{8,12},{12,8},{16,20},{20,16},{24,28},{28,24},{1,5},{5... | collective-permute-start | bytes 884744 | tf_op jit(solution)/shard_map/ppermute | solution.py:31
  12.3 1.6 %collective-permute-start.6 = (s32[1,128]{1,0:T(1,128)S(1)}, s32[1,128]{1,0:T(1,128)S(1)}, u32[]{:S(2)}, u32[]{:S(2)}) collective-permute-start(s32[1,128]{1,0:T(1,128)S(1)} %collective-permute-done.5.ids), channel_id=1, source_target_pairs={{0,4},{4,0},{8,12},{12,8},{16,20},{20,16},{24,28},{28,24},{1,5},{5... | collective-permute-start | bytes 1544 | tf_op jit(solution)/shard_map/ppermute | solution.py:31
  15.4 6.5 %collective-permute-start.7 = (bf16[288,256]{1,0:T(8,128)(2,1)S(1)}, bf16[288,256]{1,0:T(8,128)(2,1)S(1)}, u32[]{:S(2)}, u32[]{:S(2)}) collective-permute-start(bf16[288,256]{1,0:T(8,128)(2,1)S(1)} %get-tuple-element.34), channel_id=1, source_target_pairs={{0,8},{4,12},{8,0},{12,4},{16,24},{20,28},{24,16},{28,20},{1,9},{5... | collective-permute-start | bytes 442376 | tf_op jit(solution)/shard_map/ppermute | solution.py:31
  19.9 2.3 %collective-permute-start.9 = (bf16[128,1152]{1,0:T(8,128)(2,1)S(1)}, bf16[128,1152]{1,0:T(8,128)(2,1)S(1)}, u32[]{:S(2)}, u32[]{:S(2)}) collective-permute-start(bf16[128,1152]{1,0:T(8,128)(2,1)S(1)} %collective-permute-done.8.feats), channel_id=1, source_target_pairs={{0,4},{4,0},{8,12},{12,8},{16,20},{20,16},{24,28},{28,24},{1,5},{5... | collective-permute-start | bytes 884744 | tf_op jit(solution)/shard_map/ppermute | solution.py:31
  23.0 5.5 %collective-permute-start.15 = (bf16[336,128]{1,0:T(8,128)(2,1)S(1)}, bf16[336,128]{1,0:T(8,128)(2,1)S(1)}, u32[]{:S(2)}, u32[]{:S(2)}) collective-permute-start(bf16[336,128]{1,0:T(8,128)(2,1)S(1)} %get-tuple-element.43), channel_id=1, source_target_pairs={{0,16},{4,20},{8,24},{12,28},{16,0},{20,4},{24,8},{28,12},{1,17},{... | collective-permute-start | bytes 258056 | tf_op jit(solution)/shard_map/ppermute | solution.py:31
  24.5 6.6 %collective-permute-start.13 = (bf16[336,128]{1,0:T(8,128)(2,1)S(1)}, bf16[336,128]{1,0:T(8,128)(2,1)S(1)}, u32[]{:S(2)}, u32[]{:S(2)}) collective-permute-start(bf16[336,128]{1,0:T(8,128)(2,1)S(1)} %get-tuple-element.41), channel_id=1, source_target_pairs={{0,16},{4,20},{8,24},{12,28},{16,0},{20,4},{24,8},{28,12},{1,17},{... | collective-permute-start | bytes 258056 | tf_op jit(solution)/shard_map/ppermute | solution.py:31
  25.0 9.0 %collective-permute-start.11 = (bf16[336,128]{1,0:T(8,128)(2,1)S(1)}, bf16[336,128]{1,0:T(8,128)(2,1)S(1)}, u32[]{:S(2)}, u32[]{:S(2)}) collective-permute-start(bf16[336,128]{1,0:T(8,128)(2,1)S(1)} %get-tuple-element.39), channel_id=1, source_target_pairs={{0,16},{4,20},{8,24},{12,28},{16,0},{20,4},{24,8},{28,12},{1,17},{... | collective-permute-start | bytes 258056 | tf_op jit(solution)/shard_map/ppermute | solution.py:31
  26.6 7.5 %collective-permute-start.10 = (bf16[336,128]{1,0:T(8,128)(2,1)S(1)}, bf16[336,128]{1,0:T(8,128)(2,1)S(1)}, u32[]{:S(2)}, u32[]{:S(2)}) collective-permute-start(bf16[336,128]{1,0:T(8,128)(2,1)S(1)} %get-tuple-element.37), channel_id=1, source_target_pairs={{0,16},{4,20},{8,24},{12,28},{16,0},{20,4},{24,8},{28,12},{1,17},{... | collective-permute-start | bytes 258056 | tf_op jit(solution)/shard_map/ppermute | solution.py:31
  28.5 7.3 %collective-permute-start.16 = (bf16[336,128]{1,0:T(8,128)(2,1)S(1)}, bf16[336,128]{1,0:T(8,128)(2,1)S(1)}, u32[]{:S(2)}, u32[]{:S(2)}) collective-permute-start(bf16[336,128]{1,0:T(8,128)(2,1)S(1)} %add_convert_fusion), channel_id=1, source_target_pairs={{0,2},{1,3},{2,0},{3,1},{4,6},{5,7},{6,4},{7,5},{8,10},{9,11},{10,... | collective-permute-start | bytes 258056 | tf_op jit(solution)/shard_map/ppermute | solution.py:31
  31.1 6.5 %collective-permute-start.14 = (bf16[336,128]{1,0:T(8,128)(2,1)S(1)}, bf16[336,128]{1,0:T(8,128)(2,1)S(1)}, u32[]{:S(2)}, u32[]{:S(2)}) collective-permute-start(bf16[336,128]{1,0:T(8,128)(2,1)S(1)} %add_convert_fusion.1), channel_id=1, source_target_pairs={{0,3},{1,2},{2,1},{3,0},{4,7},{5,6},{6,5},{7,4},{8,11},{9,10},{10,... | collective-permute-start | bytes 258056 | tf_op jit(solution)/shard_map/ppermute | solution.py:31
  34.0 4.6 %collective-permute-start.12 = (bf16[336,128]{1,0:T(8,128)(2,1)S(1)}, bf16[336,128]{1,0:T(8,128)(2,1)S(1)}, u32[]{:S(2)}, u32[]{:S(2)}) collective-permute-start(bf16[336,128]{1,0:T(8,128)(2,1)S(1)} %add_convert_fusion.2), channel_id=1, source_target_pairs={{0,1},{1,0},{2,3},{3,2},{4,5},{5,4},{6,7},{7,6},{8,9},{9,8},{10,11... | collective-permute-start | bytes 258056 | tf_op jit(solution)/shard_map/ppermute | solution.py:31
